TPU v7x, 256 devices: a whole 4x4x8 slice. The times are simulated.
256 devices in a mesh: brick: 64 (over z, x, core), spec: 4 (over y).
Axes of the slice: x: 4, y: 4, z: 8, core: 2. Of those that a mesh axis runs over, the one named last changes fastest.
Arguments:
- rhs: float32 [4, 128, 256, 256], P('spec', 'brick'), may hold values from -24 to 24
- density: float32 [128, 256, 256], P('brick', 'spec'), may hold values from 0.01 to 0.1
- kappa: float32 [4], P('spec'), may hold values from 0.5 to 4
- block_group: int32 [64, 16], replicated, may hold values from 0 to 255, as said below
Outputs:
- solution: float32 [4, 128, 256, 256], P('spec', 'brick')
- residual: float32 [4, 128, 256, 256], P('spec', 'brick')
Inputs may be any that keep to these rules, and one draw needn't show every extreme that they name: `block_group`: every aggregate id 0 to 255 names at least one block; the blocks of one aggregate share one tile position and lie on consecutive bricks.
All inputs are finite; a program needn't handle non-finite values.
Results may differ from a plain program's by a relative error of at most 0.0003.
Values sent between devices are 32-bit elements; how exact they have to be, the bound alone decides.
No kernel may reach another device: no remote copies, remote signals or barrier semaphores. Data moves between devices by JAX's collectives and lax.ppermute only.
A program may use at most 64 MiB of HBM per device.

v0:
```python
import jax
import jax.numpy as jnp
from jax import lax
from jax.sharding import PartitionSpec as P

TILES = 4
AGG_DEV = 4
COARSE_SWEEPS = 3


relax_fine = 0.85
relax_coarse = 0.6
highest = lax.Precision.HIGHEST


def with_halo(cells, sides, width):
    for axis, dim in sides:
        count = lax.axis_size(axis)
        ends = count - 1
        head = lax.slice_in_dim(cells, 0, width, axis=dim)
        tail = lax.slice_in_dim(cells, cells.shape[dim] - width, cells.shape[dim], axis=dim)
        cells = jnp.concatenate(
            [
                lax.ppermute(tail, axis, [(i, (i + 1) % count) for i in range(ends)]),
                cells,
                lax.ppermute(head, axis, [((i + 1) % count, i) for i in range(ends)]),
            ],
            axis=dim,
        )
    return cells


def filter_along(field, axis):
    length = field.shape[axis]
    widths = [(0, 0)] * field.ndim
    widths[axis] = (1, 1)
    padded = jnp.pad(field, widths)
    lower = lax.slice_in_dim(padded, 0, length, axis=axis)
    upper = lax.slice_in_dim(padded, 2, length + 2, axis=axis)
    return field + 0.5 * (lower + upper)


def stencil_sum(extended):
    inner = extended.shape[1] - 2
    middle = lax.slice_in_dim(extended, 1, inner + 1, axis=1)
    lower = lax.slice_in_dim(extended, 0, inner, axis=1)
    upper = lax.slice_in_dim(extended, 2, inner + 2, axis=1)
    return filter_along(filter_along(middle + 0.5 * (lower + upper), 2), 3)


def relax_with(field, extended, source, center, diagonal, scale):
    image = center * field - 2.0 * scale * stencil_sum(extended)
    return field + relax_fine * (source - image) / diagonal


def coarsen(field):
    leading = field.shape[:-3]
    first, second, third = field.shape[-3:]
    count = len(leading)
    blocks = field.reshape(leading + (first // 2, 2, second // 2, 2, third // 2, 2))
    return jnp.sum(blocks, axis=(count + 1, count + 3, count + 5)) * 0.125


def refine(field):
    leading = field.shape[:-3]
    first, second, third = field.shape[-3:]
    shaped = field.reshape(leading + (first, 1, second, 1, third, 1))
    grown = jnp.broadcast_to(shaped, leading + (first, 2, second, 2, third, 2))
    return grown.reshape(leading + (2 * first, 2 * second, 2 * third))


def cell_groups(rows, thickness, height, width):
    count = rows.shape[0]
    shaped = rows.reshape(count, 1, TILES, 1, TILES, 1)
    grown = jnp.broadcast_to(
        shaped, (count, thickness, TILES, height // TILES, TILES, width // TILES)
    )
    return grown.reshape(count * thickness, height, width)


def same_weight(padded, extent):
    first, second, third = extent
    center = padded[1 : 1 + first, 1 : 1 + second, 1 : 1 + third]
    total = jnp.zeros(extent, jnp.float32)
    for first_step in (-1, 0, 1):
        for second_step in (-1, 0, 1):
            for third_step in (-1, 0, 1):
                weight = 0.5 ** (abs(first_step) + abs(second_step) + abs(third_step))
                shifted = lax.slice(
                    padded,
                    (1 + first_step, 1 + second_step, 1 + third_step),
                    (1 + first_step + first, 1 + second_step + second, 1 + third_step + third),
                )
                total = total + weight * (shifted == center).astype(jnp.float32)
    return total


def block_sums(field):
    leading, thickness, height, width = field.shape
    parts = field.reshape(leading, thickness, TILES, height // TILES, TILES, width // TILES)
    return jnp.sum(parts, axis=(1, 3, 5)).reshape(leading, TILES * TILES)


def spread_blocks(values, thickness, height, width):
    leading = values.shape[0]
    shaped = values.reshape(leading, 1, TILES, 1, TILES, 1)
    grown = jnp.broadcast_to(
        shaped, (leading, thickness, TILES, height // TILES, TILES, width // TILES)
    )
    return grown.reshape(leading, thickness, height, width)


def fine_halo(field):
    return with_halo(field, (("brick", 1),), 1)


def to_owners(partial_sums):
    return lax.psum_scatter(partial_sums, "brick", scatter_dimension=1, tiled=True)


def from_owners(owned):
    return lax.all_gather(owned, "brick", axis=1, tiled=True)


def local(rhs, density, kappa, block_group):
    density_full = lax.all_gather(density, "spec", axis=1, tiled=True)
    scale = kappa[:, None, None, None]
    center = density_full[None] + 16.0 * scale
    diagonal = density_full[None] + 14.0 * scale
    density_coarse = coarsen(density_full)
    scale_coarse = 0.25 * scale
    center_coarse = density_coarse[None] + 16.0 * scale_coarse
    diagonal_coarse = density_coarse[None] + 14.0 * scale_coarse
    bricks = lax.axis_size("brick")
    position = lax.axis_index("brick")
    cells = rhs.shape[1]
    thickness = cells // 2
    height = rhs.shape[2] // 2
    width = rhs.shape[3] // 2
    groups_total = AGG_DEV * bricks
    padded_rows = jnp.pad(block_group, ((1, 1), (0, 0)), constant_values=-1)
    nearby = lax.dynamic_slice_in_dim(padded_rows, position, 3, 0)
    selector = (nearby[1][:, None] == jnp.arange(groups_total, dtype=jnp.int32)[None, :]).astype(
        jnp.float32
    )
    stacked_ids = jnp.concatenate(
        [
            cell_groups(nearby[0:1], 1, height, width),
            cell_groups(nearby[1:2], thickness, height, width),
            cell_groups(nearby[2:3], 1, height, width),
        ],
        0,
    )
    padded_ids = jnp.pad(stacked_ids, ((0, 0), (1, 1), (1, 1)), constant_values=-1)
    same = same_weight(padded_ids, (thickness, height, width))

    def aggregate(field):
        return jnp.dot(
            block_sums(field), selector, precision=highest, preferred_element_type=jnp.float32
        )

    def spread_groups(values):
        per_block = jnp.dot(
            values, selector.T, precision=highest, preferred_element_type=jnp.float32
        )
        return spread_blocks(per_block, thickness, height, width)

    stats = to_owners(aggregate(jnp.stack([density_coarse, 16.0 - 2.0 * same])))
    coarse_diag = stats[0][None] + (0.25 * kappa)[:, None] * stats[1][None]

    def smooth_once(field):
        return relax_with(field, fine_halo(field), rhs, center, diagonal, scale)

    def operate_fine(field):
        return center * field - 2.0 * scale * stencil_sum(fine_halo(field))

    def operate_coarse(field):
        extended = with_halo(field, (("brick", 1),), 1)
        return center_coarse * field - 2.0 * scale_coarse * stencil_sum(extended)

    def relax_level(field, source):
        return field + relax_fine * (source - operate_coarse(field)) / diagonal_coarse

    solution = relax_fine * rhs / diagonal
    solution = smooth_once(solution)
    fine_res = rhs - operate_fine(solution)
    coarse_res = coarsen(fine_res)
    correction = relax_fine * coarse_res / diagonal_coarse
    correction = relax_level(correction, coarse_res)
    remainder = coarse_res - operate_coarse(correction)
    group_rhs = to_owners(aggregate(remainder))
    group_fix = relax_coarse * group_rhs / coarse_diag
    for sweep in range(COARSE_SWEEPS - 1):
        image = operate_coarse(spread_groups(from_owners(group_fix)))
        group_fix = (
            group_fix + relax_coarse * (group_rhs - to_owners(aggregate(image))) / coarse_diag
        )
    correction = correction + spread_groups(from_owners(group_fix))
    correction = relax_level(correction, coarse_res)
    correction = relax_level(correction, coarse_res)
    solution = solution + refine(correction)
    solution = smooth_once(smooth_once(solution))
    residual = rhs - operate_fine(solution)
    return (solution, residual)


def solution(mesh):
    return jax.shard_map(
        local,
        mesh=mesh,
        in_specs=(P("spec", "brick", None, None), P("brick", "spec", None), P("spec"), P()),
        out_specs=(P("spec", "brick", None, None), P("spec", "brick", None, None)),
        check_vma=False,
    )
```

profile of v0, /device:TPU:103, one launch (start us, length us, event | category | flops | bytes accessed | tf_op | source)
XLA Modules:
  0.0 986.5 jit_solution(7359123869528121073)
XLA Ops:
  1.3 12.0 %all_gather.12 = f32[2,256,256]{2,1,0:T(8,128)S(1)} all-gather(f32[2,64,256]{2,1,0:T(8,128)} %param.5), channel_id=1, replica_groups=mesh['brick'=64,'spec'=4] {'spec'}, dimensions={1}, use_global_device_ids=true | all-gather | bytes 655360 | tf_op jit(solution)/shard_map/all_gather | solution.py:126
  13.3 1.1 bitcast_divide_fusion
  14.4 6.8 collective-permute-start
  21.2 1.9 collective-permute-start.1
  25.3 6.9 collective-permute-done.1
  32.4 1.4 fusion.8
  33.9 1.9 collective-permute-start.2
  35.8 2.4 collective-permute-start.3
  38.3 18.1 %reduce_sum.72 = f32[128,2,128,2]{3,2,1,0:T(8,128)} reshape(f32[256,256]{1,0:T(8,128)S(1)} %reduce_sum.71) | data formatting | bytes 524288 | tf_op jit(solution)/shard_map/reduce_sum | solution.py:61
  56.4 8.0 reduce_sum.73
  65.4 18.1 %reduce_sum.69 = f32[128,2,128,2]{3,2,1,0:T(8,128)} reshape(f32[256,256]{1,0:T(8,128)S(1)} %fusion.15) | data formatting | bytes 524288 | tf_op jit(solution)/shard_map/reduce_sum | solution.py:61
  83.6 8.0 reduce_sum.70
  91.6 6.5 collective-permute-start.4
  98.1 1.9 collective-permute-start.5
  100.7 6.3 collective-permute-done.5
  107.1 1.9 collective-permute-start.6
  109.1 2.4 collective-permute-start.7
  113.6 4.4 collective-permute-done.7
  118.7 123.5 %all-reduce.31 = (f32[2,256]{1,0:T(2,128)S(1)}, f32[1,256]{1,0:T(1,128)S(1)}) all-reduce(f32[2,256]{1,0:T(2,128)S(1)} %fusion.143, f32[1,256]{1,0:T(1,128)S(1)} %fusion.144), channel_id=3, replica_groups=mesh['brick'=64,'spec'=4] {'brick'}, use_global_device_ids=true, to_apply=%region_7.8.clone | all-reduce | flops 768 | bytes 6144
  242.5 124.0 %all-reduce.24 = f32[256]{0:T(256)S(1)} all-reduce(f32[256]{0:T(256)S(1)} %get-tuple-element.9), channel_id=1, replica_groups=mesh['brick'=64,'spec'=4] {'brick'}, use_global_device_ids=true, to_apply=%add.24 | all-reduce | flops 256 | bytes 2048 | tf_op jit(solution)/shard_map/reshape.14
  367.1 7.7 collective-permute-start.8
  374.8 1.9 collective-permute-start.9
  376.7 7.0 collective-permute-done.9
  384.4 123.5 %all-reduce.29 = f32[1,256]{1,0:T(1,128)S(1)} all-reduce(f32[1,256]{1,0:T(1,128)S(1)} %fusion.142), channel_id=4, replica_groups=mesh['brick'=64,'spec'=4] {'brick'}, use_global_device_ids=true, to_apply=%region_9.10.clone | all-reduce | flops 256 | bytes 2048
  508.1 124.0 %all-reduce.25 = f32[256]{0:T(256)S(1)} all-reduce(f32[256]{0:T(256)S(1)} %get-tuple-element.7), channel_id=1, replica_groups=mesh['brick'=64,'spec'=4] {'brick'}, use_global_device_ids=true, to_apply=%add.25 | all-reduce | flops 256 | bytes 2048 | tf_op jit(solution)/shard_map/reshape.20
  632.7 7.5 collective-permute-start.10
  640.2 1.9 collective-permute-start.11
  642.2 7.0 collective-permute-done.11
  649.9 123.5 %all-reduce.30 = f32[1,256]{1,0:T(1,128)S(1)} all-reduce(f32[1,256]{1,0:T(1,128)S(1)} %fusion.141), channel_id=5, replica_groups=mesh['brick'=64,'spec'=4] {'brick'}, use_global_device_ids=true, to_apply=%region_11.12.clone | all-reduce | flops 256 | bytes 2048
  773.6 124.0 %all-reduce.26 = f32[256]{0:T(256)S(1)} all-reduce(f32[256]{0:T(256)S(1)} %bitcast_dynamic-update-slice_fusion), channel_id=1, replica_groups=mesh['brick'=64,'spec'=4] {'brick'}, use_global_device_ids=true, to_apply=%add.26 | all-reduce | flops 256 | bytes 2048 | tf_op jit(solution)/shard_map/reshape.52
  898.2 7.5 collective-permute-start.12
  905.7 1.9 collective-permute-start.13
  907.7 7.0 collective-permute-done.13
  914.8 1.9 collective-permute-start.14
  916.7 2.4 collective-permute-start.15
  919.2 6.5 collective-permute-done.15
  925.8 6.4 broadcast_in_dim.82
  932.2 12.7 %broadcast_in_dim.83 = f32[256,256]{1,0:T(8,128)S(1)} reshape(f32[128,2,128,2]{3,2,1,0:T(8,128)} %broadcast_in_dim.82) | data formatting | bytes 524288 | tf_op jit(solution)/shard_map/broadcast_in_dim | solution.py:68
  945.0 1.9 collective-permute-start.16
  946.9 2.4 collective-permute-start.17
  950.2 7.7 collective-permute-done.17
  958.6 1.9 collective-permute-start.18
  960.5 2.4 collective-permute-start.19
  963.8 7.7 collective-permute-done.19
  972.2 1.9 collective-permute-start.20
  974.1 2.4 collective-permute-start.21
  977.4 7.7 collective-permute-done.21
  985.3 1.2 fusion.39
  (105 shorter events, 14.0 us)
Async XLA Ops:
  14.4 10.8 %collective-permute-start = (f32[1,1,256,256]{3,2,1,0:T(8,128)S(1)}, f32[1,1,256,256]{3,2,1,0:T(8,128)S(1)}, u32[]{:S(2)}, u32[]{:S(2)}) collective-permute-start(f32[1,1,256,256]{3,2,1,0:T(8,128)S(1)} %get-tuple-element.20), channel_id=1, source_target_pairs={{0,4},{4,8},{8,12},{12,16},{16,20},{20,24},{24,28},{28,32},{32,36}... | collective-permute-start | bytes 786440 | tf_op jit(solution)/shard_map/ppermute | solution.py:24
  21.2 11.0 %collective-permute-start.1 = (f32[1,1,256,256]{3,2,1,0:T(8,128)S(1)}, f32[1,1,256,256]{3,2,1,0:T(8,128)S(1)}, u32[]{:S(2)}, u32[]{:S(2)}) collective-permute-start(f32[1,1,256,256]{3,2,1,0:T(8,128)S(1)} %get-tuple-element.21), channel_id=1, source_target_pairs={{4,0},{8,4},{12,8},{16,12},{20,16},{24,20},{28,24},{32,28},{36,32}... | collective-permute-start | bytes 786440 | tf_op jit(solution)/shard_map/ppermute | solution.py:26
  33.9 31.0 %collective-permute-start.2 = (f32[1,1,256,256]{3,2,1,0:T(8,128)S(1)}, f32[1,1,256,256]{3,2,1,0:T(8,128)S(1)}, u32[]{:S(2)}, u32[]{:S(2)}) collective-permute-start(f32[1,1,256,256]{3,2,1,0:T(8,128)S(1)} %get-tuple-element.18), channel_id=1, source_target_pairs={{0,4},{4,8},{8,12},{12,16},{16,20},{20,24},{24,28},{28,32},{32,36}... | collective-permute-start | bytes 786440 | tf_op jit(solution)/shard_map/ppermute | solution.py:24
  35.8 29.0 %collective-permute-start.3 = (f32[1,1,256,256]{3,2,1,0:T(8,128)S(1)}, f32[1,1,256,256]{3,2,1,0:T(8,128)S(1)}, u32[]{:S(2)}, u32[]{:S(2)}) collective-permute-start(f32[1,1,256,256]{3,2,1,0:T(8,128)S(1)} %get-tuple-element.19), channel_id=1, source_target_pairs={{4,0},{8,4},{12,8},{16,12},{20,16},{24,20},{28,24},{32,28},{36,32}... | collective-permute-start | bytes 786440 | tf_op jit(solution)/shard_map/ppermute | solution.py:26
  38.3 26.8 %copy-start = (f32[1,2,256,256]{3,2,1,0:T(8,128)S(1)}, f32[1,2,256,256]{3,2,1,0:T(8,128)}, u32[]{:S(2)}) copy-start(f32[1,2,256,256]{3,2,1,0:T(8,128)} %param.4) | copy-start | bytes 1572868
  65.4 46.2 %copy-start.2 = (u32[256]{0:T(256)S(1)}, u32[256]{0:T(256)}, u32[]{:S(2)}) copy-start(u32[256]{0:T(256)} %constant.138) | copy-start | bytes 3076
  91.6 9.1 collective-permute-start.4
  98.1 8.9 collective-permute-start.5
  107.1 6.4 collective-permute-start.6
  109.1 8.9 collective-permute-start.7
  367.1 9.6 collective-permute-start.8
  374.8 8.9 collective-permute-start.9
  632.7 9.4 collective-permute-start.10
  640.2 8.9 collective-permute-start.11
  898.2 9.4 collective-permute-start.12
  905.7 8.9 collective-permute-start.13
  914.8 4.3 collective-permute-start.14
  916.7 8.9 collective-permute-start.15
  945.0 5.2 collective-permute-start.16
  946.9 11.0 %collective-permute-start.17 = (f32[1,1,256,256]{3,2,1,0:T(8,128)S(1)}, f32[1,1,256,256]{3,2,1,0:T(8,128)S(1)}, u32[]{:S(2)}, u32[]{:S(2)}) collective-permute-start(f32[1,1,256,256]{3,2,1,0:T(8,128)S(1)} %get-tuple-element.17), channel_id=1, source_target_pairs={{4,0},{8,4},{12,8},{16,12},{20,16},{24,20},{28,24},{32,28},{36,32}... | collective-permute-start | bytes 786440 | tf_op jit(solution)/shard_map/ppermute | solution.py:26
  958.6 5.2 collective-permute-start.18
  960.5 11.0 %collective-permute-start.19 = (f32[1,1,256,256]{3,2,1,0:T(8,128)S(1)}, f32[1,1,256,256]{3,2,1,0:T(8,128)S(1)}, u32[]{:S(2)}, u32[]{:S(2)}) collective-permute-start(f32[1,1,256,256]{3,2,1,0:T(8,128)S(1)} %get-tuple-element.15), channel_id=1, source_target_pairs={{4,0},{8,4},{12,8},{16,12},{20,16},{24,20},{28,24},{32,28},{36,32}... | collective-permute-start | bytes 786440 | tf_op jit(solution)/shard_map/ppermute | solution.py:26
  972.1 14.4 %copy-start.1 = (f32[1,2,256,256]{3,2,1,0:T(8,128)}, f32[1,2,256,256]{3,2,1,0:T(8,128)S(1)}, u32[]{:S(2)}) copy-start(f32[1,2,256,256]{3,2,1,0:T(8,128)S(1)} %fusion.33) | copy-start | bytes 1572868
  972.2 5.2 collective-permute-start.20
  974.1 11.0 %collective-permute-start.21 = (f32[1,1,256,256]{3,2,1,0:T(8,128)S(1)}, f32[1,1,256,256]{3,2,1,0:T(8,128)S(1)}, u32[]{:S(2)}, u32[]{:S(2)}) collective-permute-start(f32[1,1,256,256]{3,2,1,0:T(8,128)S(1)} %get-tuple-element.13), channel_id=1, source_target_pairs={{4,0},{8,4},{12,8},{16,12},{20,16},{24,20},{28,24},{32,28},{36,32}... | collective-permute-start | bytes 786440 | tf_op jit(solution)/shard_map/ppermute | solution.py:26
where the time goes:
time: 988 us; the launch traced here: 987 us
  blocking collectives  755 us (76%)
  starting transfers between devices  71.5 us (7%)
  waiting for transfers between devices  70.8 us (7%)
  local copies, waits for them, and re-layouts  60.3 us (6%)
  other arithmetic  24.5 us (2%)
    another operation x3, blocking collectives  372 us
    unnamed x3, blocking collectives  371 us
    ppermute x11, waiting for transfers between devices, with_halo(): lax.ppermute(head, axis, [((i + 1) % count, i) for i in range(ends)])  68.1 us
    ppermute x11, starting transfers between devices, with_halo(): lax.ppermute(tail, axis, [(i, (i + 1) % count) for i in range(ends)])  47.5 us
    reduce_sum x2, local copies, waits for them, and re-layouts, coarsen(): return jnp.sum(blocks, axis=(count + 1, count + 3, count + 5)) * 0.125  36.2 us
    ppermute x11, starting transfers between devices, with_halo(): lax.ppermute(head, axis, [((i + 1) % count, i) for i in range(ends)])  24 us
  transfers between devices with their start and end apart: 22, of which 13 were waited for; matrix products, arithmetic and copies ran while one was open for 3% of the time, Pallas kernels for 0%

commit v1 on v0

v1 whole, which is shorter than its diff:
```python
import functools

import jax
import jax.numpy as jnp
from jax import lax
from jax.experimental import pallas as pl
from jax.experimental.pallas import tpu as pltpu
from jax.sharding import PartitionSpec as P

WEIGHT = 0.85
COARSE_WEIGHT = 0.6
COARSE_SWEEPS = 3
TILES = 4
CHUNK = 64
f32 = jnp.float32
bf16 = jnp.bfloat16
VM = pl.BlockSpec(memory_space=pltpu.VMEM)
SM = pl.BlockSpec(memory_space=pltpu.SMEM)
PARAMS = pltpu.CompilerParams(vmem_limit_bytes=48 * 1024 * 1024)


def iota(shape, dim):
    return lax.broadcasted_iota(jnp.int32, shape, dim)


def split(x):
    high = x.astype(bf16)
    rest = x - high.astype(f32)
    middle = rest.astype(bf16)
    low = (rest - middle.astype(f32)).astype(bf16)
    return high, middle, low


def dot_exact(x, w):
    high, middle, low = split(x)
    dot = functools.partial(jnp.dot, preferred_element_type=f32)
    return dot(high, w) + (dot(middle, w) + dot(low, w))


def filter_z(y):
    width = y.shape[1]
    lane = iota(y.shape, 1)
    before = jnp.where(lane == 0, 0.0, pltpu.roll(y, 1, 1))
    after = jnp.where(lane == width - 1, 0.0, pltpu.roll(y, width - 1, 1))
    return y + 0.5 * (before + after)


def filter_yz(m):
    rows = m.shape[0]
    y = m + 0.5 * (pltpu.roll(m, 1, 0) + pltpu.roll(m, rows - 1, 0))
    return filter_z(y[8 : rows - 8])


def stencil(ref, i, row, rows):
    part = pl.ds(row, rows + 16)
    return filter_yz(ref[i, part, :] + 0.5 * (ref[i - 1, part, :] + ref[i + 1, part, :]))


def clear_edges(ref):
    layers, rows, width = ref.shape
    zero = jnp.zeros((layers, 8, width), f32)
    ref[:, 0:8, :] = zero
    ref[:, rows - 8 : rows, :] = zero


def chunks(rows, body):
    def step(c, carry):
        body(pl.multiple_of(c * CHUNK, CHUNK))
        return carry

    lax.fori_loop(0, rows // CHUNK, step, 0)


def coarsen_z(rows, width):
    return ((iota((width, width // 2), 0) >> 1) == iota((width, width // 2), 1)).astype(bf16)


def put_halves(ref, i, part, x):
    half = x.shape[1] // 2
    ref[i, 0, part, :] = x[:, :half]
    ref[i, 1, part, :] = x[:, half:]


def pair_rows(ref, i, half):
    even, odd = pl.ds(0, half, stride=2), pl.ds(1, half, stride=2)
    return jnp.concatenate([ref[i, k, even, :] + ref[i, k, odd, :] for k in range(2)], 1)


def gather_kernel(meta, rhs, shard, p1, p2, p3, own):
    count = 4
    rows = shard.shape[1]
    own[0:2] = rhs[0]
    for k, piece in enumerate((shard, p1, p2, p3)):
        owner = lax.rem(meta[2] - k + count, count)
        own[2:4, pl.ds(pl.multiple_of(owner * rows, rows), rows), :] = piece[...]


def first_kernel(
    meta, kappa, own, from_a, from_b,
    s2_out, wd_out, rhs_halo, send_a, send_b, payload,
    s1, s2, wd, rhs_w, work,
):
    core, brick, bricks = meta[0], meta[1], meta[3]
    scale = kappa[0]
    scale1 = 0.25 * scale
    height, width = own.shape[1:]
    half = height // 2
    clear_edges(s1)
    clear_edges(s2)

    base_b = 4 * core
    base_a = 4 * (1 - core)
    valid_lo = (brick > 0).astype(f32)
    valid_hi = (brick < bricks - 1).astype(f32)
    valid_b = jnp.where(core == 0, valid_lo, valid_hi)
    valid_a = jnp.where(core == 0, valid_hi, valid_lo)
    for ref, base, valid in ((from_b, base_b, valid_b), (from_a, base_a, valid_a), (own, 2, None)):
        top = WEIGHT if valid is None else WEIGHT * valid

        def begin(row, ref=ref, base=base, top=top):
            part = pl.ds(row, CHUNK)
            pair = jnp.zeros((CHUNK, width), f32)
            for layer in range(2):
                density = ref[2 + layer, part, :]
                source = ref[layer, part, :]
                factor = top / (density + 14.0 * scale)
                wd[base + layer, part, :] = factor
                rhs_w[base + layer, part, :] = source
                s1[base + layer, pl.ds(row + 8, CHUNK), :] = factor * source
                pair = pair + density
            put_halves(work, base >> 1, part, pair)

        chunks(height, begin)

    for j in range(1, 5):

        def smooth(row, j=j):
            part = pl.ds(row, CHUNK)
            v = s1[j, pl.ds(row + 8, CHUNK), :]
            f = stencil(s1, j, row, CHUNK)
            new = (1.0 - WEIGHT) * v + wd[j, part, :] * (rhs_w[j, part, :] + 2.0 * scale * (f - v))
            s2[j - 1, pl.ds(row + 8, CHUNK), :] = new
            s2_out[j - 1, part, :] = new
            wd_out[j - 1, part, :] = wd[j, part, :]

        chunks(height, smooth)
    rhs_halo[0] = rhs_w[1]
    rhs_halo[1] = rhs_w[4]

    def restrict(row):
        part = pl.ds(row, CHUNK)
        total = jnp.zeros((CHUNK, width), f32)
        for layer in range(2):
            v = s2[1 + layer, pl.ds(row + 8, CHUNK), :]
            f = stencil(s2, 1 + layer, row, CHUNK)
            center = own[2 + layer, part, :] + 16.0 * scale
            total = total + (own[layer, part, :] - center * v + 2.0 * scale * f)
        put_halves(work, 3, part, total)

    chunks(height, restrict)
    columns = coarsen_z(height, width)
    density1 = [0.125 * dot_exact(pair_rows(work, i, half), columns) for i in range(3)]
    coarse_res = 0.125 * dot_exact(pair_rows(work, 3, half), columns)

    send_a[0:half, :] = coarse_res
    send_a[half : 2 * half, :] = density1[1]
    mine = s2_out[1 + core]
    other = s2_out[2 - core]
    send_a[2 * half : 4 * half, :] = mine[:, :half]
    send_a[4 * half : 6 * half, :] = mine[:, half:]
    send_b[0] = other

    first = 0.85 * coarse_res / (density1[1] + 14.0 * scale1)
    pad = jnp.zeros((8, half), f32)
    spread = filter_yz(jnp.concatenate([pad, first, pad], 0))
    own_factor = WEIGHT / (density1[1] + 14.0 * scale1)
    shares = [
        (WEIGHT * valid_lo) * scale1 / (density1[0] + 14.0 * scale1) * spread,
        (1.0 - WEIGHT) * first + own_factor * (coarse_res + 2.0 * scale1 * (spread - first)),
        (WEIGHT * valid_hi) * scale1 / (density1[2] + 14.0 * scale1) * spread,
    ]
    block = half // TILES
    filtered = []
    plain = []
    for e, share in enumerate(shares):
        rest = -(density1[e] + 16.0 * scale1) * share
        if e == 1:
            rest = rest + coarse_res
        for t in range(TILES):
            at = t * block
            row = 2.0 * jnp.sum(share[at : at + block], axis=0, keepdims=True)
            row = row - 0.5 * (share[at : at + 1] + share[at + block - 1 : at + block])
            if t > 0:
                row = row + 0.5 * share[at - 1 : at]
            if t < TILES - 1:
                row = row + 0.5 * share[at + block : at + block + 1]
            filtered.append(row)
            plain.append(jnp.sum(rest[at : at + block], axis=0, keepdims=True))
    for t in range(TILES):
        plain.append(jnp.sum(density1[1][t * block : (t + 1) * block], axis=0, keepdims=True))
    filtered.append(jnp.zeros((4, half), f32))
    filtered = jnp.concatenate(filtered, 0)
    plain = jnp.concatenate(plain, 0)
    cell = iota((half, 128), 0)
    tile = iota((half, 128), 1) & 3
    start = tile * block
    inside = ((cell >= start) & (cell < start + block)).astype(f32)
    ends = ((cell == start) | (cell == start + block - 1)).astype(f32)
    beside = ((cell == start - 1) | (cell == start + block)).astype(f32)
    plain_w = inside.astype(bf16)
    filter_w = (2.0 * inside - 0.5 * ends + 0.5 * beside).astype(bf16)
    row = iota((16, 128), 0)
    lane = iota((16, 128), 1)
    fits = ((lane >> 2) & 3) == (row & 3)
    out = jnp.where(fits & ((lane >> 4) == (row >> 2)), dot_exact(filtered, filter_w), 0.0)
    out = jnp.where(row >= 12, 0.0, out)
    out = out + jnp.where(fits & ((lane >> 4) == (row >> 2) + 3), dot_exact(plain, plain_w), 0.0)
    payload[...] = jnp.broadcast_to(jnp.sum(out, axis=0, keepdims=True), payload.shape)


def lanes_sum(x):
    for step in (16, 32, 64):
        x = x + pltpu.roll(x, step, 1)
    return x


def row_before(x):
    return jnp.where(iota(x.shape, 0) == 0, 0.0, pltpu.roll(x, 1, 0))


def row_after(x):
    return jnp.where(iota(x.shape, 0) == x.shape[0] - 1, 0.0, pltpu.roll(x, x.shape[0] - 1, 0))


def solve_groups(gathered, ids, ids_packed, scale1, block):
    bricks = gathered.shape[0]
    lane = iota(gathered.shape, 1)
    slot = lane >> 4
    up = pltpu.roll(gathered, bricks - 1, 0)
    down = pltpu.roll(gathered, 1, 0)

    def pick(first):
        return lanes_sum(
            jnp.where(
                slot == first,
                up,
                jnp.where(slot == first + 1, gathered, jnp.where(slot == first + 2, down, 0.0)),
            )
        )

    filtered = pick(0)
    plain = pick(3)
    density_sum = lanes_sum(jnp.where(slot == 6, gathered, 0.0))
    remainder = plain + 2.0 * scale1 * filtered + scale1 * (row_before(filtered) + row_after(filtered))

    member = [(ids == ids_packed[j : j + 1]).astype(f32) for j in range(bricks // 8)]
    diagonal_lane = (iota(gathered.shape, 0) & 7) == slot

    def project(x):
        chosen = jnp.where(diagonal_lane, x, 0.0)
        total = jnp.zeros_like(x)
        for j in range(bricks // 8):
            total = total + member[j] * jnp.sum(chosen[8 * j : 8 * j + 8], axis=0, keepdims=True)
        return lanes_sum(total)

    place = iota(ids.shape, 0)
    ids_float = ids.astype(f32)
    as_before = jnp.where((place > 0) & (pltpu.roll(ids_float, 1, 0) == ids_float), 0.5, 0.0)
    as_after = jnp.where((place < bricks - 1) & (pltpu.roll(ids_float, bricks - 1, 0) == ids_float), 0.5, 0.0)
    inner = 2.0 * block - 1.0
    same = inner * inner * (1.0 + as_before + as_after)
    cells = float(block * block)
    diagonal = project(density_sum + scale1 * (16.0 * cells - 2.0 * same))
    group_rhs = project(remainder)
    column = lane & 3
    line = (lane >> 2) & 3
    center = density_sum + 16.0 * cells * scale1

    def image(g):
        z = inner * g + 0.5 * (
            jnp.where(column > 0, pltpu.roll(g, 1, 1), 0.0) + jnp.where(column < 3, pltpu.roll(g, 127, 1), 0.0)
        )
        y = inner * z + 0.5 * (
            jnp.where(line > 0, pltpu.roll(z, 4, 1), 0.0) + jnp.where(line < 3, pltpu.roll(z, 124, 1), 0.0)
        )
        return center * g - 2.0 * scale1 * (y + 0.5 * (row_before(y) + row_after(y)))

    factor = COARSE_WEIGHT / diagonal
    fix = factor * group_rhs
    for _ in range(COARSE_SWEEPS - 1):
        fix = fix + factor * (group_rhs - project(image(fix)))
    return fix


def second_kernel(
    meta, kappa, rhs, rhs_halo, s2, wd, send_a, sib, near_f, near, far, sib_near, sib_far, gathered, ids, ids_packed,
    sol_out, to_a, to_b,
    fixes, cres, cden, c1, c2, c3, grown, s3, s4,
):
    core, brick, bricks = meta[0], meta[1], meta[3]
    scale = kappa[0]
    scale1 = 0.25 * scale
    half = cres.shape[1]
    height, width = rhs.shape[2:]
    block = half // TILES
    for ref in (c1, c2, c3, s3, s4):
        clear_edges(ref)

    fixes[0:8, :] = jnp.zeros((8, 128), f32)
    count = gathered.shape[0]
    fixes[8 + count : 32 + count, :] = jnp.zeros((24, 128), f32)
    fixes[8 : 8 + count, :] = solve_groups(gathered[:, 0, :], ids[...], ids_packed[...], scale1, block)
    window = fixes[pl.ds(brick + 4, 16), :]
    lane = iota((128, TILES * half), 1)
    per = (lane >> (half.bit_length() - 1)) * 4 + ((lane & (half - 1)) >> (block.bit_length() - 1))
    spread = dot_exact(window, (iota((128, TILES * half), 0) == per).astype(bf16))

    sign = 2 * core - 1
    for ref, first, at in (
        (send_a, 0, 0), (sib, 0, -1),
        (near, 0, 1), (near, 2, 2), (far, 0, 3), (far, 2, 4),
        (sib_near, 0, -2), (sib_near, 2, -3), (sib_far, 0, -4),
    ):
        index = 4 + sign * at
        cres[index] = ref[first * half : (first + 1) * half, :]
        cden[index] = ref[(first + 1) * half : (first + 2) * half, :]

    body = pl.ds(8, half)
    factors = []
    for i in range(9):
        place = brick + (i - 4)
        valid = ((place >= 0) & (place < bricks)).astype(f32)
        factor = (WEIGHT * valid) / (cden[i] + 14.0 * scale1)
        cden[i] = factor
        c1[i, body, :] = factor * cres[i]

    def relax(ref, i, k):
        v = ref[i, body, :]
        f = stencil(ref, i, 0, half)
        return (1.0 - WEIGHT) * v + cden[k] * (cres[k] + 2.0 * scale1 * (f - v))

    for i in range(7):
        value = relax(c1, i + 1, i + 1)
        pieces = [
            jnp.broadcast_to(spread[i + 1 : i + 2, t * half : (t + 1) * half], (block, half)) for t in range(TILES)
        ]
        c2[i, body, :] = value + jnp.concatenate(pieces, 0)
    for i in range(5):
        c3[i, body, :] = relax(c2, i + 1, i + 2)
    columns = (iota((half, width), 0) == (iota((half, width), 1) >> 1)).astype(bf16)
    for i in range(3):
        fine = dot_exact(relax(c3, i + 1, i + 3), columns)
        put_halves(grown, i, pl.ds(0, half, stride=2), fine)
        put_halves(grown, i, pl.ds(1, half, stride=2), fine)

    inner = pl.ds(8, height)
    for k in range(2):
        side = slice(k * half, (k + 1) * half)
        for i in range(4):
            s3[i + 1, inner, side] = s2[i, :, side] + grown[(i + 1) >> 1, k]
        s3[5 * core, inner, side] = near_f[0, :, side] + grown[2 * core, k]
        s3[5 * (1 - core), inner, side] = sib[2 * (k + 1) * half : 2 * (k + 2) * half, :] + grown[2 * (1 - core), k]

    for j in range(4):

        def smooth(row, j=j):
            part = pl.ds(row, CHUNK)
            v = s3[j + 1, pl.ds(row + 8, CHUNK), :]
            f = stencil(s3, j + 1, row, CHUNK)
            source = rhs[0, j - 1, part, :] if j in (1, 2) else rhs_halo[j // 3, part, :]
            s4[j, pl.ds(row + 8, CHUNK), :] = (1.0 - WEIGHT) * v + wd[j, part, :] * (source + 2.0 * scale * (f - v))

        chunks(height, smooth)
    for j in range(2):

        def smooth_last(row, j=j):
            part = pl.ds(row, CHUNK)
            v = s4[j + 1, pl.ds(row + 8, CHUNK), :]
            f = stencil(s4, j + 1, row, CHUNK)
            new = (1.0 - WEIGHT) * v + wd[j + 1, part, :] * (rhs[0, j, part, :] + 2.0 * scale * (f - v))
            sol_out[0, j, part, :] = new

        chunks(height, smooth_last)
    to_a[...] = sol_out[0, pl.ds(1 - core, 1), :, :]
    to_b[...] = sol_out[0, pl.ds(core, 1), :, :]


def residual_kernel(meta, kappa, rhs, own, sol, halo_a, halo_b, out, s):
    core = meta[0]
    scale = kappa[0]
    height, width = rhs.shape[2:]
    clear_edges(s)
    inner = pl.ds(8, height)
    s[1, inner, :] = sol[0, 0]
    s[2, inner, :] = sol[0, 1]
    s[3 * core, inner, :] = halo_b[0]
    s[3 * (1 - core), inner, :] = halo_a[0]
    for j in range(2):

        def finish(row, j=j):
            part = pl.ds(row, CHUNK)
            v = s[j + 1, pl.ds(row + 8, CHUNK), :]
            f = stencil(s, j + 1, row, CHUNK)
            center = own[2 + j, part, :] + 16.0 * scale
            out[0, j, part, :] = rhs[0, j, part, :] - center * v + 2.0 * scale * f

        chunks(height, finish)


def shape(*dims):
    return jax.ShapeDtypeStruct(dims, f32)


def local(rhs, density, kappa, block_group):
    bricks = lax.axis_size("brick")
    species = lax.axis_size("spec")
    brick = lax.axis_index("brick")
    height, width = rhs.shape[2:]
    half = height // 2
    meta = jnp.stack([brick % 2, brick, lax.axis_index("spec"), jnp.int32(bricks)]).astype(jnp.int32)
    ids = jnp.tile(block_group, (1, 8))
    ids_packed = block_group.reshape(bricks // 8, 128)
    in_chip = [(i, i ^ 1) for i in range(bricks)]
    next_chip = [(i, ((i + 1) ^ 1) - 1) for i in range(1, bricks - 1)]
    second_chip = [(i, i - 3) for i in range(4, bricks, 2)] + [(i, i + 3) for i in range(1, bricks - 3, 2)]

    def swap_a(x):
        return lax.ppermute(x, "brick", in_chip)

    def swap_b(x):
        return lax.ppermute(x, "brick", next_chip)

    def swap_far(x):
        return lax.ppermute(x, "brick", second_chip)

    def around(x, k):
        return lax.ppermute(x, "spec", [(i, (i + k) % species) for i in range(species)])

    pieces = [around(density, k) for k in (1, 2, 3)]
    own = pl.pallas_call(
        gather_kernel,
        out_shape=shape(4, height, width),
        in_specs=[SM] + [VM] * 5,
        out_specs=VM,
        compiler_params=PARAMS,
        name="collect_density",
    )(meta, rhs, density, *pieces)

    from_b = swap_b(own)
    from_a = swap_a(own)
    s2, wd, rhs_halo, send_a, send_b, payload = pl.pallas_call(
        first_kernel,
        out_shape=(
            shape(4, height, width),
            shape(4, height, width),
            shape(2, height, width),
            shape(6 * half, half),
            shape(1, height, width),
            shape(bricks, 128),
        ),
        in_specs=[SM, SM] + [VM] * 3,
        out_specs=[VM] * 6,
        scratch_shapes=[
            pltpu.VMEM((6, height + 16, width), f32),
            pltpu.VMEM((4, height + 16, width), f32),
            pltpu.VMEM((6, height, width), f32),
            pltpu.VMEM((6, height, width), f32),
            pltpu.VMEM((4, 2, height, half), f32),
        ],
        compiler_params=PARAMS,
        name="smooth_and_restrict",
    )(meta, kappa, own, from_a, from_b)

    gathered = lax.all_to_all(payload.reshape(bricks, 1, 128), "brick", 0, 0, tiled=True)
    sib = swap_a(send_a)
    near_f = swap_b(send_b)
    both = jnp.concatenate([send_a[: 2 * half], sib[: 2 * half]], 0)
    near = swap_b(both)
    far = swap_far(both)
    sib_near = swap_a(near)
    sib_far = swap_a(far)

    solution, to_a, to_b = pl.pallas_call(
        second_kernel,
        out_shape=(shape(1, 2, height, width), shape(1, height, width), shape(1, height, width)),
        in_specs=[SM, SM] + [VM] * 14,
        out_specs=[VM] * 3,
        scratch_shapes=[
            pltpu.VMEM((bricks + 32, 128), f32),
            pltpu.VMEM((9, half, half), f32),
            pltpu.VMEM((9, half, half), f32),
            pltpu.VMEM((9, half + 16, half), f32),
            pltpu.VMEM((7, half + 16, half), f32),
            pltpu.VMEM((5, half + 16, half), f32),
            pltpu.VMEM((3, 2, height, half), f32),
            pltpu.VMEM((6, height + 16, width), f32),
            pltpu.VMEM((4, height + 16, width), f32),
        ],
        compiler_params=PARAMS,
        name="correct_and_smooth",
    )(
        meta, kappa, rhs, rhs_halo, s2, wd, send_a, sib, near_f, near, far, sib_near, sib_far, gathered, ids, ids_packed
    )

    halo_b = swap_b(to_b)
    halo_a = swap_a(to_a)
    residual = pl.pallas_call(
        residual_kernel,
        out_shape=shape(1, 2, height, width),
        in_specs=[SM, SM] + [VM] * 5,
        out_specs=VM,
        scratch_shapes=[pltpu.VMEM((4, height + 16, width), f32)],
        compiler_params=PARAMS,
        name="residual",
    )(meta, kappa, rhs, own, solution, halo_a, halo_b)
    return (solution, residual)


def solution(mesh):
    return jax.shard_map(
        local,
        mesh=mesh,
        in_specs=(P("spec", "brick", None, None), P("brick", "spec", None), P("spec"), P()),
        out_specs=(P("spec", "brick", None, None), P("spec", "brick", None, None)),
        check_vma=False,
    )
```

time: 988 us -> 102 us (0.10)
  the two profiles are of different devices: /device:TPU:103 before, /device:TPU:1 now
where the time goes in v1:
time: 102 us; the launch traced here: 101 us
  waiting for transfers between devices  38.4 us (38%)
  starting transfers between devices  36.5 us (36%)
  Pallas kernels  16.7 us (16%)
  local copies, waits for them, and re-layouts  8.33 us (8%)
  between operations  1.42 us (1%)
    ppermute x4, waiting for transfers between devices, swap_b(): return lax.ppermute(x, 'brick', next_chip)  22.2 us
    all_to_all x1, starting transfers between devices, local(): lax.all_to_all(payload.reshape(bricks, 1, 128), 'brick', 0, 0, tiled=True)  13.4 us
    ppermute x4, starting transfers between devices, swap_b(): return lax.ppermute(x, 'brick', next_chip)  11 us
    all_to_all x1, waiting for transfers between devices, local(): lax.all_to_all(payload.reshape(bricks, 1, 128), 'brick', 0, 0, tiled=True)  9.12 us
    unnamed x21, local copies, waits for them, and re-layouts  8.16 us
    pallas_call x1, Pallas kernels, local(): pl.pallas_call(second_kernel, out_shape=(shape(1, 2, height, width), shap...  7.64 us
    ppermute x3, starting transfers between devices, around(): lax.ppermute(x, 'spec', [(i, (i + k) % species) for i in range(species)])  6.51 us
    pallas_call x1, Pallas kernels, local(): pl.pallas_call(first_kernel, out_shape=(shape(4, height, width), shape(4,...  5.98 us
  transfers between devices with their start and end apart: 14, of which 7 were waited for; matrix products, arithmetic and copies ran while one was open for 0% of the time, Pallas kernels for 0%

profile of v1, /device:TPU:1, one launch (start us, length us, event | category | flops | bytes accessed | tf_op | source)
XLA Modules:
  0.0 101.4 jit_solution(9801406457795573237)
XLA Ops:
  0.6 3.8 %collective-permute-start.1 = (f32[2,64,256]{2,1,0:T(8,128)}, f32[2,64,256]{2,1,0:T(8,128)S(1)}, u32[]{:S(2)}, u32[]{:S(2)}) collective-permute-start(f32[2,64,256]{2,1,0:T(8,128)} %shard.1), channel_id=1, source_target_pairs={{0,2},{1,3},{2,0},{3,1},{4,6},{5,7},{6,4},{7,5},{8,10},{9,11},{10,... | collective-permute-start | bytes 393224 | tf_op jit(solution)/shard_map/ppermute | solution.py:437
  4.5 0.4 collective-permute-start
  4.9 2.3 %collective-permute-start.2 = (f32[2,64,256]{2,1,0:T(8,128)}, f32[2,64,256]{2,1,0:T(8,128)S(1)}, u32[]{:S(2)}, u32[]{:S(2)}) collective-permute-start(f32[2,64,256]{2,1,0:T(8,128)} %shard.1), channel_id=1, source_target_pairs={{0,3},{1,0},{2,1},{3,2},{4,7},{5,4},{6,5},{7,6},{8,11},{9,8},{10,9... | collective-permute-start | bytes 393224 | tf_op jit(solution)/shard_map/ppermute | solution.py:437
  7.1 0.1 pad_add_fusion.meta
  7.2 0.0 collective-permute-done.1.p2
  7.2 4.8 %collective-permute-done.p1 = f32[2,64,256]{2,1,0:T(8,128)S(1)} collective-permute-done((f32[2,64,256]{2,1,0:T(8,128)}, f32[2,64,256]{2,1,0:T(8,128)S(1)}, u32[]{:S(2)}, u32[]{:S(2)}) %collective-permute-start) | collective-permute-done | bytes 131104 | tf_op jit(solution)/shard_map/ppermute | solution.py:437
  12.0 0.0 collective-permute-done.2.p3
  12.0 1.0 %copy-done = f32[1,2,256,256]{3,2,1,0:T(8,128)S(1)} copy-done((f32[1,2,256,256]{3,2,1,0:T(8,128)S(1)}, f32[1,2,256,256]{3,2,1,0:T(8,128)}, u32[]{:S(2)}) %copy-start) | copy-done | bytes 524312
  13.1 0.9 copy-done.7
  14.0 0.6 collect_density.1.own
  14.6 3.3 %collective-permute-start.4 = (f32[4,256,256]{2,1,0:T(8,128)S(1)}, f32[4,256,256]{2,1,0:T(8,128)S(1)}, u32[]{:S(2)}, u32[]{:S(2)}) collective-permute-start(f32[4,256,256]{2,1,0:T(8,128)S(1)} %collect_density.1.own), channel_id=1, source_target_pairs={{4,8},{8,4},{12,16},{16,12},{20,24},{24,20},{28,32},{32,28},{36,40... | collective-permute-start | bytes 3145736 | tf_op jit(solution)/shard_map/ppermute | solution.py:431
  17.9 0.1 collective-permute-start.3
  18.7 12.0 %collective-permute-done.4.from_b = f32[4,256,256]{2,1,0:T(8,128)S(1)} collective-permute-done((f32[4,256,256]{2,1,0:T(8,128)S(1)}, f32[4,256,256]{2,1,0:T(8,128)S(1)}, u32[]{:S(2)}, u32[]{:S(2)}) %collective-permute-start.4) | collective-permute-done | bytes 1048608 | tf_op jit(solution)/shard_map/ppermute | solution.py:431
  30.7 0.0 collective-permute-done.3.from_a
  30.7 1.0 copy-done.8
  31.7 6.0 %smooth_and_restrict.1 = (f32[4,256,256]{2,1,0:T(8,128)S(1)}, f32[4,256,256]{2,1,0:T(8,128)S(1)}, f32[2,256,256]{2,1,0:T(8,128)S(1)}, f32[768,128]{1,0:T(8,128)S...) custom-call(s32[4]{0:T(128)S(1)} %pad_add_fusion.meta, f32[1]{0:T(128)S(6)} %copy.10.kappa, ...), custom_call_target="tpu_custom_call" | custom-call | tf_op jit(solution)/shard_map/smooth_and_restrict/pallas_call | solution.py:451
  37.7 1.0 %copy-done.2 = f32[4,256,256]{2,1,0:T(8,128)} copy-done((f32[4,256,256]{2,1,0:T(8,128)}, f32[4,256,256]{2,1,0:T(8,128)S(1)}, u32[]{:S(2)}) %copy-start.2) | copy-done | bytes 1048600
  38.7 0.8 copy-done.4
  39.5 0.0 collective-permute-start.5
  39.5 0.0 copy-start.1
  39.6 1.7 %collective-permute-done.5.sib = f32[768,128]{1,0:T(8,128)S(1)} collective-permute-done((f32[768,128]{1,0:T(8,128)S(1)}, f32[768,128]{1,0:T(8,128)S(1)}, u32[]{:S(2)}, u32[]{:S(2)}) %collective-permute-start.5) | collective-permute-done | bytes 393248 | tf_op jit(solution)/shard_map/ppermute | solution.py:428
  41.3 4.9 %collective-permute-start.8 = (f32[512,128]{1,0:T(8,128)S(1)}, f32[512,128]{1,0:T(8,128)}, u32[]{:S(2)}, u32[]{:S(2)}) collective-permute-start(f32[512,128]{1,0:T(8,128)S(1)} %pad_maximum_fusion), channel_id=1, source_target_pairs={{16,4},{24,12},{32,20},{40,28},{48,36},{56,44},{64,52},{72,60},{80... | collective-permute-start | bytes 786440 | tf_op jit(solution)/shard_map/ppermute | solution.py:434
  46.2 1.9 %collective-permute-start.7 = (f32[512,128]{1,0:T(8,128)S(1)}, f32[512,128]{1,0:T(8,128)}, u32[]{:S(2)}, u32[]{:S(2)}) collective-permute-start(f32[512,128]{1,0:T(8,128)S(1)} %pad_maximum_fusion), channel_id=1, source_target_pairs={{4,8},{8,4},{12,16},{16,12},{20,24},{24,20},{28,32},{32,28},{36,40... | collective-permute-start | bytes 786440 | tf_op jit(solution)/shard_map/ppermute | solution.py:431
  48.1 3.6 %collective-permute-start.6 = (f32[1,256,256]{2,1,0:T(8,128)}, f32[1,256,256]{2,1,0:T(8,128)}, u32[]{:S(2)}, u32[]{:S(2)}) collective-permute-start(f32[1,256,256]{2,1,0:T(8,128)} %get-tuple-element.15), channel_id=1, source_target_pairs={{4,8},{8,4},{12,16},{16,12},{20,24},{24,20},{28,32},{32,28},{36,40... | collective-permute-start | bytes 786440 | tf_op jit(solution)/shard_map/ppermute | solution.py:431
  51.7 0.6 collective-permute-done.8.far
  52.3 0.0 collective-permute-start.10
  52.3 4.6 %collective-permute-done.7.near = f32[512,128]{1,0:T(8,128)} collective-permute-done((f32[512,128]{1,0:T(8,128)S(1)}, f32[512,128]{1,0:T(8,128)}, u32[]{:S(2)}, u32[]{:S(2)}) %collective-permute-start.7) | collective-permute-done | bytes 262176 | tf_op jit(solution)/shard_map/ppermute | solution.py:431
  56.9 0.0 collective-permute-start.9
  56.9 13.4 %all-to-all-start = ((f32[64,1,128]{2,1,0:T(1,128)}), f32[64,1,128]{2,1,0:T(1,128)S(1)}, u32[]{:S(2)}, u32[]{:S(2)}) async-start(f32[64,1,128]{2,1,0:T(1,128)} %bitcast.3), calls=%async_computation | async-start | bytes 65536 | tf_op jit(solution)/shard_map/all_to_all | solution.py:474
  70.3 0.0 copy-done.9
  70.3 0.1 copy.8
  70.4 0.1 reshape.15.ids_packed
  70.5 0.1 copy.9.ids
  70.5 9.1 %all-to-all-done.gathered = f32[64,1,128]{2,1,0:T(1,128)S(1)} async-done(((f32[64,1,128]{2,1,0:T(1,128)}), f32[64,1,128]{2,1,0:T(1,128)S(1)}, u32[]{:S(2)}, u32[]{:S(2)}) %all-to-all-start) | async-done | bytes 32800 | tf_op jit(solution)/shard_map/all_to_all | solution.py:474
  79.7 0.0 collective-permute-done.6.near_f
  79.7 0.0 collective-permute-done.10.sib_far
  79.7 0.0 collective-permute-done.9.sib_near
  79.7 0.0 copy-done.1
  79.7 0.0 copy-start.3
  79.7 1.2 %copy-done.3 = f32[4,256,256]{2,1,0:T(8,128)S(1)} copy-done((f32[4,256,256]{2,1,0:T(8,128)S(1)}, f32[4,256,256]{2,1,0:T(8,128)}, u32[]{:S(2)}) %copy-start.3) | copy-done | bytes 1048600
  80.9 1.0 %copy-done.5 = f32[2,256,256]{2,1,0:T(8,128)S(1)} copy-done((f32[2,256,256]{2,1,0:T(8,128)S(1)}, f32[2,256,256]{2,1,0:T(8,128)}, u32[]{:S(2)}) %copy-start.5) | copy-done | bytes 524312
  82.0 7.6 %correct_and_smooth.1 = (f32[1,2,256,256]{3,2,1,0:T(8,128)}, f32[1,256,256]{2,1,0:T(8,128)S(1)}, f32[1,256,256]{2,1,0:T(8,128)S(1)}) custom-call(s32[4]{0:T(128)S(1)} %pad_add_fusion.meta, f32[1]{0:T(128)S(6)} %copy.10.kappa, f32[1,2,256,256]{3,2,1,0:T(8,128)S(1)} %copy-done.1, f32[2,256,256]{2,1,0:T(8,128)S(1)} %copy-done.5, ...), custom_call_target="tpu_custom_call" | custom-call | tf_op jit(solution)/shard_map/correct_and_smooth/pallas_call | solution.py:483
  89.6 0.7 collective-permute-start.11
  90.3 2.1 %collective-permute-start.12 = (f32[1,256,256]{2,1,0:T(8,128)S(1)}, f32[1,256,256]{2,1,0:T(8,128)S(1)}, u32[]{:S(2)}, u32[]{:S(2)}) collective-permute-start(f32[1,256,256]{2,1,0:T(8,128)S(1)} %get-tuple-element.19), channel_id=1, source_target_pairs={{4,8},{8,4},{12,16},{16,12},{20,24},{24,20},{28,32},{32,28},{36,40... | collective-permute-start | bytes 786440 | tf_op jit(solution)/shard_map/ppermute | solution.py:431
  92.3 0.0 collective-permute-done.11.halo_a
  92.4 5.6 %collective-permute-done.12.halo_b = f32[1,256,256]{2,1,0:T(8,128)S(1)} collective-permute-done((f32[1,256,256]{2,1,0:T(8,128)S(1)}, f32[1,256,256]{2,1,0:T(8,128)S(1)}, u32[]{:S(2)}, u32[]{:S(2)}) %collective-permute-start.12) | collective-permute-done | bytes 262176 | tf_op jit(solution)/shard_map/ppermute | solution.py:431
  98.0 1.0 %copy-done.6 = f32[1,2,256,256]{3,2,1,0:T(8,128)S(1)} copy-done((f32[1,2,256,256]{3,2,1,0:T(8,128)S(1)}, f32[1,2,256,256]{3,2,1,0:T(8,128)}, u32[]{:S(2)}) %copy-start.6) | copy-done | bytes 524312
  99.0 2.4 %residual.1 = f32[1,2,256,256]{3,2,1,0:T(8,128)} custom-call(s32[4]{0:T(128)S(1)} %pad_add_fusion.meta, f32[1]{0:T(128)S(6)} %copy.10.kappa, f32[1,2,256,256]{3,2,1,0:T(8,128)S(1)} %copy-done.1, f32[4,256,256]{2,1,0:T(8,128)S(1)} %collect_density.1.own, f32[1,2,256,256]{3,2,1,0:T(8,128)S(1)} %copy-done.6, f32[1,256,256]{2,1,0:T(8,128)S(1)} %collective-permute-done.11.halo_a, ...), custom_call_target="tpu_custom_call" | custom-call | tf_op jit(solution)/shard_map/residual/pallas_call | solution.py:507
  (12 shorter events, 0.1 us)
Async XLA Ops:
  0.6 6.6 %collective-permute-start.1 = (f32[2,64,256]{2,1,0:T(8,128)}, f32[2,64,256]{2,1,0:T(8,128)S(1)}, u32[]{:S(2)}, u32[]{:S(2)}) collective-permute-start(f32[2,64,256]{2,1,0:T(8,128)} %shard.1), channel_id=1, source_target_pairs={{0,2},{1,3},{2,0},{3,1},{4,6},{5,7},{6,4},{7,5},{8,10},{9,11},{10,... | collective-permute-start | bytes 393224 | tf_op jit(solution)/shard_map/ppermute | solution.py:437
  4.5 7.6 %collective-permute-start = (f32[2,64,256]{2,1,0:T(8,128)}, f32[2,64,256]{2,1,0:T(8,128)S(1)}, u32[]{:S(2)}, u32[]{:S(2)}) collective-permute-start(f32[2,64,256]{2,1,0:T(8,128)} %shard.1), channel_id=1, source_target_pairs={{0,1},{1,2},{2,3},{3,0},{4,5},{5,6},{6,7},{7,4},{8,9},{9,10},{10,1... | collective-permute-start | bytes 393224 | tf_op jit(solution)/shard_map/ppermute | solution.py:437
  4.9 7.2 %collective-permute-start.2 = (f32[2,64,256]{2,1,0:T(8,128)}, f32[2,64,256]{2,1,0:T(8,128)S(1)}, u32[]{:S(2)}, u32[]{:S(2)}) collective-permute-start(f32[2,64,256]{2,1,0:T(8,128)} %shard.1), channel_id=1, source_target_pairs={{0,3},{1,0},{2,1},{3,2},{4,7},{5,4},{6,5},{7,6},{8,11},{9,8},{10,9... | collective-permute-start | bytes 393224 | tf_op jit(solution)/shard_map/ppermute | solution.py:437
  12.0 1.0 %copy-start = (f32[1,2,256,256]{3,2,1,0:T(8,128)S(1)}, f32[1,2,256,256]{3,2,1,0:T(8,128)}, u32[]{:S(2)}) copy-start(f32[1,2,256,256]{3,2,1,0:T(8,128)} %rhs.5) | copy-start | bytes 1572868
  13.1 0.9 copy-start.7
  14.6 16.1 %collective-permute-start.4 = (f32[4,256,256]{2,1,0:T(8,128)S(1)}, f32[4,256,256]{2,1,0:T(8,128)S(1)}, u32[]{:S(2)}, u32[]{:S(2)}) collective-permute-start(f32[4,256,256]{2,1,0:T(8,128)S(1)} %collect_density.1.own), channel_id=1, source_target_pairs={{4,8},{8,4},{12,16},{16,12},{20,24},{24,20},{28,32},{32,28},{36,40... | collective-permute-start | bytes 3145736 | tf_op jit(solution)/shard_map/ppermute | solution.py:431
  17.9 12.8 %collective-permute-start.3 = (f32[4,256,256]{2,1,0:T(8,128)S(1)}, f32[4,256,256]{2,1,0:T(8,128)S(1)}, u32[]{:S(2)}, u32[]{:S(2)}) collective-permute-start(f32[4,256,256]{2,1,0:T(8,128)S(1)} %collect_density.1.own), channel_id=1, source_target_pairs={{0,4},{4,0},{8,12},{12,8},{16,20},{20,16},{24,28},{28,24},{32,36},... | collective-permute-start | bytes 3145736 | tf_op jit(solution)/shard_map/ppermute | solution.py:428
  30.7 1.0 %copy-start.8 = (f32[4,256,256]{2,1,0:T(8,128)}, f32[4,256,256]{2,1,0:T(8,128)S(1)}, u32[]{:S(2)}) copy-start(f32[4,256,256]{2,1,0:T(8,128)S(1)} %collective-permute-done.4.from_b) | copy-start | bytes 3145732
  37.7 1.0 %copy-start.2 = (f32[4,256,256]{2,1,0:T(8,128)}, f32[4,256,256]{2,1,0:T(8,128)S(1)}, u32[]{:S(2)}) copy-start(f32[4,256,256]{2,1,0:T(8,128)S(1)} %get-tuple-element.13.wd) | copy-start | bytes 3145732
  38.7 0.8 copy-start.4
  39.5 1.7 %collective-permute-start.5 = (f32[768,128]{1,0:T(8,128)S(1)}, f32[768,128]{1,0:T(8,128)S(1)}, u32[]{:S(2)}, u32[]{:S(2)}) collective-permute-start(f32[768,128]{1,0:T(8,128)S(1)} %get-tuple-element.14.send_a), channel_id=1, source_target_pairs={{0,4},{4,0},{8,12},{12,8},{16,20},{20,16},{24,28},{28,24},{32,36},... | collective-permute-start | bytes 1179656 | tf_op jit(solution)/shard_map/ppermute | solution.py:428
  39.5 40.1 %copy-start.1 = (f32[1,2,256,256]{3,2,1,0:T(8,128)S(1)}, f32[1,2,256,256]{3,2,1,0:T(8,128)}, u32[]{:S(2)}) copy-start(f32[1,2,256,256]{3,2,1,0:T(8,128)} %rhs.5) | copy-start | bytes 1572868
  41.3 11.0 %collective-permute-start.8 = (f32[512,128]{1,0:T(8,128)S(1)}, f32[512,128]{1,0:T(8,128)}, u32[]{:S(2)}, u32[]{:S(2)}) collective-permute-start(f32[512,128]{1,0:T(8,128)S(1)} %pad_maximum_fusion), channel_id=1, source_target_pairs={{16,4},{24,12},{32,20},{40,28},{48,36},{56,44},{64,52},{72,60},{80... | collective-permute-start | bytes 786440 | tf_op jit(solution)/shard_map/ppermute | solution.py:434
  46.2 10.7 %collective-permute-start.7 = (f32[512,128]{1,0:T(8,128)S(1)}, f32[512,128]{1,0:T(8,128)}, u32[]{:S(2)}, u32[]{:S(2)}) collective-permute-start(f32[512,128]{1,0:T(8,128)S(1)} %pad_maximum_fusion), channel_id=1, source_target_pairs={{4,8},{8,4},{12,16},{16,12},{20,24},{24,20},{28,32},{32,28},{36,40... | collective-permute-start | bytes 786440 | tf_op jit(solution)/shard_map/ppermute | solution.py:431
  48.1 31.6 %collective-permute-start.6 = (f32[1,256,256]{2,1,0:T(8,128)}, f32[1,256,256]{2,1,0:T(8,128)}, u32[]{:S(2)}, u32[]{:S(2)}) collective-permute-start(f32[1,256,256]{2,1,0:T(8,128)} %get-tuple-element.15), channel_id=1, source_target_pairs={{4,8},{8,4},{12,16},{16,12},{20,24},{24,20},{28,32},{32,28},{36,40... | collective-permute-start | bytes 786440 | tf_op jit(solution)/shard_map/ppermute | solution.py:431
  52.3 27.4 %collective-permute-start.10 = (f32[512,128]{1,0:T(8,128)}, f32[512,128]{1,0:T(8,128)}, u32[]{:S(2)}, u32[]{:S(2)}) collective-permute-start(f32[512,128]{1,0:T(8,128)} %collective-permute-done.8.far), channel_id=1, source_target_pairs={{0,4},{4,0},{8,12},{12,8},{16,20},{20,16},{24,28},{28,24},{32,36},... | collective-permute-start | bytes 786440 | tf_op jit(solution)/shard_map/ppermute | solution.py:428
  56.9 22.8 %collective-permute-start.9 = (f32[512,128]{1,0:T(8,128)}, f32[512,128]{1,0:T(8,128)}, u32[]{:S(2)}, u32[]{:S(2)}) collective-permute-start(f32[512,128]{1,0:T(8,128)} %collective-permute-done.7.near), channel_id=1, source_target_pairs={{0,4},{4,0},{8,12},{12,8},{16,20},{20,16},{24,28},{28,24},{32,36},... | collective-permute-start | bytes 786440 | tf_op jit(solution)/shard_map/ppermute | solution.py:428
  56.9 13.4 %copy-start.9 = (s32[64,16]{0,1:T(8,128)S(1)}, s32[64,16]{0,1:T(8,128)}, u32[]{:S(2)}) copy-start(s32[64,16]{0,1:T(8,128)} %param.7) | copy-start | bytes 12292
  56.9 22.8 %all-to-all-start = ((f32[64,1,128]{2,1,0:T(1,128)}), f32[64,1,128]{2,1,0:T(1,128)S(1)}, u32[]{:S(2)}, u32[]{:S(2)}) async-start(f32[64,1,128]{2,1,0:T(1,128)} %bitcast.3), calls=%async_computation | async-start | bytes 65536 | tf_op jit(solution)/shard_map/all_to_all | solution.py:474
  79.7 1.2 %copy-start.3 = (f32[4,256,256]{2,1,0:T(8,128)S(1)}, f32[4,256,256]{2,1,0:T(8,128)}, u32[]{:S(2)}) copy-start(f32[4,256,256]{2,1,0:T(8,128)} %copy-done.2) | copy-start | bytes 3145732
  80.9 1.0 %copy-start.5 = (f32[2,256,256]{2,1,0:T(8,128)S(1)}, f32[2,256,256]{2,1,0:T(8,128)}, u32[]{:S(2)}) copy-start(f32[2,256,256]{2,1,0:T(8,128)} %copy-done.4) | copy-start | bytes 1572868
  89.6 2.8 %collective-permute-start.11 = (f32[1,256,256]{2,1,0:T(8,128)S(1)}, f32[1,256,256]{2,1,0:T(8,128)S(1)}, u32[]{:S(2)}, u32[]{:S(2)}) collective-permute-start(f32[1,256,256]{2,1,0:T(8,128)S(1)} %get-tuple-element.18), channel_id=1, source_target_pairs={{0,4},{4,0},{8,12},{12,8},{16,20},{20,16},{24,28},{28,24},{32,36},... | collective-permute-start | bytes 786440 | tf_op jit(solution)/shard_map/ppermute | solution.py:428
  90.3 7.7 %collective-permute-start.12 = (f32[1,256,256]{2,1,0:T(8,128)S(1)}, f32[1,256,256]{2,1,0:T(8,128)S(1)}, u32[]{:S(2)}, u32[]{:S(2)}) collective-permute-start(f32[1,256,256]{2,1,0:T(8,128)S(1)} %get-tuple-element.19), channel_id=1, source_target_pairs={{4,8},{8,4},{12,16},{16,12},{20,24},{24,20},{28,32},{32,28},{36,40... | collective-permute-start | bytes 786440 | tf_op jit(solution)/shard_map/ppermute | solution.py:431
  98.0 1.0 %copy-start.6 = (f32[1,2,256,256]{3,2,1,0:T(8,128)S(1)}, f32[1,2,256,256]{3,2,1,0:T(8,128)}, u32[]{:S(2)}) copy-start(f32[1,2,256,256]{3,2,1,0:T(8,128)} %get-tuple-element.9.sol) | copy-start | bytes 1572868

commit v2 on v1

--- a/solution.py
+++ b/solution.py
@@ -15,8 +15,8 @@
 f32 = jnp.float32
 bf16 = jnp.bfloat16
 VM = pl.BlockSpec(memory_space=pltpu.VMEM)
-SM = pl.BlockSpec(memory_space=pltpu.SMEM)
-PARAMS = pltpu.CompilerParams(vmem_limit_bytes=48 * 1024 * 1024)
+ANY = pl.BlockSpec(memory_space=pl.ANY)
+PARAMS = pltpu.CompilerParams(vmem_limit_bytes=16 * 1024 * 1024)
 
 
 def iota(shape, dim):
@@ -86,27 +86,58 @@
     return jnp.concatenate([ref[i, k, even, :] + ref[i, k, odd, :] for k in range(2)], 1)
 
 
-def gather_kernel(meta, rhs, shard, p1, p2, p3, own):
+def position():
+    brick = lax.axis_index("brick")
+    return brick & 1, brick, lax.axis_size("brick")
+
+
+def start_all(copies):
+    for copy in copies:
+        copy.start()
+
+
+def wait_all(copies):
+    for copy in copies:
+        copy.wait()
+
+
+def join_kernel(mine, other, out, sems):
+    rows = out.shape[0] // 2
+    copies = [
+        pltpu.make_async_copy(mine.at[pl.ds(0, rows)], out.at[pl.ds(0, rows)], sems.at[0]),
+        pltpu.make_async_copy(other.at[pl.ds(0, rows)], out.at[pl.ds(rows, rows)], sems.at[1]),
+    ]
+    start_all(copies)
+    wait_all(copies)
+
+
+def gather_kernel(shard, p1, p2, p3, dens, sems):
     count = 4
     rows = shard.shape[1]
-    own[0:2] = rhs[0]
+    copies = []
     for k, piece in enumerate((shard, p1, p2, p3)):
-        owner = lax.rem(meta[2] - k + count, count)
-        own[2:4, pl.ds(pl.multiple_of(owner * rows, rows), rows), :] = piece[...]
+        owner = lax.rem(lax.axis_index("spec") - k + count, count)
+        place = pl.ds(pl.multiple_of(owner * rows, rows), rows)
+        copies.append(pltpu.make_async_copy(piece, dens.at[:, place, :], sems.at[k]))
+    start_all(copies)
+    wait_all(copies)
 
 
 def first_kernel(
-    meta, kappa, own, from_a, from_b,
-    s2_out, wd_out, rhs_halo, send_a, send_b, payload,
-    s1, s2, wd, rhs_w, work,
+    kappa_in, rhs, dens, rhs_a, dens_a, rhs_b, dens_b,
+    s2_out, halo_out, send_a, send_b, payload,
+    s1, s2, wd, rhs_w, work, kappa, sems,
 ):
-    core, brick, bricks = meta[0], meta[1], meta[3]
-    scale = kappa[0]
-    scale1 = 0.25 * scale
-    height, width = own.shape[1:]
+    core, brick, bricks = position()
+    load = pltpu.make_async_copy(kappa_in, kappa, sems.at[0])
+    load.start()
+    height, width = dens.shape[1:]
     half = height // 2
     clear_edges(s1)
     clear_edges(s2)
+    load.wait()
+    scale = kappa[0]
+    scale1 = 0.25 * scale
 
     base_b = 4 * core
     base_a = 4 * (1 - core)
@@ -114,17 +145,17 @@
     valid_hi = (brick < bricks - 1).astype(f32)
     valid_b = jnp.where(core == 0, valid_lo, valid_hi)
     valid_a = jnp.where(core == 0, valid_hi, valid_lo)
-    for ref, base, valid in ((from_b, base_b, valid_b), (from_a, base_a, valid_a), (own, 2, None)):
+    for ref, density_ref, base, valid in ((rhs_b, dens_b, base_b, valid_b), (rhs_a, dens_a, base_a, valid_a), (rhs, dens, 2, None)):
         top = WEIGHT if valid is None else WEIGHT * valid
 
-        def begin(row, ref=ref, base=base, top=top):
+        def begin(row, ref=ref, density_ref=density_ref, base=base, top=top):
             part = pl.ds(row, CHUNK)
             pair = jnp.zeros((CHUNK, width), f32)
             for layer in range(2):
-                density = ref[2 + layer, part, :]
-                source = ref[layer, part, :]
+                density = density_ref[layer, part, :]
                 factor = top / (density + 14.0 * scale)
                 wd[base + layer, part, :] = factor
+                source = ref[0, layer, part, :]
                 rhs_w[base + layer, part, :] = source
                 s1[base + layer, pl.ds(row + 8, CHUNK), :] = factor * source
                 pair = pair + density
@@ -141,11 +172,16 @@
             new = (1.0 - WEIGHT) * v + wd[j, part, :] * (rhs_w[j, part, :] + 2.0 * scale * (f - v))
             s2[j - 1, pl.ds(row + 8, CHUNK), :] = new
             s2_out[j - 1, part, :] = new
-            wd_out[j - 1, part, :] = wd[j, part, :]
 
         chunks(height, smooth)
-    rhs_halo[0] = rhs_w[1]
-    rhs_halo[1] = rhs_w[4]
+    halo_out[0] = rhs_w[1]
+    halo_out[1] = rhs_w[4]
+    for ref, layer, edge in ((dens_b, 1 - core, core), (dens_a, core, 1 - core)):
+        halo_out[2 + edge] = ref[layer]
+    mine = 1 + core
+    send_a[2 * half : 4 * half, :] = s2_out[mine, :, :half]
+    send_a[4 * half : 6 * half, :] = s2_out[mine, :, half:]
+    send_b[0] = s2_out[2 - core]
 
     def restrict(row):
         part = pl.ds(row, CHUNK)
@@ -153,8 +189,8 @@
         for layer in range(2):
             v = s2[1 + layer, pl.ds(row + 8, CHUNK), :]
             f = stencil(s2, 1 + layer, row, CHUNK)
-            center = own[2 + layer, part, :] + 16.0 * scale
-            total = total + (own[layer, part, :] - center * v + 2.0 * scale * f)
+            center = dens[layer, part, :] + 16.0 * scale
+            total = total + (rhs_w[2 + layer, part, :] - center * v + 2.0 * scale * f)
         put_halves(work, 3, part, total)
 
     chunks(height, restrict)
@@ -164,11 +200,6 @@
 
     send_a[0:half, :] = coarse_res
     send_a[half : 2 * half, :] = density1[1]
-    mine = s2_out[1 + core]
-    other = s2_out[2 - core]
-    send_a[2 * half : 4 * half, :] = mine[:, :half]
-    send_a[4 * half : 6 * half, :] = mine[:, half:]
-    send_b[0] = other
 
     first = 0.85 * coarse_res / (density1[1] + 14.0 * scale1)
     pad = jnp.zeros((8, half), f32)
@@ -232,7 +263,7 @@
     return jnp.where(iota(x.shape, 0) == x.shape[0] - 1, 0.0, pltpu.roll(x, x.shape[0] - 1, 0))
 
 
-def solve_groups(gathered, ids, ids_packed, scale1, block):
+def solve_groups(gathered, groups, scale1, block):
     bricks = gathered.shape[0]
     lane = iota(gathered.shape, 1)
     slot = lane >> 4
@@ -253,8 +284,14 @@
     density_sum = lanes_sum(jnp.where(slot == 6, gathered, 0.0))
     remainder = plain + 2.0 * scale1 * filtered + scale1 * (row_before(filtered) + row_after(filtered))
 
-    member = [(ids == ids_packed[j : j + 1]).astype(f32) for j in range(bricks // 8)]
+    blocks = groups.shape[1]
+    repeat = (iota((blocks, 128), 0) == (iota((blocks, 128), 1) & (blocks - 1))).astype(bf16)
+    ids = jnp.dot(groups.astype(f32).astype(bf16), repeat, preferred_element_type=f32)
     diagonal_lane = (iota(gathered.shape, 0) & 7) == slot
+    packed = jnp.where(diagonal_lane, ids, 0.0)
+    member = [
+        (ids == jnp.sum(packed[8 * j : 8 * j + 8], axis=0, keepdims=True)).astype(f32) for j in range(bricks // 8)
+    ]
 
     def project(x):
         chosen = jnp.where(diagonal_lane, x, 0.0)
@@ -264,9 +301,8 @@
         return lanes_sum(total)
 
     place = iota(ids.shape, 0)
-    ids_float = ids.astype(f32)
-    as_before = jnp.where((place > 0) & (pltpu.roll(ids_float, 1, 0) == ids_float), 0.5, 0.0)
-    as_after = jnp.where((place < bricks - 1) & (pltpu.roll(ids_float, bricks - 1, 0) == ids_float), 0.5, 0.0)
+    as_before = jnp.where((place > 0) & (pltpu.roll(ids, 1, 0) == ids), 0.5, 0.0)
+    as_after = jnp.where((place < bricks - 1) & (pltpu.roll(ids, bricks - 1, 0) == ids), 0.5, 0.0)
     inner = 2.0 * block - 1.0
     same = inner * inner * (1.0 + as_before + as_after)
     cells = float(block * block)
@@ -293,23 +329,27 @@
 
 
 def second_kernel(
-    meta, kappa, rhs, rhs_halo, s2, wd, send_a, sib, near_f, near, far, sib_near, sib_far, gathered, ids, ids_packed,
+    kappa_in, rhs, dens, halo, s2, near_f, send_a, sib, near, far, sib_near, sib_far, gathered, groups,
     sol_out, to_a, to_b,
-    fixes, cres, cden, c1, c2, c3, grown, s3, s4,
+    fixes, cres, cden, c1, c2, c3, grown, s3, s4, wd, kappa, sems,
 ):
-    core, brick, bricks = meta[0], meta[1], meta[3]
-    scale = kappa[0]
-    scale1 = 0.25 * scale
+    core, brick, bricks = position()
+    load = pltpu.make_async_copy(kappa_in, kappa, sems.at[0])
+    load.start()
     half = cres.shape[1]
     height, width = rhs.shape[2:]
     block = half // TILES
+    inner = pl.ds(8, height)
     for ref in (c1, c2, c3, s3, s4):
         clear_edges(ref)
+    load.wait()
+    scale = kappa[0]
+    scale1 = 0.25 * scale
 
     fixes[0:8, :] = jnp.zeros((8, 128), f32)
     count = gathered.shape[0]
     fixes[8 + count : 32 + count, :] = jnp.zeros((24, 128), f32)
-    fixes[8 : 8 + count, :] = solve_groups(gathered[:, 0, :], ids[...], ids_packed[...], scale1, block)
+    fixes[8 : 8 + count, :] = solve_groups(gathered[:, 0, :], groups[...], scale1, block)
     window = fixes[pl.ds(brick + 4, 16), :]
     lane = iota((128, TILES * half), 1)
     per = (lane >> (half.bit_length() - 1)) * 4 + ((lane & (half - 1)) >> (block.bit_length() - 1))
@@ -353,7 +393,6 @@
         put_halves(grown, i, pl.ds(0, half, stride=2), fine)
         put_halves(grown, i, pl.ds(1, half, stride=2), fine)
 
-    inner = pl.ds(8, height)
     for k in range(2):
         side = slice(k * half, (k + 1) * half)
         for i in range(4):
@@ -367,8 +406,16 @@
             part = pl.ds(row, CHUNK)
             v = s3[j + 1, pl.ds(row + 8, CHUNK), :]
             f = stencil(s3, j + 1, row, CHUNK)
-            source = rhs[0, j - 1, part, :] if j in (1, 2) else rhs_halo[j // 3, part, :]
-            s4[j, pl.ds(row + 8, CHUNK), :] = (1.0 - WEIGHT) * v + wd[j, part, :] * (source + 2.0 * scale * (f - v))
+            if j in (1, 2):
+                source, density, top = rhs[0, j - 1, part, :], dens[j - 1, part, :], WEIGHT
+            else:
+                edge = j // 3
+                source, density = halo[edge, part, :], halo[2 + edge, part, :]
+                top = WEIGHT * (brick < bricks - 1 if edge else brick > 0).astype(f32)
+            factor = top / (density + 14.0 * scale)
+            wd[j, part, :] = factor
+            new = (1.0 - WEIGHT) * v + factor * (source + 2.0 * scale * (f - v))
+            s4[j, pl.ds(row + 8, CHUNK), :] = new
 
         chunks(height, smooth)
     for j in range(2):
@@ -385,24 +432,47 @@
     to_b[...] = sol_out[0, pl.ds(core, 1), :, :]
 
 
-def residual_kernel(meta, kappa, rhs, own, sol, halo_a, halo_b, out, s):
-    core = meta[0]
+def inside_kernel(kappa_in, rhs, dens, sol_in, out, s, kappa, sems):
+    height, width = dens.shape[1:]
+    inner = pl.ds(8, height)
+    loads = [
+        pltpu.make_async_copy(sol_in.at[0], s.at[:, inner, :], sems.at[0]),
+        pltpu.make_async_copy(kappa_in, kappa, sems.at[1]),
+    ]
+    start_all(loads)
+    clear_edges(s)
+    wait_all(loads)
     scale = kappa[0]
-    height, width = rhs.shape[2:]
-    clear_edges(s)
-    inner = pl.ds(8, height)
-    s[1, inner, :] = sol[0, 0]
-    s[2, inner, :] = sol[0, 1]
-    s[3 * core, inner, :] = halo_b[0]
-    s[3 * (1 - core), inner, :] = halo_a[0]
     for j in range(2):
 
         def finish(row, j=j):
             part = pl.ds(row, CHUNK)
-            v = s[j + 1, pl.ds(row + 8, CHUNK), :]
-            f = stencil(s, j + 1, row, CHUNK)
-            center = own[2 + j, part, :] + 16.0 * scale
-            out[0, j, part, :] = rhs[0, j, part, :] - center * v + 2.0 * scale * f
+            more = pl.ds(row, CHUNK + 16)
+            f = filter_yz(s[j, more, :] + 0.5 * s[1 - j, more, :])
+            center = dens[j, part, :] + 16.0 * scale
+            out[j, part, :] = rhs[0, j, part, :] - center * s[j, pl.ds(row + 8, CHUNK), :] + 2.0 * scale * f
+
+        chunks(height, finish)
+
+
+def residual_kernel(kappa_in, inside, halo_a, halo_b, out, s, kappa, sems):
+    core = position()[0]
+    height = inside.shape[1]
+    inner = pl.ds(8, height)
+    loads = [
+        pltpu.make_async_copy(halo_b.at[0], s.at[core, inner, :], sems.at[0]),
+        pltpu.make_async_copy(halo_a.at[0], s.at[1 - core, inner, :], sems.at[1]),
+        pltpu.make_async_copy(kappa_in, kappa, sems.at[2]),
+    ]
+    start_all(loads)
+    clear_edges(s)
+    wait_all(loads)
+    scale = kappa[0]
+    for j in range(2):
+
+        def finish(row, j=j):
+            part = pl.ds(row, CHUNK)
+            out[0, j, part, :] = inside[j, part, :] + scale * filter_yz(s[j, pl.ds(row, CHUNK + 16), :])
 
         chunks(height, finish)
 
@@ -414,12 +484,8 @@
 def local(rhs, density, kappa, block_group):
     bricks = lax.axis_size("brick")
     species = lax.axis_size("spec")
-    brick = lax.axis_index("brick")
     height, width = rhs.shape[2:]
     half = height // 2
-    meta = jnp.stack([brick % 2, brick, lax.axis_index("spec"), jnp.int32(bricks)]).astype(jnp.int32)
-    ids = jnp.tile(block_group, (1, 8))
-    ids_packed = block_group.reshape(bricks // 8, 128)
     in_chip = [(i, i ^ 1) for i in range(bricks)]
     next_chip = [(i, ((i + 1) ^ 1) - 1) for i in range(1, bricks - 1)]
     second_chip = [(i, i - 3) for i in range(4, bricks, 2)] + [(i, i + 3) for i in range(1, bricks - 3, 2)]
@@ -437,53 +503,66 @@
         return lax.ppermute(x, "spec", [(i, (i + k) % species) for i in range(species)])
 
     pieces = [around(density, k) for k in (1, 2, 3)]
-    own = pl.pallas_call(
+    rhs_b = swap_b(rhs)
+    rhs_a = swap_a(rhs)
+    dens = pl.pallas_call(
         gather_kernel,
-        out_shape=shape(4, height, width),
-        in_specs=[SM] + [VM] * 5,
+        out_shape=shape(2, height, width),
+        in_specs=[ANY] * 4,
         out_specs=VM,
+        scratch_shapes=[pltpu.SemaphoreType.DMA((4,))],
         compiler_params=PARAMS,
         name="collect_density",
-    )(meta, rhs, density, *pieces)
-
-    from_b = swap_b(own)
-    from_a = swap_a(own)
-    s2, wd, rhs_halo, send_a, send_b, payload = pl.pallas_call(
+    )(density, *pieces)
+
+    dens_b = swap_b(dens)
+    dens_a = swap_a(dens)
+    s2, halo, send_a, send_b, payload = pl.pallas_call(
         first_kernel,
         out_shape=(
             shape(4, height, width),
             shape(4, height, width),
-            shape(2, height, width),
             shape(6 * half, half),
             shape(1, height, width),
             shape(bricks, 128),
         ),
-        in_specs=[SM, SM] + [VM] * 3,
-        out_specs=[VM] * 6,
+        in_specs=[ANY] + [VM] * 6,
+        out_specs=[VM] * 5,
         scratch_shapes=[
             pltpu.VMEM((6, height + 16, width), f32),
             pltpu.VMEM((4, height + 16, width), f32),
             pltpu.VMEM((6, height, width), f32),
             pltpu.VMEM((6, height, width), f32),
             pltpu.VMEM((4, 2, height, half), f32),
+            pltpu.SMEM((1,), f32),
+            pltpu.SemaphoreType.DMA((1,)),
         ],
         compiler_params=PARAMS,
         name="smooth_and_restrict",
-    )(meta, kappa, own, from_a, from_b)
+    )(kappa, rhs, dens, rhs_a, dens_a, rhs_b, dens_b)
 
     gathered = lax.all_to_all(payload.reshape(bricks, 1, 128), "brick", 0, 0, tiled=True)
     sib = swap_a(send_a)
     near_f = swap_b(send_b)
-    both = jnp.concatenate([send_a[: 2 * half], sib[: 2 * half]], 0)
+    both = pl.pallas_call(
+        join_kernel,
+        out_shape=shape(4 * half, half),
+        in_specs=[ANY] * 2,
+        out_specs=VM,
+        scratch_shapes=[pltpu.SemaphoreType.DMA((2,))],
+        compiler_params=PARAMS,
+        name="join_chip",
+    )(send_a, sib)
     near = swap_b(both)
     far = swap_far(both)
+    near, far, gathered = lax.optimization_barrier((near, far, gathered))
     sib_near = swap_a(near)
     sib_far = swap_a(far)
 
     solution, to_a, to_b = pl.pallas_call(
         second_kernel,
         out_shape=(shape(1, 2, height, width), shape(1, height, width), shape(1, height, width)),
-        in_specs=[SM, SM] + [VM] * 14,
+        in_specs=[ANY] + [VM] * 13,
         out_specs=[VM] * 3,
         scratch_shapes=[
             pltpu.VMEM((bricks + 32, 128), f32),
@@ -495,24 +574,36 @@
             pltpu.VMEM((3, 2, height, half), f32),
             pltpu.VMEM((6, height + 16, width), f32),
             pltpu.VMEM((4, height + 16, width), f32),
+            pltpu.VMEM((4, height, width), f32),
+            pltpu.SMEM((1,), f32),
+            pltpu.SemaphoreType.DMA((1,)),
         ],
         compiler_params=PARAMS,
         name="correct_and_smooth",
     )(
-        meta, kappa, rhs, rhs_halo, s2, wd, send_a, sib, near_f, near, far, sib_near, sib_far, gathered, ids, ids_packed
+        kappa, rhs, dens, halo, s2, near_f, send_a, sib, near, far, sib_near, sib_far, gathered, block_group
     )
 
     halo_b = swap_b(to_b)
     halo_a = swap_a(to_a)
+    inside = pl.pallas_call(
+        inside_kernel,
+        out_shape=shape(2, height, width),
+        in_specs=[ANY] + [VM] * 2 + [ANY],
+        out_specs=VM,
+        scratch_shapes=[pltpu.VMEM((2, height + 16, width), f32), pltpu.SMEM((1,), f32), pltpu.SemaphoreType.DMA((2,))],
+        compiler_params=PARAMS,
+        name="residual_inside",
+    )(kappa, rhs, dens, solution)
     residual = pl.pallas_call(
         residual_kernel,
         out_shape=shape(1, 2, height, width),
-        in_specs=[SM, SM] + [VM] * 5,
+        in_specs=[ANY, VM] + [ANY] * 2,
         out_specs=VM,
-        scratch_shapes=[pltpu.VMEM((4, height + 16, width), f32)],
+        scratch_shapes=[pltpu.VMEM((2, height + 16, width), f32), pltpu.SMEM((1,), f32), pltpu.SemaphoreType.DMA((3,))],
         compiler_params=PARAMS,
         name="residual",
-    )(meta, kappa, rhs, own, solution, halo_a, halo_b)
+    )(kappa, inside, halo_a, halo_b)
     return (solution, residual)
 
 

time: 102 us -> 86.1 us (0.84)
  the two profiles are of different devices: /device:TPU:1 before, /device:TPU:103 now
where the time goes in v2:
time: 86.1 us; the launch traced here: 85.6 us
  starting transfers between devices  40.5 us (47%)
  waiting for transfers between devices  20.7 us (24%)
  Pallas kernels  18.7 us (22%)
  local copies, waits for them, and re-layouts  4.25 us (5%)
  between operations  1.49 us (2%)
    ppermute x5, starting transfers between devices, swap_b(): return lax.ppermute(x, 'brick', next_chip)  23.1 us
    ppermute x5, waiting for transfers between devices, swap_b(): return lax.ppermute(x, 'brick', next_chip)  18.7 us
    all_to_all x1, starting transfers between devices, local(): lax.all_to_all(payload.reshape(bricks, 1, 128), 'brick', 0, 0, tiled=True)  8.46 us
    pallas_call x1, Pallas kernels, local(): pl.pallas_call(second_kernel, out_shape=(shape(1, 2, height, width), shap...  8.07 us
    ppermute x3, starting transfers between devices, around(): lax.ppermute(x, 'spec', [(i, (i + k) % species) for i in range(species)])  5.68 us
    pallas_call x1, Pallas kernels, local(): pl.pallas_call(first_kernel, out_shape=(shape(4, height, width), shape(4,...  5.31 us
    unnamed x15, local copies, waits for them, and re-layouts  4.25 us
    pallas_call x1, Pallas kernels, local(): pl.pallas_call(residual_kernel, out_shape=shape(1, 2, height, width), in_...  2.33 us
  transfers between devices with their start and end apart: 16, of which 6 were waited for; matrix products, arithmetic and copies ran while one was open for 0% of the time, Pallas kernels for 2%

profile of v2, /device:TPU:103, one launch (start us, length us, event | category | flops | bytes accessed | tf_op | source)
XLA Modules:
  0.0 85.6 jit_solution(124563526733990602)
XLA Ops:
  0.6 0.0 copy-start
  0.6 3.0 %collective-permute-start.1 = (f32[2,64,256]{2,1,0:T(8,128)}, f32[2,64,256]{2,1,0:T(8,128)S(1)}, u32[]{:S(2)}, u32[]{:S(2)}) collective-permute-start(f32[2,64,256]{2,1,0:T(8,128)} %shard.1), channel_id=1, source_target_pairs={{0,2},{1,3},{2,0},{3,1},{4,6},{5,7},{6,4},{7,5},{8,10},{9,11},{10,... | collective-permute-start | bytes 393224 | tf_op jit(solution)/shard_map/ppermute | solution.py:503
  3.6 0.4 collective-permute-start
  4.0 2.3 %collective-permute-start.2 = (f32[2,64,256]{2,1,0:T(8,128)}, f32[2,64,256]{2,1,0:T(8,128)S(1)}, u32[]{:S(2)}, u32[]{:S(2)}) collective-permute-start(f32[2,64,256]{2,1,0:T(8,128)} %shard.1), channel_id=1, source_target_pairs={{0,3},{1,0},{2,1},{3,2},{4,7},{5,4},{6,5},{7,6},{8,11},{9,8},{10,9... | collective-permute-start | bytes 393224 | tf_op jit(solution)/shard_map/ppermute | solution.py:503
  6.3 6.1 %collective-permute-start.5 = (f32[1,2,256,256]{3,2,1,0:T(8,128)}, f32[1,2,256,256]{3,2,1,0:T(8,128)S(1)}, u32[]{:S(2)}, u32[]{:S(2)}) collective-permute-start(f32[1,2,256,256]{3,2,1,0:T(8,128)} %rhs.5), channel_id=1, source_target_pairs={{4,8},{8,4},{12,16},{16,12},{20,24},{24,20},{28,32},{32,28},{36,40... | collective-permute-start | bytes 1572872 | tf_op jit(solution)/shard_map/ppermute | solution.py:497
  12.4 0.1 collective-permute-start.3
  12.5 0.0 collective-permute-done.1.p2
  12.5 0.0 collective-permute-done.p1
  12.5 0.0 collective-permute-done.2.p3
  12.5 0.0 copy-start.4
  12.5 0.9 %copy-done.4 = f32[2,64,256]{2,1,0:T(8,128)S(1)} copy-done((f32[2,64,256]{2,1,0:T(8,128)S(1)}, f32[2,64,256]{2,1,0:T(8,128)}, u32[]{:S(2)}) %copy-start.4) | copy-done | bytes 131096
  13.4 0.4 collect_density.1.dens
  13.8 3.6 %collective-permute-start.6 = (f32[2,256,256]{2,1,0:T(8,128)S(1)}, f32[2,256,256]{2,1,0:T(8,128)S(1)}, u32[]{:S(2)}, u32[]{:S(2)}) collective-permute-start(f32[2,256,256]{2,1,0:T(8,128)S(1)} %collect_density.1.dens), channel_id=1, source_target_pairs={{4,8},{8,4},{12,16},{16,12},{20,24},{24,20},{28,32},{32,28},{36,40... | collective-permute-start | bytes 1572872 | tf_op jit(solution)/shard_map/ppermute | solution.py:497
  17.4 0.1 collective-permute-start.4
  18.1 2.2 %collective-permute-done.5.rhs_b = f32[1,2,256,256]{3,2,1,0:T(8,128)S(1)} collective-permute-done((f32[1,2,256,256]{3,2,1,0:T(8,128)}, f32[1,2,256,256]{3,2,1,0:T(8,128)S(1)}, u32[]{:S(2)}, u32[]{:S(2)}) %collective-permute-start.5) | collective-permute-done | bytes 524320 | tf_op jit(solution)/shard_map/ppermute | solution.py:497
  20.3 0.0 collective-permute-done.3.rhs_a
  20.3 7.3 %collective-permute-done.6.dens_b = f32[2,256,256]{2,1,0:T(8,128)S(1)} collective-permute-done((f32[2,256,256]{2,1,0:T(8,128)S(1)}, f32[2,256,256]{2,1,0:T(8,128)S(1)}, u32[]{:S(2)}, u32[]{:S(2)}) %collective-permute-start.6) | collective-permute-done | bytes 524320 | tf_op jit(solution)/shard_map/ppermute | solution.py:497
  27.6 0.0 collective-permute-done.4.dens_a
  27.6 0.0 copy-done
  27.6 5.3 %smooth_and_restrict.1 = (f32[4,256,256]{2,1,0:T(8,128)S(1)}, f32[4,256,256]{2,1,0:T(8,128)S(1)}, f32[768,128]{1,0:T(8,128)S(1)}, f32[1,256,256]{2,1,0:T(8,128)S(1)}, f32[64,128]{1,0:T(8,128)}) custom-call(f32[1]{0:T(128)S(6)} %copy.7.kappa_in, f32[1,2,256,256]{3,2,1,0:T(8,128)S(1)} %copy-done, f32[2,256,256]{2,1,0:T(8,128)S(1)} %collect_density.1.dens, ...), custom_call_target="tpu_custom_call" | custom-call | tf_op jit(solution)/shard_map/smooth_and_restrict/pallas_call | solution.py:520
  32.9 1.0 %copy-done.1 = f32[4,256,256]{2,1,0:T(8,128)} copy-done((f32[4,256,256]{2,1,0:T(8,128)}, f32[4,256,256]{2,1,0:T(8,128)S(1)}, u32[]{:S(2)}) %copy-start.1) | copy-done | bytes 1048600
  33.9 0.0 collective-permute-start.8
  33.9 1.7 %collective-permute-done.8.other.sib = f32[768,128]{1,0:T(8,128)S(1)} collective-permute-done((f32[768,128]{1,0:T(8,128)S(1)}, f32[768,128]{1,0:T(8,128)S(1)}, u32[]{:S(2)}, u32[]{:S(2)}) %collective-permute-start.8) | collective-permute-done | bytes 393248 | tf_op jit(solution)/shard_map/ppermute | solution.py:494
  35.7 1.0 %join_chip.1 = f32[512,128]{1,0:T(8,128)} custom-call(f32[768,128]{1,0:T(8,128)S(1)} %get-tuple-element.16.mine.send_a, f32[768,128]{1,0:T(8,128)S(1)} %collective-permute-done.8.other.sib), custom_call_target="tpu_custom_call" | custom-call | tf_op jit(solution)/shard_map/join_chip/pallas_call | solution.py:547
  36.7 2.0 %collective-permute-start.10 = (f32[512,128]{1,0:T(8,128)}, f32[512,128]{1,0:T(8,128)S(1)}, u32[]{:S(2)}, u32[]{:S(2)}) collective-permute-start(f32[512,128]{1,0:T(8,128)} %join_chip.1), channel_id=1, source_target_pairs={{16,4},{24,12},{32,20},{40,28},{48,36},{56,44},{64,52},{72,60},{80... | collective-permute-start | bytes 786440 | tf_op jit(solution)/shard_map/ppermute | solution.py:500
  38.8 4.3 %collective-permute-start.9 = (f32[512,128]{1,0:T(8,128)}, f32[512,128]{1,0:T(8,128)S(1)}, u32[]{:S(2)}, u32[]{:S(2)}) collective-permute-start(f32[512,128]{1,0:T(8,128)} %join_chip.1), channel_id=1, source_target_pairs={{4,8},{8,4},{12,16},{16,12},{20,24},{24,20},{28,32},{32,28},{36,40... | collective-permute-start | bytes 786440 | tf_op jit(solution)/shard_map/ppermute | solution.py:497
  43.1 0.0 copy-start.6
  43.1 8.5 %all-to-all-start = ((f32[64,1,128]{2,1,0:T(1,128)}), f32[64,1,128]{2,1,0:T(1,128)S(1)}, u32[]{:S(2)}, u32[]{:S(2)}) async-start(f32[64,1,128]{2,1,0:T(1,128)} %bitcast), calls=%async_computation | async-start | bytes 65536 | tf_op jit(solution)/shard_map/all_to_all | solution.py:544
  51.6 4.6 %collective-permute-start.7 = (f32[1,256,256]{2,1,0:T(8,128)}, f32[1,256,256]{2,1,0:T(8,128)}, u32[]{:S(2)}, u32[]{:S(2)}) collective-permute-start(f32[1,256,256]{2,1,0:T(8,128)} %copy-done.5), channel_id=1, source_target_pairs={{4,8},{8,4},{12,16},{16,12},{20,24},{24,20},{28,32},{32,28},{36,40... | collective-permute-start | bytes 786440 | tf_op jit(solution)/shard_map/ppermute | solution.py:497
  56.1 0.3 all-to-all-done.gathered
  56.4 0.0 collective-permute-done.10.far
  56.4 0.0 collective-permute-done.9.near
  56.4 0.9 %collective-permute-start.11 = (f32[512,128]{1,0:T(8,128)S(1)}, f32[512,128]{1,0:T(8,128)}, u32[]{:S(2)}, u32[]{:S(2)}) collective-permute-start(f32[512,128]{1,0:T(8,128)S(1)} %collective-permute-done.9.near), channel_id=1, source_target_pairs={{0,4},{4,0},{8,12},{12,8},{16,20},{20,16},{24,28},{28,24},{32,36},... | collective-permute-start | bytes 786440 | tf_op jit(solution)/shard_map/ppermute | solution.py:494
  57.3 0.1 collective-permute-start.12
  57.4 0.1 copy.6.groups
  57.5 5.4 %collective-permute-done.7.near_f = f32[1,256,256]{2,1,0:T(8,128)} collective-permute-done((f32[1,256,256]{2,1,0:T(8,128)}, f32[1,256,256]{2,1,0:T(8,128)}, u32[]{:S(2)}, u32[]{:S(2)}) %collective-permute-start.7) | collective-permute-done | bytes 262176 | tf_op jit(solution)/shard_map/ppermute | solution.py:497
  62.9 0.0 collective-permute-done.11.sib_near
  62.9 0.0 collective-permute-done.12.sib_far
  62.9 1.2 %copy-done.2 = f32[4,256,256]{2,1,0:T(8,128)S(1)} copy-done((f32[4,256,256]{2,1,0:T(8,128)S(1)}, f32[4,256,256]{2,1,0:T(8,128)}, u32[]{:S(2)}) %copy-start.2) | copy-done | bytes 1048600
  64.1 8.1 %correct_and_smooth.1 = (f32[1,2,256,256]{3,2,1,0:T(8,128)}, f32[1,256,256]{2,1,0:T(8,128)S(1)}, f32[1,256,256]{2,1,0:T(8,128)S(1)}) custom-call(f32[1]{0:T(128)S(6)} %copy.7.kappa_in, f32[1,2,256,256]{3,2,1,0:T(8,128)S(1)} %copy-done, f32[2,256,256]{2,1,0:T(8,128)S(1)} %collect_density.1.dens, f32[4,256,256]{2,1,0:T(8,128)S(1)} %copy-done.2, ...), custom_call_target="tpu_custom_call" | custom-call | tf_op jit(solution)/shard_map/correct_and_smooth/pallas_call | solution.py:562
  72.2 0.1 collective-permute-start.13
  72.3 4.6 %collective-permute-start.14 = (f32[1,256,256]{2,1,0:T(8,128)S(1)}, f32[1,256,256]{2,1,0:T(8,128)S(1)}, u32[]{:S(2)}, u32[]{:S(2)}) collective-permute-start(f32[1,256,256]{2,1,0:T(8,128)S(1)} %get-tuple-element.23), channel_id=1, source_target_pairs={{4,8},{8,4},{12,16},{16,12},{20,24},{24,20},{28,32},{32,28},{36,40... | collective-permute-start | bytes 786440 | tf_op jit(solution)/shard_map/ppermute | solution.py:497
  76.9 0.0 copy-start.3
  76.9 1.0 %copy-done.3 = f32[1,2,256,256]{3,2,1,0:T(8,128)S(1)} copy-done((f32[1,2,256,256]{3,2,1,0:T(8,128)S(1)}, f32[1,2,256,256]{3,2,1,0:T(8,128)}, u32[]{:S(2)}) %copy-start.3) | copy-done | bytes 524312
  77.9 1.6 %residual_inside.1.inside = f32[2,256,256]{2,1,0:T(8,128)S(1)} custom-call(f32[1]{0:T(128)S(6)} %copy.7.kappa_in, f32[1,2,256,256]{3,2,1,0:T(8,128)S(1)} %copy-done, f32[2,256,256]{2,1,0:T(8,128)S(1)} %collect_density.1.dens, f32[1,2,256,256]{3,2,1,0:T(8,128)S(1)} %copy-done.3), custom_call_target="tpu_custom_call" | custom-call | tf_op jit(solution)/shard_map/residual_inside/pallas_call | solution.py:589
  79.5 0.0 collective-permute-done.13.halo_a
  79.5 3.8 %collective-permute-done.14.halo_b = f32[1,256,256]{2,1,0:T(8,128)S(1)} collective-permute-done((f32[1,256,256]{2,1,0:T(8,128)S(1)}, f32[1,256,256]{2,1,0:T(8,128)S(1)}, u32[]{:S(2)}, u32[]{:S(2)}) %collective-permute-start.14) | collective-permute-done | bytes 262176 | tf_op jit(solution)/shard_map/ppermute | solution.py:497
  83.3 2.3 %residual.1 = f32[1,2,256,256]{3,2,1,0:T(8,128)} custom-call(f32[1]{0:T(128)S(6)} %copy.7.kappa_in, f32[2,256,256]{2,1,0:T(8,128)S(1)} %residual_inside.1.inside, f32[1,256,256]{2,1,0:T(8,128)S(1)} %collective-permute-done.13.halo_a, f32[1,256,256]{2,1,0:T(8,128)S(1)} %collective-permute-done.14.halo_b), custom_call_target="tpu_custom_call" | custom-call | tf_op jit(solution)/shard_map/residual/pallas_call | solution.py:598
  (5 shorter events, 0.0 us)
Async XLA Ops:
  0.6 27.0 %copy-start = (f32[1,2,256,256]{3,2,1,0:T(8,128)S(1)}, f32[1,2,256,256]{3,2,1,0:T(8,128)}, u32[]{:S(2)}) copy-start(f32[1,2,256,256]{3,2,1,0:T(8,128)} %rhs.5) | copy-start | bytes 1572868
  0.6 11.8 %collective-permute-start.1 = (f32[2,64,256]{2,1,0:T(8,128)}, f32[2,64,256]{2,1,0:T(8,128)S(1)}, u32[]{:S(2)}, u32[]{:S(2)}) collective-permute-start(f32[2,64,256]{2,1,0:T(8,128)} %shard.1), channel_id=1, source_target_pairs={{0,2},{1,3},{2,0},{3,1},{4,6},{5,7},{6,4},{7,5},{8,10},{9,11},{10,... | collective-permute-start | bytes 393224 | tf_op jit(solution)/shard_map/ppermute | solution.py:503
  3.6 8.9 %collective-permute-start = (f32[2,64,256]{2,1,0:T(8,128)}, f32[2,64,256]{2,1,0:T(8,128)S(1)}, u32[]{:S(2)}, u32[]{:S(2)}) collective-permute-start(f32[2,64,256]{2,1,0:T(8,128)} %shard.1), channel_id=1, source_target_pairs={{0,1},{1,2},{2,3},{3,0},{4,5},{5,6},{6,7},{7,4},{8,9},{9,10},{10,1... | collective-permute-start | bytes 393224 | tf_op jit(solution)/shard_map/ppermute | solution.py:503
  4.0 8.5 %collective-permute-start.2 = (f32[2,64,256]{2,1,0:T(8,128)}, f32[2,64,256]{2,1,0:T(8,128)S(1)}, u32[]{:S(2)}, u32[]{:S(2)}) collective-permute-start(f32[2,64,256]{2,1,0:T(8,128)} %shard.1), channel_id=1, source_target_pairs={{0,3},{1,0},{2,1},{3,2},{4,7},{5,4},{6,5},{7,6},{8,11},{9,8},{10,9... | collective-permute-start | bytes 393224 | tf_op jit(solution)/shard_map/ppermute | solution.py:503
  6.3 14.0 %collective-permute-start.5 = (f32[1,2,256,256]{3,2,1,0:T(8,128)}, f32[1,2,256,256]{3,2,1,0:T(8,128)S(1)}, u32[]{:S(2)}, u32[]{:S(2)}) collective-permute-start(f32[1,2,256,256]{3,2,1,0:T(8,128)} %rhs.5), channel_id=1, source_target_pairs={{4,8},{8,4},{12,16},{16,12},{20,24},{24,20},{28,32},{32,28},{36,40... | collective-permute-start | bytes 1572872 | tf_op jit(solution)/shard_map/ppermute | solution.py:497
  12.4 8.0 %collective-permute-start.3 = (f32[1,2,256,256]{3,2,1,0:T(8,128)}, f32[1,2,256,256]{3,2,1,0:T(8,128)S(1)}, u32[]{:S(2)}, u32[]{:S(2)}) collective-permute-start(f32[1,2,256,256]{3,2,1,0:T(8,128)} %rhs.5), channel_id=1, source_target_pairs={{0,4},{4,0},{8,12},{12,8},{16,20},{20,16},{24,28},{28,24},{32,36},... | collective-permute-start | bytes 1572872 | tf_op jit(solution)/shard_map/ppermute | solution.py:494
  12.5 0.9 %copy-start.4 = (f32[2,64,256]{2,1,0:T(8,128)S(1)}, f32[2,64,256]{2,1,0:T(8,128)}, u32[]{:S(2)}) copy-start(f32[2,64,256]{2,1,0:T(8,128)} %shard.1) | copy-start | bytes 393220
  13.8 13.8 %collective-permute-start.6 = (f32[2,256,256]{2,1,0:T(8,128)S(1)}, f32[2,256,256]{2,1,0:T(8,128)S(1)}, u32[]{:S(2)}, u32[]{:S(2)}) collective-permute-start(f32[2,256,256]{2,1,0:T(8,128)S(1)} %collect_density.1.dens), channel_id=1, source_target_pairs={{4,8},{8,4},{12,16},{16,12},{20,24},{24,20},{28,32},{32,28},{36,40... | collective-permute-start | bytes 1572872 | tf_op jit(solution)/shard_map/ppermute | solution.py:497
  17.4 10.2 %collective-permute-start.4 = (f32[2,256,256]{2,1,0:T(8,128)S(1)}, f32[2,256,256]{2,1,0:T(8,128)S(1)}, u32[]{:S(2)}, u32[]{:S(2)}) collective-permute-start(f32[2,256,256]{2,1,0:T(8,128)S(1)} %collect_density.1.dens), channel_id=1, source_target_pairs={{0,4},{4,0},{8,12},{12,8},{16,20},{20,16},{24,28},{28,24},{32,36},... | collective-permute-start | bytes 1572872 | tf_op jit(solution)/shard_map/ppermute | solution.py:494
  32.9 1.0 %copy-start.1 = (f32[4,256,256]{2,1,0:T(8,128)}, f32[4,256,256]{2,1,0:T(8,128)S(1)}, u32[]{:S(2)}) copy-start(f32[4,256,256]{2,1,0:T(8,128)S(1)} %get-tuple-element.13.halo) | copy-start | bytes 3145732
  33.9 2.8 %copy-start.5 = (f32[1,256,256]{2,1,0:T(8,128)}, f32[1,256,256]{2,1,0:T(8,128)S(1)}, u32[]{:S(2)}) copy-start(f32[1,256,256]{2,1,0:T(8,128)S(1)} %get-tuple-element.15) | copy-start | bytes 786436
  33.9 1.7 %collective-permute-start.8 = (f32[768,128]{1,0:T(8,128)S(1)}, f32[768,128]{1,0:T(8,128)S(1)}, u32[]{:S(2)}, u32[]{:S(2)}) collective-permute-start(f32[768,128]{1,0:T(8,128)S(1)} %get-tuple-element.16.mine.send_a), channel_id=1, source_target_pairs={{0,4},{4,0},{8,12},{12,8},{16,20},{20,16},{24,28},{28,24},{32,36},... | collective-permute-start | bytes 1179656 | tf_op jit(solution)/shard_map/ppermute | solution.py:494
  36.7 19.7 %collective-permute-start.10 = (f32[512,128]{1,0:T(8,128)}, f32[512,128]{1,0:T(8,128)S(1)}, u32[]{:S(2)}, u32[]{:S(2)}) collective-permute-start(f32[512,128]{1,0:T(8,128)} %join_chip.1), channel_id=1, source_target_pairs={{16,4},{24,12},{32,20},{40,28},{48,36},{56,44},{64,52},{72,60},{80... | collective-permute-start | bytes 786440 | tf_op jit(solution)/shard_map/ppermute | solution.py:500
  38.8 17.7 %collective-permute-start.9 = (f32[512,128]{1,0:T(8,128)}, f32[512,128]{1,0:T(8,128)S(1)}, u32[]{:S(2)}, u32[]{:S(2)}) collective-permute-start(f32[512,128]{1,0:T(8,128)} %join_chip.1), channel_id=1, source_target_pairs={{4,8},{8,4},{12,16},{16,12},{20,24},{24,20},{28,32},{32,28},{36,40... | collective-permute-start | bytes 786440 | tf_op jit(solution)/shard_map/ppermute | solution.py:497
  43.1 14.3 %copy-start.6 = (s32[64,16]{0,1:T(8,128)S(1)}, s32[64,16]{0,1:T(8,128)}, u32[]{:S(2)}) copy-start(s32[64,16]{0,1:T(8,128)} %param.7) | copy-start | bytes 12292
  43.1 13.4 %all-to-all-start = ((f32[64,1,128]{2,1,0:T(1,128)}), f32[64,1,128]{2,1,0:T(1,128)S(1)}, u32[]{:S(2)}, u32[]{:S(2)}) async-start(f32[64,1,128]{2,1,0:T(1,128)} %bitcast), calls=%async_computation | async-start | bytes 65536 | tf_op jit(solution)/shard_map/all_to_all | solution.py:544
  51.6 11.3 %collective-permute-start.7 = (f32[1,256,256]{2,1,0:T(8,128)}, f32[1,256,256]{2,1,0:T(8,128)}, u32[]{:S(2)}, u32[]{:S(2)}) collective-permute-start(f32[1,256,256]{2,1,0:T(8,128)} %copy-done.5), channel_id=1, source_target_pairs={{4,8},{8,4},{12,16},{16,12},{20,24},{24,20},{28,32},{32,28},{36,40... | collective-permute-start | bytes 786440 | tf_op jit(solution)/shard_map/ppermute | solution.py:497
  56.4 6.4 %collective-permute-start.11 = (f32[512,128]{1,0:T(8,128)S(1)}, f32[512,128]{1,0:T(8,128)}, u32[]{:S(2)}, u32[]{:S(2)}) collective-permute-start(f32[512,128]{1,0:T(8,128)S(1)} %collective-permute-done.9.near), channel_id=1, source_target_pairs={{0,4},{4,0},{8,12},{12,8},{16,20},{20,16},{24,28},{28,24},{32,36},... | collective-permute-start | bytes 786440 | tf_op jit(solution)/shard_map/ppermute | solution.py:494
  57.3 5.6 %collective-permute-start.12 = (f32[512,128]{1,0:T(8,128)S(1)}, f32[512,128]{1,0:T(8,128)}, u32[]{:S(2)}, u32[]{:S(2)}) collective-permute-start(f32[512,128]{1,0:T(8,128)S(1)} %collective-permute-done.10.far), channel_id=1, source_target_pairs={{0,4},{4,0},{8,12},{12,8},{16,20},{20,16},{24,28},{28,24},{32,36},... | collective-permute-start | bytes 786440 | tf_op jit(solution)/shard_map/ppermute | solution.py:494
  62.9 1.2 %copy-start.2 = (f32[4,256,256]{2,1,0:T(8,128)S(1)}, f32[4,256,256]{2,1,0:T(8,128)}, u32[]{:S(2)}) copy-start(f32[4,256,256]{2,1,0:T(8,128)} %copy-done.1) | copy-start | bytes 3145732
  72.2 7.3 %collective-permute-start.13 = (f32[1,256,256]{2,1,0:T(8,128)S(1)}, f32[1,256,256]{2,1,0:T(8,128)S(1)}, u32[]{:S(2)}, u32[]{:S(2)}) collective-permute-start(f32[1,256,256]{2,1,0:T(8,128)S(1)} %get-tuple-element.22), channel_id=1, source_target_pairs={{0,4},{4,0},{8,12},{12,8},{16,20},{20,16},{24,28},{28,24},{32,36},... | collective-permute-start | bytes 786440 | tf_op jit(solution)/shard_map/ppermute | solution.py:494
  72.3 11.0 %collective-permute-start.14 = (f32[1,256,256]{2,1,0:T(8,128)S(1)}, f32[1,256,256]{2,1,0:T(8,128)S(1)}, u32[]{:S(2)}, u32[]{:S(2)}) collective-permute-start(f32[1,256,256]{2,1,0:T(8,128)S(1)} %get-tuple-element.23), channel_id=1, source_target_pairs={{4,8},{8,4},{12,16},{16,12},{20,24},{24,20},{28,32},{32,28},{36,40... | collective-permute-start | bytes 786440 | tf_op jit(solution)/shard_map/ppermute | solution.py:497
  76.9 1.0 %copy-start.3 = (f32[1,2,256,256]{3,2,1,0:T(8,128)S(1)}, f32[1,2,256,256]{3,2,1,0:T(8,128)}, u32[]{:S(2)}) copy-start(f32[1,2,256,256]{3,2,1,0:T(8,128)} %get-tuple-element.11.sol_in) | copy-start | bytes 1572868

commit v3 on v2

--- a/solution.py
+++ b/solution.py
@@ -16,6 +16,7 @@
 bf16 = jnp.bfloat16
 VM = pl.BlockSpec(memory_space=pltpu.VMEM)
 ANY = pl.BlockSpec(memory_space=pl.ANY)
+HBM = pl.BlockSpec(memory_space=pltpu.HBM)
 PARAMS = pltpu.CompilerParams(vmem_limit_bytes=16 * 1024 * 1024)
 
 
@@ -39,10 +40,10 @@
 
 def filter_z(y):
     width = y.shape[1]
-    lane = iota(y.shape, 1)
-    before = jnp.where(lane == 0, 0.0, pltpu.roll(y, 1, 1))
-    after = jnp.where(lane == width - 1, 0.0, pltpu.roll(y, width - 1, 1))
-    return y + 0.5 * (before + after)
+    lane = iota((1, width), 1)
+    before = jnp.where(lane == 0, 0.0, 0.5)
+    after = jnp.where(lane == width - 1, 0.0, 0.5)
+    return y + before * pltpu.roll(y, 1, 1) + after * pltpu.roll(y, width - 1, 1)
 
 
 def filter_yz(m):
@@ -64,11 +65,8 @@
 
 
 def chunks(rows, body):
-    def step(c, carry):
-        body(pl.multiple_of(c * CHUNK, CHUNK))
-        return carry
-
-    lax.fori_loop(0, rows // CHUNK, step, 0)
+    for row in range(0, rows, CHUNK):
+        body(row)
 
 
 def coarsen_z(rows, width):
@@ -163,6 +161,14 @@
 
         chunks(height, begin)
 
+    stores = [
+        pltpu.make_async_copy(rhs_w.at[1], halo_out.at[0], sems.at[1]),
+        pltpu.make_async_copy(rhs_w.at[4], halo_out.at[1], sems.at[2]),
+        pltpu.make_async_copy(dens_b.at[1 - core], halo_out.at[2 + core], sems.at[3]),
+        pltpu.make_async_copy(dens_a.at[core], halo_out.at[3 - core], sems.at[4]),
+    ]
+    start_all(stores)
+
     for j in range(1, 5):
 
         def smooth(row, j=j):
@@ -174,10 +180,6 @@
             s2_out[j - 1, part, :] = new
 
         chunks(height, smooth)
-    halo_out[0] = rhs_w[1]
-    halo_out[1] = rhs_w[4]
-    for ref, layer, edge in ((dens_b, 1 - core, core), (dens_a, core, 1 - core)):
-        halo_out[2 + edge] = ref[layer]
     mine = 1 + core
     send_a[2 * half : 4 * half, :] = s2_out[mine, :, :half]
     send_a[4 * half : 6 * half, :] = s2_out[mine, :, half:]
@@ -246,7 +248,8 @@
     out = jnp.where(fits & ((lane >> 4) == (row >> 2)), dot_exact(filtered, filter_w), 0.0)
     out = jnp.where(row >= 12, 0.0, out)
     out = out + jnp.where(fits & ((lane >> 4) == (row >> 2) + 3), dot_exact(plain, plain_w), 0.0)
-    payload[...] = jnp.broadcast_to(jnp.sum(out, axis=0, keepdims=True), payload.shape)
+    payload[...] = jnp.broadcast_to(jnp.sum(out, axis=0, keepdims=True)[None], payload.shape)
+    wait_all(stores)
 
 
 def lanes_sum(x):
@@ -329,13 +332,15 @@
 
 
 def second_kernel(
-    kappa_in, rhs, dens, halo, s2, near_f, send_a, sib, near, far, sib_near, sib_far, gathered, groups,
-    sol_out, to_a, to_b,
-    fixes, cres, cden, c1, c2, c3, grown, s3, s4, wd, kappa, sems,
+    kappa_in, halo_in, rhs, dens, s2, near_f, send_a, sib, near, far, sib_near, sib_far, gathered, groups,
+    to_a, to_b,
+    fixes, cres, cden, c1, c2, c3, grown, s3, s4, wd, halo, last, kappa, sems,
 ):
     core, brick, bricks = position()
     load = pltpu.make_async_copy(kappa_in, kappa, sems.at[0])
     load.start()
+    load_halo = pltpu.make_async_copy(halo_in, halo, sems.at[1])
+    load_halo.start()
     half = cres.shape[1]
     height, width = rhs.shape[2:]
     block = half // TILES
@@ -393,6 +398,7 @@
         put_halves(grown, i, pl.ds(0, half, stride=2), fine)
         put_halves(grown, i, pl.ds(1, half, stride=2), fine)
 
+    load_halo.wait()
     for k in range(2):
         side = slice(k * half, (k + 1) * half)
         for i in range(4):
@@ -425,23 +431,28 @@
             v = s4[j + 1, pl.ds(row + 8, CHUNK), :]
             f = stencil(s4, j + 1, row, CHUNK)
             new = (1.0 - WEIGHT) * v + wd[j + 1, part, :] * (rhs[0, j, part, :] + 2.0 * scale * (f - v))
-            sol_out[0, j, part, :] = new
+            last[j, part, :] = new
 
         chunks(height, smooth_last)
-    to_a[...] = sol_out[0, pl.ds(1 - core, 1), :, :]
-    to_b[...] = sol_out[0, pl.ds(core, 1), :, :]
-
-
-def inside_kernel(kappa_in, rhs, dens, sol_in, out, s, kappa, sems):
-    height, width = dens.shape[1:]
+    to_a[0] = last[1 - core]
+    to_b[0] = last[core]
+
+
+def inside_kernel(kappa_in, rhs, dens, to_a, to_b, sol_out, out, s, kappa, sems):
+    core = position()[0]
+    load = pltpu.make_async_copy(kappa_in, kappa, sems.at[0])
+    stores = [
+        pltpu.make_async_copy(to_b.at[0], sol_out.at[0, core], sems.at[1]),
+        pltpu.make_async_copy(to_a.at[0], sol_out.at[0, 1 - core], sems.at[2]),
+    ]
+    load.start()
+    start_all(stores)
+    height = dens.shape[1]
     inner = pl.ds(8, height)
-    loads = [
-        pltpu.make_async_copy(sol_in.at[0], s.at[:, inner, :], sems.at[0]),
-        pltpu.make_async_copy(kappa_in, kappa, sems.at[1]),
-    ]
-    start_all(loads)
     clear_edges(s)
-    wait_all(loads)
+    s[core, inner, :] = to_b[0]
+    s[1 - core, inner, :] = to_a[0]
+    load.wait()
     scale = kappa[0]
     for j in range(2):
 
@@ -453,28 +464,31 @@
             out[j, part, :] = rhs[0, j, part, :] - center * s[j, pl.ds(row + 8, CHUNK), :] + 2.0 * scale * f
 
         chunks(height, finish)
-
-
-def residual_kernel(kappa_in, inside, halo_a, halo_b, out, s, kappa, sems):
+    wait_all(stores)
+
+
+def residual_kernel(kappa_in, inside, halo_a, halo_b, out, s, done, kappa, sems):
     core = position()[0]
+    load = pltpu.make_async_copy(kappa_in, kappa, sems.at[0])
+    load.start()
     height = inside.shape[1]
     inner = pl.ds(8, height)
-    loads = [
-        pltpu.make_async_copy(halo_b.at[0], s.at[core, inner, :], sems.at[0]),
-        pltpu.make_async_copy(halo_a.at[0], s.at[1 - core, inner, :], sems.at[1]),
-        pltpu.make_async_copy(kappa_in, kappa, sems.at[2]),
-    ]
-    start_all(loads)
     clear_edges(s)
-    wait_all(loads)
+    s[core, inner, :] = halo_b[0]
+    s[1 - core, inner, :] = halo_a[0]
+    load.wait()
     scale = kappa[0]
+    stores = []
     for j in range(2):
 
         def finish(row, j=j):
             part = pl.ds(row, CHUNK)
-            out[0, j, part, :] = inside[j, part, :] + scale * filter_yz(s[j, pl.ds(row, CHUNK + 16), :])
+            done[j, part, :] = inside[j, part, :] + scale * filter_yz(s[j, pl.ds(row, CHUNK + 16), :])
 
         chunks(height, finish)
+        stores.append(pltpu.make_async_copy(done.at[j], out.at[0, j], sems.at[1 + j]))
+        stores[-1].start()
+    wait_all(stores)
 
 
 def shape(*dims):
@@ -508,12 +522,12 @@
     dens = pl.pallas_call(
         gather_kernel,
         out_shape=shape(2, height, width),
-        in_specs=[ANY] * 4,
+        in_specs=[HBM] + [ANY] * 3,
         out_specs=VM,
         scratch_shapes=[pltpu.SemaphoreType.DMA((4,))],
         compiler_params=PARAMS,
         name="collect_density",
-    )(density, *pieces)
+    )(pltpu.with_memory_space_constraint(density, pltpu.HBM), *pieces)
 
     dens_b = swap_b(dens)
     dens_a = swap_a(dens)
@@ -521,13 +535,13 @@
         first_kernel,
         out_shape=(
             shape(4, height, width),
-            shape(4, height, width),
+            pltpu.HBM((4, height, width), f32),
             shape(6 * half, half),
             shape(1, height, width),
-            shape(bricks, 128),
+            shape(bricks, 8, 128),
         ),
         in_specs=[ANY] + [VM] * 6,
-        out_specs=[VM] * 5,
+        out_specs=[VM, HBM, VM, VM, VM],
         scratch_shapes=[
             pltpu.VMEM((6, height + 16, width), f32),
             pltpu.VMEM((4, height + 16, width), f32),
@@ -535,13 +549,13 @@
             pltpu.VMEM((6, height, width), f32),
             pltpu.VMEM((4, 2, height, half), f32),
             pltpu.SMEM((1,), f32),
-            pltpu.SemaphoreType.DMA((1,)),
+            pltpu.SemaphoreType.DMA((5,)),
         ],
         compiler_params=PARAMS,
         name="smooth_and_restrict",
     )(kappa, rhs, dens, rhs_a, dens_a, rhs_b, dens_b)
 
-    gathered = lax.all_to_all(payload.reshape(bricks, 1, 128), "brick", 0, 0, tiled=True)
+    gathered = lax.all_to_all(payload, "brick", 0, 0, tiled=True)
     sib = swap_a(send_a)
     near_f = swap_b(send_b)
     both = pl.pallas_call(
@@ -559,11 +573,11 @@
     sib_near = swap_a(near)
     sib_far = swap_a(far)
 
-    solution, to_a, to_b = pl.pallas_call(
+    to_a, to_b = pl.pallas_call(
         second_kernel,
-        out_shape=(shape(1, 2, height, width), shape(1, height, width), shape(1, height, width)),
-        in_specs=[ANY] + [VM] * 13,
-        out_specs=[VM] * 3,
+        out_shape=(shape(1, height, width), shape(1, height, width)),
+        in_specs=[ANY, HBM] + [VM] * 12,
+        out_specs=[VM] * 2,
         scratch_shapes=[
             pltpu.VMEM((bricks + 32, 128), f32),
             pltpu.VMEM((9, half, half), f32),
@@ -575,32 +589,43 @@
             pltpu.VMEM((6, height + 16, width), f32),
             pltpu.VMEM((4, height + 16, width), f32),
             pltpu.VMEM((4, height, width), f32),
+            pltpu.VMEM((4, height, width), f32),
+            pltpu.VMEM((2, height, width), f32),
             pltpu.SMEM((1,), f32),
-            pltpu.SemaphoreType.DMA((1,)),
+            pltpu.SemaphoreType.DMA((2,)),
         ],
         compiler_params=PARAMS,
         name="correct_and_smooth",
     )(
-        kappa, rhs, dens, halo, s2, near_f, send_a, sib, near, far, sib_near, sib_far, gathered, block_group
+        kappa, pltpu.with_memory_space_constraint(halo, pltpu.HBM), rhs, dens, s2, near_f, send_a, sib, near, far, sib_near, sib_far, gathered, block_group
     )
 
     halo_b = swap_b(to_b)
     halo_a = swap_a(to_a)
-    inside = pl.pallas_call(
+    solution, inside = pl.pallas_call(
         inside_kernel,
-        out_shape=shape(2, height, width),
-        in_specs=[ANY] + [VM] * 2 + [ANY],
-        out_specs=VM,
-        scratch_shapes=[pltpu.VMEM((2, height + 16, width), f32), pltpu.SMEM((1,), f32), pltpu.SemaphoreType.DMA((2,))],
+        out_shape=(shape(1, 2, height, width), shape(2, height, width)),
+        in_specs=[ANY] + [VM] * 4,
+        out_specs=[ANY, VM],
+        scratch_shapes=[
+            pltpu.VMEM((2, height + 16, width), f32),
+            pltpu.SMEM((1,), f32),
+            pltpu.SemaphoreType.DMA((3,)),
+        ],
         compiler_params=PARAMS,
         name="residual_inside",
-    )(kappa, rhs, dens, solution)
+    )(kappa, rhs, dens, to_a, to_b)
     residual = pl.pallas_call(
         residual_kernel,
         out_shape=shape(1, 2, height, width),
-        in_specs=[ANY, VM] + [ANY] * 2,
-        out_specs=VM,
-        scratch_shapes=[pltpu.VMEM((2, height + 16, width), f32), pltpu.SMEM((1,), f32), pltpu.SemaphoreType.DMA((3,))],
+        in_specs=[ANY] + [VM] * 3,
+        out_specs=ANY,
+        scratch_shapes=[
+            pltpu.VMEM((2, height + 16, width), f32),
+            pltpu.VMEM((2, height, width), f32),
+            pltpu.SMEM((1,), f32),
+            pltpu.SemaphoreType.DMA((3,)),
+        ],
         compiler_params=PARAMS,
         name="residual",
     )(kappa, inside, halo_a, halo_b)

time: 86.1 us -> 81.2 us (0.943)
  starting transfers between devices: 40.5 us -> 45.7 us
  Pallas kernels: 18.7 us -> 14.5 us
  local copies, waits for them, and re-layouts: 4.25 us -> 0.09 us
  waiting for transfers between devices: 20.7 us -> 18.9 us
    unnamed x15 -> x5, local copies, waits for them, and re-layouts: 4.25 us -> 0.09 us
    pallas_call x3, Pallas kernels: 15 us -> 10.9 us  [the longest x1 5.41 us: local(): pl.pallas_call(second_kernel, out_shape=(shape(1, height, width), shape(1...]
    ppermute x1, starting transfers between devices: 2.03 us -> 5.47 us  [swap_far(): return lax.ppermute(x, 'brick', second_chip)]
    ppermute x6, waiting for transfers between devices: 1.73 us -> 0.02 us  [swap_a(): return lax.ppermute(x, 'brick', in_chip)]
    ppermute x6, starting transfers between devices: 1.24 us -> 2.58 us  [swap_a(): return lax.ppermute(x, 'brick', in_chip)]
    all_to_all x1, starting transfers between devices: 8.46 us -> 9.35 us  [local(): gathered = lax.all_to_all(payload, 'brick', 0, 0, tiled=True)]
  transfers between devices with their start and end apart: 16 -> 16, of which waited for: 6 -> 5; matrix products, arithmetic and copies ran while one was open for 0% -> 0% of each run, Pallas kernels for 2% -> 4%
where the time goes in v3:
time: 81.2 us; the launch traced here: 80.8 us
  starting transfers between devices  45.7 us (56%)
  waiting for transfers between devices  18.9 us (23%)
  Pallas kernels  14.5 us (18%)
  between operations  1.64 us (2%)
    ppermute x5, starting transfers between devices, swap_b(): return lax.ppermute(x, 'brick', next_chip)  23.2 us
    ppermute x5, waiting for transfers between devices, swap_b(): return lax.ppermute(x, 'brick', next_chip)  18.9 us
    all_to_all x1, starting transfers between devices, local(): gathered = lax.all_to_all(payload, 'brick', 0, 0, tiled=True)  9.35 us
    ppermute x1, starting transfers between devices, swap_far(): return lax.ppermute(x, 'brick', second_chip)  5.47 us
    pallas_call x1, Pallas kernels, local(): pl.pallas_call(second_kernel, out_shape=(shape(1, height, width), shape(1...  5.41 us
    ppermute x3, starting transfers between devices, around(): lax.ppermute(x, 'spec', [(i, (i + k) % species) for i in range(species)])  5.06 us
    pallas_call x1, Pallas kernels, local(): pl.pallas_call(first_kernel, out_shape=(shape(4, height, width), pltpu.HB...  4.51 us
    ppermute x6, starting transfers between devices, swap_a(): return lax.ppermute(x, 'brick', in_chip)  2.58 us
  transfers between devices with their start and end apart: 16, of which 5 were waited for; matrix products, arithmetic and copies ran while one was open for 0% of the time, Pallas kernels for 4%

profile of v3, /device:TPU:103, one launch (start us, length us, event | category | flops | bytes accessed | tf_op | source)
XLA Modules:
  0.0 80.8 jit_solution(17561663123150472036)
XLA Ops:
  0.6 0.0 copy-start
  0.6 1.4 %collective-permute-start = (f32[2,64,256]{2,1,0:T(8,128)}, f32[2,64,256]{2,1,0:T(8,128)S(1)}, u32[]{:S(2)}, u32[]{:S(2)}) collective-permute-start(f32[2,64,256]{2,1,0:T(8,128)} %shard.1), channel_id=1, source_target_pairs={{0,1},{1,2},{2,3},{3,0},{4,5},{5,6},{6,7},{7,4},{8,9},{9,10},{10,1... | collective-permute-start | bytes 393224 | tf_op jit(solution)/shard_map/ppermute | solution.py:517
  2.0 2.6 %collective-permute-start.1 = (f32[2,64,256]{2,1,0:T(8,128)}, f32[2,64,256]{2,1,0:T(8,128)S(1)}, u32[]{:S(2)}, u32[]{:S(2)}) collective-permute-start(f32[2,64,256]{2,1,0:T(8,128)} %shard.1), channel_id=1, source_target_pairs={{0,2},{1,3},{2,0},{3,1},{4,6},{5,7},{6,4},{7,5},{8,10},{9,11},{10,... | collective-permute-start | bytes 393224 | tf_op jit(solution)/shard_map/ppermute | solution.py:517
  4.6 1.1 %collective-permute-start.2 = (f32[2,64,256]{2,1,0:T(8,128)}, f32[2,64,256]{2,1,0:T(8,128)S(1)}, u32[]{:S(2)}, u32[]{:S(2)}) collective-permute-start(f32[2,64,256]{2,1,0:T(8,128)} %shard.1), channel_id=1, source_target_pairs={{0,3},{1,0},{2,1},{3,2},{4,7},{5,4},{6,5},{7,6},{8,11},{9,8},{10,9... | collective-permute-start | bytes 393224 | tf_op jit(solution)/shard_map/ppermute | solution.py:517
  5.7 1.5 %collective-permute-start.3 = (f32[1,2,256,256]{3,2,1,0:T(8,128)}, f32[1,2,256,256]{3,2,1,0:T(8,128)S(1)}, u32[]{:S(2)}, u32[]{:S(2)}) collective-permute-start(f32[1,2,256,256]{3,2,1,0:T(8,128)} %rhs.5), channel_id=1, source_target_pairs={{0,4},{4,0},{8,12},{12,8},{16,20},{20,16},{24,28},{28,24},{32,36},... | collective-permute-start | bytes 1572872 | tf_op jit(solution)/shard_map/ppermute | solution.py:508
  7.2 4.5 %collective-permute-start.5 = (f32[1,2,256,256]{3,2,1,0:T(8,128)}, f32[1,2,256,256]{3,2,1,0:T(8,128)S(1)}, u32[]{:S(2)}, u32[]{:S(2)}) collective-permute-start(f32[1,2,256,256]{3,2,1,0:T(8,128)} %rhs.5), channel_id=1, source_target_pairs={{4,8},{8,4},{12,16},{16,12},{20,24},{24,20},{28,32},{32,28},{36,40... | collective-permute-start | bytes 1572872 | tf_op jit(solution)/shard_map/ppermute | solution.py:511
  11.8 0.0 collective-permute-done.p1
  11.8 0.0 collective-permute-done.1.p2
  11.8 0.0 collective-permute-done.2.p3
  11.8 1.0 %collect_density.1.dens = f32[2,256,256]{2,1,0:T(8,128)S(1)} custom-call(f32[2,64,256]{2,1,0:T(8,128)} %shard.1, f32[2,64,256]{2,1,0:T(8,128)S(1)} %collective-permute-done.p1, f32[2,64,256]{2,1,0:T(8,128)S(1)} %collective-permute-done.1.p2, f32[2,64,256]{2,1,0:T(8,128)S(1)} %collective-permute-done.2.p3), custom_call_target="tpu_custom_call" | custom-call | tf_op jit(solution)/shard_map/collect_density/pallas_call | solution.py:522
  12.8 0.4 collective-permute-start.4
  13.1 4.6 %collective-permute-start.6 = (f32[2,256,256]{2,1,0:T(8,128)S(1)}, f32[2,256,256]{2,1,0:T(8,128)S(1)}, u32[]{:S(2)}, u32[]{:S(2)}) collective-permute-start(f32[2,256,256]{2,1,0:T(8,128)S(1)} %collect_density.1.dens), channel_id=1, source_target_pairs={{4,8},{8,4},{12,16},{16,12},{20,24},{24,20},{28,32},{32,28},{36,40... | collective-permute-start | bytes 1572872 | tf_op jit(solution)/shard_map/ppermute | solution.py:511
  18.4 0.0 collective-permute-done.3.rhs_a
  18.4 2.9 %collective-permute-done.5.rhs_b = f32[1,2,256,256]{3,2,1,0:T(8,128)S(1)} collective-permute-done((f32[1,2,256,256]{3,2,1,0:T(8,128)}, f32[1,2,256,256]{3,2,1,0:T(8,128)S(1)}, u32[]{:S(2)}, u32[]{:S(2)}) %collective-permute-start.5) | collective-permute-done | bytes 524320 | tf_op jit(solution)/shard_map/ppermute | solution.py:511
  21.2 0.0 collective-permute-done.4.dens_a
  21.2 5.7 %collective-permute-done.6.dens_b = f32[2,256,256]{2,1,0:T(8,128)S(1)} collective-permute-done((f32[2,256,256]{2,1,0:T(8,128)S(1)}, f32[2,256,256]{2,1,0:T(8,128)S(1)}, u32[]{:S(2)}, u32[]{:S(2)}) %collective-permute-start.6) | collective-permute-done | bytes 524320 | tf_op jit(solution)/shard_map/ppermute | solution.py:511
  26.9 0.0 copy-done
  27.0 4.5 %smooth_and_restrict.1 = (f32[4,256,256]{2,1,0:T(8,128)S(1)}, f32[4,256,256]{2,1,0:T(8,128)}, f32[768,128]{1,0:T(8,128)S(1)}, f32[1,256,256]{2,1,0:T(8,128)}, f32[64,8,128]{2,1,0:T(8,128)}) custom-call(f32[1]{0:T(128)S(6)} %copy.7.kappa_in, f32[1,2,256,256]{3,2,1,0:T(8,128)S(1)} %copy-done, f32[2,256,256]{2,1,0:T(8,128)S(1)} %collect_density.1.dens, ...), custom_call_target="tpu_custom_call" | custom-call | tf_op jit(solution)/shard_map/smooth_and_restrict/pallas_call | solution.py:534
  31.5 0.1 collective-permute-start.8
  31.6 9.3 %all-to-all-start = ((f32[64,8,128]{2,1,0:T(8,128)}), f32[64,8,128]{2,1,0:T(8,128)S(1)}, u32[]{:S(2)}, u32[]{:S(2)}) async-start(f32[64,8,128]{2,1,0:T(8,128)} %get-tuple-element.18), calls=%async_computation | async-start | bytes 524288 | tf_op jit(solution)/shard_map/all_to_all | solution.py:558
  40.9 0.0 copy-start.1
  40.9 0.0 collective-permute-done.8.other.sib
  40.9 1.0 %join_chip.1 = f32[512,128]{1,0:T(8,128)} custom-call(f32[768,128]{1,0:T(8,128)S(1)} %get-tuple-element.17.mine.send_a, f32[768,128]{1,0:T(8,128)S(1)} %collective-permute-done.8.other.sib), custom_call_target="tpu_custom_call" | custom-call | tf_op jit(solution)/shard_map/join_chip/pallas_call | solution.py:561
  42.0 5.5 %collective-permute-start.10 = (f32[512,128]{1,0:T(8,128)}, f32[512,128]{1,0:T(8,128)S(1)}, u32[]{:S(2)}, u32[]{:S(2)}) collective-permute-start(f32[512,128]{1,0:T(8,128)} %join_chip.1), channel_id=1, source_target_pairs={{16,4},{24,12},{32,20},{40,28},{48,36},{56,44},{64,52},{72,60},{80... | collective-permute-start | bytes 786440 | tf_op jit(solution)/shard_map/ppermute | solution.py:514
  47.5 3.7 %collective-permute-start.9 = (f32[512,128]{1,0:T(8,128)}, f32[512,128]{1,0:T(8,128)}, u32[]{:S(2)}, u32[]{:S(2)}) collective-permute-start(f32[512,128]{1,0:T(8,128)} %join_chip.1), channel_id=1, source_target_pairs={{4,8},{8,4},{12,16},{16,12},{20,24},{24,20},{28,32},{32,28},{36,40... | collective-permute-start | bytes 786440 | tf_op jit(solution)/shard_map/ppermute | solution.py:511
  51.2 5.2 %collective-permute-start.7 = (f32[1,256,256]{2,1,0:T(8,128)}, f32[1,256,256]{2,1,0:T(8,128)}, u32[]{:S(2)}, u32[]{:S(2)}) collective-permute-start(f32[1,256,256]{2,1,0:T(8,128)} %get-tuple-element.16), channel_id=1, source_target_pairs={{4,8},{8,4},{12,16},{16,12},{20,24},{24,20},{28,32},{32,28},{36,40... | collective-permute-start | bytes 786440 | tf_op jit(solution)/shard_map/ppermute | solution.py:511
  56.4 0.0 all-to-all-done.gathered
  56.4 0.0 collective-permute-done.10.far
  56.4 2.4 %collective-permute-done.9.near = f32[512,128]{1,0:T(8,128)} collective-permute-done((f32[512,128]{1,0:T(8,128)}, f32[512,128]{1,0:T(8,128)}, u32[]{:S(2)}, u32[]{:S(2)}) %collective-permute-start.9) | collective-permute-done | bytes 262176 | tf_op jit(solution)/shard_map/ppermute | solution.py:511
  58.8 0.0 collective-permute-start.11
  58.8 0.5 collective-permute-start.12
  59.3 0.0 copy-done.1
  59.3 0.1 copy.6.groups
  59.4 3.1 %collective-permute-done.7.near_f = f32[1,256,256]{2,1,0:T(8,128)} collective-permute-done((f32[1,256,256]{2,1,0:T(8,128)}, f32[1,256,256]{2,1,0:T(8,128)}, u32[]{:S(2)}, u32[]{:S(2)}) %collective-permute-start.7) | collective-permute-done | bytes 262176 | tf_op jit(solution)/shard_map/ppermute | solution.py:511
  62.5 0.0 collective-permute-done.11.sib_near
  62.5 0.0 collective-permute-done.12.sib_far
  62.5 5.4 %correct_and_smooth.1 = (f32[1,256,256]{2,1,0:T(8,128)S(1)}, f32[1,256,256]{2,1,0:T(8,128)S(1)}) custom-call(f32[1]{0:T(128)S(6)} %copy.7.kappa_in, f32[4,256,256]{2,1,0:T(8,128)} %get-tuple-element.14.halo_in, f32[1,2,256,256]{3,2,1,0:T(8,128)S(1)} %copy-done, f32[2,256,256]{2,1,0:T(8,128)S(1)} %collect_density.1.dens, ...), custom_call_target="tpu_custom_call" | custom-call | tf_op jit(solution)/shard_map/correct_and_smooth/pallas_call | solution.py:576
  67.9 0.1 collective-permute-start.13
  68.0 5.2 %collective-permute-start.14 = (f32[1,256,256]{2,1,0:T(8,128)S(1)}, f32[1,256,256]{2,1,0:T(8,128)S(1)}, u32[]{:S(2)}, u32[]{:S(2)}) collective-permute-start(f32[1,256,256]{2,1,0:T(8,128)S(1)} %get-tuple-element.23.to_b), channel_id=1, source_target_pairs={{4,8},{8,4},{12,16},{16,12},{20,24},{24,20},{28,32},{32,28},{36,40... | collective-permute-start | bytes 786440 | tf_op jit(solution)/shard_map/ppermute | solution.py:511
  73.2 1.0 %residual_inside.1 = (f32[1,2,256,256]{3,2,1,0:T(8,128)}, f32[2,256,256]{2,1,0:T(8,128)S(1)}) custom-call(f32[1]{0:T(128)S(6)} %copy.7.kappa_in, f32[1,2,256,256]{3,2,1,0:T(8,128)S(1)} %copy-done, f32[2,256,256]{2,1,0:T(8,128)S(1)} %collect_density.1.dens, f32[1,256,256]{2,1,0:T(8,128)S(1)} %get-tuple-element.22.to_a, f32[1,256,256]{2,1,0:T(8,128)S(1)} %get-tuple-element.23.to_b), custom_call_target="tpu_custom_call" | custom-call | tf_op jit(solution)/shard_map/residual_inside/pallas_call | solution.py:605
  74.2 0.0 collective-permute-done.13.halo_a
  74.2 4.8 %collective-permute-done.14.halo_b = f32[1,256,256]{2,1,0:T(8,128)S(1)} collective-permute-done((f32[1,256,256]{2,1,0:T(8,128)S(1)}, f32[1,256,256]{2,1,0:T(8,128)S(1)}, u32[]{:S(2)}, u32[]{:S(2)}) %collective-permute-start.14) | collective-permute-done | bytes 262176 | tf_op jit(solution)/shard_map/ppermute | solution.py:511
  79.0 1.6 %residual.1 = f32[1,2,256,256]{3,2,1,0:T(8,128)} custom-call(f32[1]{0:T(128)S(6)} %copy.7.kappa_in, f32[2,256,256]{2,1,0:T(8,128)S(1)} %get-tuple-element.25.inside, f32[1,256,256]{2,1,0:T(8,128)S(1)} %collective-permute-done.13.halo_a, f32[1,256,256]{2,1,0:T(8,128)S(1)} %collective-permute-done.14.halo_b), custom_call_target="tpu_custom_call" | custom-call | tf_op jit(solution)/shard_map/residual/pallas_call | solution.py:618
Async XLA Ops:
  0.6 26.3 %copy-start = (f32[1,2,256,256]{3,2,1,0:T(8,128)S(1)}, f32[1,2,256,256]{3,2,1,0:T(8,128)}, u32[]{:S(2)}) copy-start(f32[1,2,256,256]{3,2,1,0:T(8,128)} %rhs.5) | copy-start | bytes 1572868
  0.6 11.1 %collective-permute-start = (f32[2,64,256]{2,1,0:T(8,128)}, f32[2,64,256]{2,1,0:T(8,128)S(1)}, u32[]{:S(2)}, u32[]{:S(2)}) collective-permute-start(f32[2,64,256]{2,1,0:T(8,128)} %shard.1), channel_id=1, source_target_pairs={{0,1},{1,2},{2,3},{3,0},{4,5},{5,6},{6,7},{7,4},{8,9},{9,10},{10,1... | collective-permute-start | bytes 393224 | tf_op jit(solution)/shard_map/ppermute | solution.py:517
  2.0 9.8 %collective-permute-start.1 = (f32[2,64,256]{2,1,0:T(8,128)}, f32[2,64,256]{2,1,0:T(8,128)S(1)}, u32[]{:S(2)}, u32[]{:S(2)}) collective-permute-start(f32[2,64,256]{2,1,0:T(8,128)} %shard.1), channel_id=1, source_target_pairs={{0,2},{1,3},{2,0},{3,1},{4,6},{5,7},{6,4},{7,5},{8,10},{9,11},{10,... | collective-permute-start | bytes 393224 | tf_op jit(solution)/shard_map/ppermute | solution.py:517
  4.6 7.2 %collective-permute-start.2 = (f32[2,64,256]{2,1,0:T(8,128)}, f32[2,64,256]{2,1,0:T(8,128)S(1)}, u32[]{:S(2)}, u32[]{:S(2)}) collective-permute-start(f32[2,64,256]{2,1,0:T(8,128)} %shard.1), channel_id=1, source_target_pairs={{0,3},{1,0},{2,1},{3,2},{4,7},{5,4},{6,5},{7,6},{8,11},{9,8},{10,9... | collective-permute-start | bytes 393224 | tf_op jit(solution)/shard_map/ppermute | solution.py:517
  5.7 12.7 %collective-permute-start.3 = (f32[1,2,256,256]{3,2,1,0:T(8,128)}, f32[1,2,256,256]{3,2,1,0:T(8,128)S(1)}, u32[]{:S(2)}, u32[]{:S(2)}) collective-permute-start(f32[1,2,256,256]{3,2,1,0:T(8,128)} %rhs.5), channel_id=1, source_target_pairs={{0,4},{4,0},{8,12},{12,8},{16,20},{20,16},{24,28},{28,24},{32,36},... | collective-permute-start | bytes 1572872 | tf_op jit(solution)/shard_map/ppermute | solution.py:508
  7.2 14.0 %collective-permute-start.5 = (f32[1,2,256,256]{3,2,1,0:T(8,128)}, f32[1,2,256,256]{3,2,1,0:T(8,128)S(1)}, u32[]{:S(2)}, u32[]{:S(2)}) collective-permute-start(f32[1,2,256,256]{3,2,1,0:T(8,128)} %rhs.5), channel_id=1, source_target_pairs={{4,8},{8,4},{12,16},{16,12},{20,24},{24,20},{28,32},{32,28},{36,40... | collective-permute-start | bytes 1572872 | tf_op jit(solution)/shard_map/ppermute | solution.py:511
  12.8 8.5 %collective-permute-start.4 = (f32[2,256,256]{2,1,0:T(8,128)S(1)}, f32[2,256,256]{2,1,0:T(8,128)S(1)}, u32[]{:S(2)}, u32[]{:S(2)}) collective-permute-start(f32[2,256,256]{2,1,0:T(8,128)S(1)} %collect_density.1.dens), channel_id=1, source_target_pairs={{0,4},{4,0},{8,12},{12,8},{16,20},{20,16},{24,28},{28,24},{32,36},... | collective-permute-start | bytes 1572872 | tf_op jit(solution)/shard_map/ppermute | solution.py:508
  13.1 13.8 %collective-permute-start.6 = (f32[2,256,256]{2,1,0:T(8,128)S(1)}, f32[2,256,256]{2,1,0:T(8,128)S(1)}, u32[]{:S(2)}, u32[]{:S(2)}) collective-permute-start(f32[2,256,256]{2,1,0:T(8,128)S(1)} %collect_density.1.dens), channel_id=1, source_target_pairs={{4,8},{8,4},{12,16},{16,12},{20,24},{24,20},{28,32},{32,28},{36,40... | collective-permute-start | bytes 1572872 | tf_op jit(solution)/shard_map/ppermute | solution.py:511
  31.5 9.5 %collective-permute-start.8 = (f32[768,128]{1,0:T(8,128)S(1)}, f32[768,128]{1,0:T(8,128)S(1)}, u32[]{:S(2)}, u32[]{:S(2)}) collective-permute-start(f32[768,128]{1,0:T(8,128)S(1)} %get-tuple-element.17.mine.send_a), channel_id=1, source_target_pairs={{0,4},{4,0},{8,12},{12,8},{16,20},{20,16},{24,28},{28,24},{32,36},... | collective-permute-start | bytes 1179656 | tf_op jit(solution)/shard_map/ppermute | solution.py:508
  31.6 24.8 %all-to-all-start = ((f32[64,8,128]{2,1,0:T(8,128)}), f32[64,8,128]{2,1,0:T(8,128)S(1)}, u32[]{:S(2)}, u32[]{:S(2)}) async-start(f32[64,8,128]{2,1,0:T(8,128)} %get-tuple-element.18), calls=%async_computation | async-start | bytes 524288 | tf_op jit(solution)/shard_map/all_to_all | solution.py:558
  40.9 18.4 %copy-start.1 = (s32[64,16]{0,1:T(8,128)S(1)}, s32[64,16]{0,1:T(8,128)}, u32[]{:S(2)}) copy-start(s32[64,16]{0,1:T(8,128)} %param.7) | copy-start | bytes 12292
  42.0 14.4 %collective-permute-start.10 = (f32[512,128]{1,0:T(8,128)}, f32[512,128]{1,0:T(8,128)S(1)}, u32[]{:S(2)}, u32[]{:S(2)}) collective-permute-start(f32[512,128]{1,0:T(8,128)} %join_chip.1), channel_id=1, source_target_pairs={{16,4},{24,12},{32,20},{40,28},{48,36},{56,44},{64,52},{72,60},{80... | collective-permute-start | bytes 786440 | tf_op jit(solution)/shard_map/ppermute | solution.py:514
  47.5 11.3 %collective-permute-start.9 = (f32[512,128]{1,0:T(8,128)}, f32[512,128]{1,0:T(8,128)}, u32[]{:S(2)}, u32[]{:S(2)}) collective-permute-start(f32[512,128]{1,0:T(8,128)} %join_chip.1), channel_id=1, source_target_pairs={{4,8},{8,4},{12,16},{16,12},{20,24},{24,20},{28,32},{32,28},{36,40... | collective-permute-start | bytes 786440 | tf_op jit(solution)/shard_map/ppermute | solution.py:511
  51.2 11.3 %collective-permute-start.7 = (f32[1,256,256]{2,1,0:T(8,128)}, f32[1,256,256]{2,1,0:T(8,128)}, u32[]{:S(2)}, u32[]{:S(2)}) collective-permute-start(f32[1,256,256]{2,1,0:T(8,128)} %get-tuple-element.16), channel_id=1, source_target_pairs={{4,8},{8,4},{12,16},{16,12},{20,24},{24,20},{28,32},{32,28},{36,40... | collective-permute-start | bytes 786440 | tf_op jit(solution)/shard_map/ppermute | solution.py:511
  58.8 3.7 %collective-permute-start.11 = (f32[512,128]{1,0:T(8,128)}, f32[512,128]{1,0:T(8,128)}, u32[]{:S(2)}, u32[]{:S(2)}) collective-permute-start(f32[512,128]{1,0:T(8,128)} %collective-permute-done.9.near), channel_id=1, source_target_pairs={{0,4},{4,0},{8,12},{12,8},{16,20},{20,16},{24,28},{28,24},{32,36},... | collective-permute-start | bytes 786440 | tf_op jit(solution)/shard_map/ppermute | solution.py:508
  58.8 3.7 %collective-permute-start.12 = (f32[512,128]{1,0:T(8,128)S(1)}, f32[512,128]{1,0:T(8,128)}, u32[]{:S(2)}, u32[]{:S(2)}) collective-permute-start(f32[512,128]{1,0:T(8,128)S(1)} %collective-permute-done.10.far), channel_id=1, source_target_pairs={{0,4},{4,0},{8,12},{12,8},{16,20},{20,16},{24,28},{28,24},{32,36},... | collective-permute-start | bytes 786440 | tf_op jit(solution)/shard_map/ppermute | solution.py:508
  67.9 6.3 %collective-permute-start.13 = (f32[1,256,256]{2,1,0:T(8,128)S(1)}, f32[1,256,256]{2,1,0:T(8,128)S(1)}, u32[]{:S(2)}, u32[]{:S(2)}) collective-permute-start(f32[1,256,256]{2,1,0:T(8,128)S(1)} %get-tuple-element.22.to_a), channel_id=1, source_target_pairs={{0,4},{4,0},{8,12},{12,8},{16,20},{20,16},{24,28},{28,24},{32,36},... | collective-permute-start | bytes 786440 | tf_op jit(solution)/shard_map/ppermute | solution.py:508
  68.0 11.0 %collective-permute-start.14 = (f32[1,256,256]{2,1,0:T(8,128)S(1)}, f32[1,256,256]{2,1,0:T(8,128)S(1)}, u32[]{:S(2)}, u32[]{:S(2)}) collective-permute-start(f32[1,256,256]{2,1,0:T(8,128)S(1)} %get-tuple-element.23.to_b), channel_id=1, source_target_pairs={{4,8},{8,4},{12,16},{16,12},{20,24},{24,20},{28,32},{32,28},{36,40... | collective-permute-start | bytes 786440 | tf_op jit(solution)/shard_map/ppermute | solution.py:511

commit v4 on v3

--- a/solution.py
+++ b/solution.py
@@ -99,11 +99,18 @@
         copy.wait()
 
 
-def join_kernel(mine, other, out, sems):
-    rows = out.shape[0] // 2
+def join_kernel(mine, other, density1_sib, density1_own, near_f, near, far, sems):
+    del near_f
+    half = far.shape[0] // 3
+    parts = [pl.ds(i * half, half) for i in range(4)]
     copies = [
-        pltpu.make_async_copy(mine.at[pl.ds(0, rows)], out.at[pl.ds(0, rows)], sems.at[0]),
-        pltpu.make_async_copy(other.at[pl.ds(0, rows)], out.at[pl.ds(rows, rows)], sems.at[1]),
+        pltpu.make_async_copy(mine.at[parts[0]], near.at[parts[0]], sems.at[0]),
+        pltpu.make_async_copy(density1_own, near.at[parts[1]], sems.at[1]),
+        pltpu.make_async_copy(other.at[parts[0]], near.at[parts[2]], sems.at[2]),
+        pltpu.make_async_copy(density1_sib, near.at[parts[3]], sems.at[3]),
+        pltpu.make_async_copy(mine.at[parts[0]], far.at[parts[0]], sems.at[4]),
+        pltpu.make_async_copy(density1_own, far.at[parts[1]], sems.at[5]),
+        pltpu.make_async_copy(other.at[parts[1]], far.at[parts[2]], sems.at[6]),
     ]
     start_all(copies)
     wait_all(copies)
@@ -121,89 +128,125 @@
     wait_all(copies)
 
 
+def begin_layers(source, density, layers, work, index, wd, s1, scale, top, keep):
+    height = density.shape[1]
+
+    def begin(row):
+        part = pl.ds(row, CHUNK)
+        pair = density[0, part, :] + density[1, part, :]
+        put_halves(work, index, part, pair)
+        for layer, slot in layers:
+            factor = top / (density[layer, part, :] + 14.0 * scale)
+            if slot in keep:
+                wd[keep[slot], part, :] = factor
+            s1[slot, pl.ds(row + 8, CHUNK), :] = factor * source[0, layer, part, :]
+
+    chunks(height, begin)
+
+
+def near_kernel(
+    kappa_in, rhs, dens, rhs_a, dens_a, rhs_b,
+    s1_own, s2_hi, wd_own, halo_out, density1_own, density1_sib, send_b,
+    s1, wd, work, kappa, sems,
+):
+    del rhs_b
+    core, brick, bricks = position()
+    load = pltpu.make_async_copy(kappa_in, kappa, sems.at[0])
+    stores = [
+        pltpu.make_async_copy(rhs_a.at[0, core], halo_out.at[0], sems.at[1]),
+        pltpu.make_async_copy(dens_a.at[core], halo_out.at[1], sems.at[2]),
+    ]
+    load.start()
+    start_all(stores)
+    height, width = dens.shape[1:]
+    half = height // 2
+    clear_edges(s1)
+    clear_edges(s2_hi)
+    load.wait()
+    scale = kappa[0]
+    valid = jnp.where(core == 0, brick < bricks - 1, brick > 0).astype(f32)
+    begin_layers(rhs, dens, ((core, 0), (1 - core, 1)), work, 0, wd, s1, scale, WEIGHT, {0: 0, 1: 1})
+    begin_layers(rhs_a, dens_a, ((core, 2), (1 - core, 3)), work, 1, wd, s1, scale, WEIGHT * valid, {2: 2})
+    for j in (1, 2):
+
+        def smooth(row, j=j):
+            part = pl.ds(row, CHUNK)
+            v = s1[j, pl.ds(row + 8, CHUNK), :]
+            f = stencil(s1, j, row, CHUNK)
+            source = rhs[0, 1 - core, part, :] if j == 1 else rhs_a[0, core, part, :]
+            new = (1.0 - WEIGHT) * v + wd[j, part, :] * (source + 2.0 * scale * (f - v))
+            s2_hi[j - 1, pl.ds(row + 8, CHUNK), :] = new
+            if j == 1:
+                send_b[0, part, :] = new
+
+        chunks(height, smooth)
+    s1_own[...] = s1[0:2]
+    wd_own[...] = wd[0]
+    columns = coarsen_z(height, width)
+    density1_own[...] = 0.125 * dot_exact(pair_rows(work, 0, half), columns)
+    density1_sib[...] = 0.125 * dot_exact(pair_rows(work, 1, half), columns)
+    wait_all(stores)
+
+
 def first_kernel(
-    kappa_in, rhs, dens, rhs_a, dens_a, rhs_b, dens_b,
-    s2_out, halo_out, send_a, send_b, payload,
-    s1, s2, wd, rhs_w, work, kappa, sems,
+    kappa_in, rhs, dens, rhs_b, dens_b, s1_own, s2_hi, wd_own, density1_own, density1_sib,
+    s2_lo, halo_out, send_a, send_f, payload,
+    s1, s2, wd, work, kappa, sems,
 ):
     core, brick, bricks = position()
     load = pltpu.make_async_copy(kappa_in, kappa, sems.at[0])
+    stores = [
+        pltpu.make_async_copy(rhs_b.at[0, 1 - core], halo_out.at[0], sems.at[1]),
+        pltpu.make_async_copy(dens_b.at[1 - core], halo_out.at[1], sems.at[2]),
+    ]
     load.start()
+    start_all(stores)
     height, width = dens.shape[1:]
     half = height // 2
     clear_edges(s1)
     clear_edges(s2)
+    s1[2:4] = s1_own[...]
+    s2[2:4] = s2_hi[...]
     load.wait()
     scale = kappa[0]
     scale1 = 0.25 * scale
-
-    base_b = 4 * core
-    base_a = 4 * (1 - core)
-    valid_lo = (brick > 0).astype(f32)
-    valid_hi = (brick < bricks - 1).astype(f32)
-    valid_b = jnp.where(core == 0, valid_lo, valid_hi)
-    valid_a = jnp.where(core == 0, valid_hi, valid_lo)
-    for ref, density_ref, base, valid in ((rhs_b, dens_b, base_b, valid_b), (rhs_a, dens_a, base_a, valid_a), (rhs, dens, 2, None)):
-        top = WEIGHT if valid is None else WEIGHT * valid
-
-        def begin(row, ref=ref, density_ref=density_ref, base=base, top=top):
-            part = pl.ds(row, CHUNK)
-            pair = jnp.zeros((CHUNK, width), f32)
-            for layer in range(2):
-                density = density_ref[layer, part, :]
-                factor = top / (density + 14.0 * scale)
-                wd[base + layer, part, :] = factor
-                source = ref[0, layer, part, :]
-                rhs_w[base + layer, part, :] = source
-                s1[base + layer, pl.ds(row + 8, CHUNK), :] = factor * source
-                pair = pair + density
-            put_halves(work, base >> 1, part, pair)
-
-        chunks(height, begin)
-
-    stores = [
-        pltpu.make_async_copy(rhs_w.at[1], halo_out.at[0], sems.at[1]),
-        pltpu.make_async_copy(rhs_w.at[4], halo_out.at[1], sems.at[2]),
-        pltpu.make_async_copy(dens_b.at[1 - core], halo_out.at[2 + core], sems.at[3]),
-        pltpu.make_async_copy(dens_a.at[core], halo_out.at[3 - core], sems.at[4]),
-    ]
-    start_all(stores)
-
-    for j in range(1, 5):
+    valid_lo = jnp.where(core == 0, brick > 0, brick < bricks - 1).astype(f32)
+    valid_hi = jnp.where(core == 0, brick < bricks - 1, brick > 0).astype(f32)
+    begin_layers(rhs_b, dens_b, ((core, 0), (1 - core, 1)), work, 0, wd, s1, scale, WEIGHT * valid_lo, {1: 0})
+
+    for j in (1, 2):
 
         def smooth(row, j=j):
             part = pl.ds(row, CHUNK)
             v = s1[j, pl.ds(row + 8, CHUNK), :]
             f = stencil(s1, j, row, CHUNK)
-            new = (1.0 - WEIGHT) * v + wd[j, part, :] * (rhs_w[j, part, :] + 2.0 * scale * (f - v))
+            source, factor = (rhs_b[0, 1 - core, part, :], wd[0, part, :]) if j == 1 else (rhs[0, core, part, :], wd_own[part, :])
+            new = (1.0 - WEIGHT) * v + factor * (source + 2.0 * scale * (f - v))
             s2[j - 1, pl.ds(row + 8, CHUNK), :] = new
-            s2_out[j - 1, part, :] = new
+            s2_lo[j - 1, part, :] = new
 
         chunks(height, smooth)
-    mine = 1 + core
-    send_a[2 * half : 4 * half, :] = s2_out[mine, :, :half]
-    send_a[4 * half : 6 * half, :] = s2_out[mine, :, half:]
-    send_b[0] = s2_out[2 - core]
 
     def restrict(row):
         part = pl.ds(row, CHUNK)
         total = jnp.zeros((CHUNK, width), f32)
-        for layer in range(2):
-            v = s2[1 + layer, pl.ds(row + 8, CHUNK), :]
-            f = stencil(s2, 1 + layer, row, CHUNK)
+        for slot, layer in ((1, core), (2, 1 - core)):
+            v = s2[slot, pl.ds(row + 8, CHUNK), :]
+            f = stencil(s2, slot, row, CHUNK)
             center = dens[layer, part, :] + 16.0 * scale
-            total = total + (rhs_w[2 + layer, part, :] - center * v + 2.0 * scale * f)
-        put_halves(work, 3, part, total)
+            total = total + (rhs[0, layer, part, :] - center * v + 2.0 * scale * f)
+        put_halves(work, 1, part, total)
 
     chunks(height, restrict)
     columns = coarsen_z(height, width)
-    density1 = [0.125 * dot_exact(pair_rows(work, i, half), columns) for i in range(3)]
-    coarse_res = 0.125 * dot_exact(pair_rows(work, 3, half), columns)
+    density1 = [0.125 * dot_exact(pair_rows(work, 0, half), columns), density1_own[...], density1_sib[...]]
+    coarse_res = 0.125 * dot_exact(pair_rows(work, 1, half), columns)
 
     send_a[0:half, :] = coarse_res
-    send_a[half : 2 * half, :] = density1[1]
-
-    first = 0.85 * coarse_res / (density1[1] + 14.0 * scale1)
+    send_f[0] = s2_lo[1]
+
+    first = WEIGHT * coarse_res / (density1[1] + 14.0 * scale1)
+    send_a[half : 2 * half, :] = first
     pad = jnp.zeros((8, half), f32)
     spread = filter_yz(jnp.concatenate([pad, first, pad], 0))
     own_factor = WEIGHT / (density1[1] + 14.0 * scale1)
@@ -231,6 +274,11 @@
             plain.append(jnp.sum(rest[at : at + block], axis=0, keepdims=True))
     for t in range(TILES):
         plain.append(jnp.sum(density1[1][t * block : (t + 1) * block], axis=0, keepdims=True))
+    for rows in (filtered, plain):
+        for t in range(TILES):
+            low, high = rows[t], rows[2 * TILES + t]
+            rows[t] = jnp.where(core == 0, low, high)
+            rows[2 * TILES + t] = jnp.where(core == 0, high, low)
     filtered.append(jnp.zeros((4, half), f32))
     filtered = jnp.concatenate(filtered, 0)
     plain = jnp.concatenate(plain, 0)
@@ -332,19 +380,21 @@
 
 
 def second_kernel(
-    kappa_in, halo_in, rhs, dens, s2, near_f, send_a, sib, near, far, sib_near, sib_far, gathered, groups,
+    kappa_in, halo_lo_in, halo_hi_in, rhs, dens, s2_lo, s2_hi, near_f, sib_f, density1_sib, density1_own, send_a, sib, near, far, sib_near, sib_far, gathered, groups,
     to_a, to_b,
-    fixes, cres, cden, c1, c2, c3, grown, s3, s4, wd, halo, last, kappa, sems,
+    fixes, cres, cden, c1, c2, c3, grown, s3, s4, wd, halo, kappa, sems,
 ):
     core, brick, bricks = position()
     load = pltpu.make_async_copy(kappa_in, kappa, sems.at[0])
     load.start()
-    load_halo = pltpu.make_async_copy(halo_in, halo, sems.at[1])
-    load_halo.start()
+    loads = [
+        pltpu.make_async_copy(halo_lo_in, halo.at[pl.ds(0, 2)], sems.at[1]),
+        pltpu.make_async_copy(halo_hi_in, halo.at[pl.ds(2, 2)], sems.at[2]),
+    ]
+    start_all(loads)
     half = cres.shape[1]
     height, width = rhs.shape[2:]
     block = half // TILES
-    inner = pl.ds(8, height)
     for ref in (c1, c2, c3, s3, s4):
         clear_edges(ref)
     load.wait()
@@ -360,20 +410,23 @@
     per = (lane >> (half.bit_length() - 1)) * 4 + ((lane & (half - 1)) >> (block.bit_length() - 1))
     spread = dot_exact(window, (iota((128, TILES * half), 0) == per).astype(bf16))
 
-    sign = 2 * core - 1
-    for ref, first, at in (
-        (send_a, 0, 0), (sib, 0, -1),
-        (near, 0, 1), (near, 2, 2), (far, 0, 3), (far, 2, 4),
-        (sib_near, 0, -2), (sib_near, 2, -3), (sib_far, 0, -4),
+    for index, (ref, i), (ref_density, k) in (
+        (1, (far, 0), (far, 1)),
+        (2, (near, 2), (near, 3)),
+        (3, (near, 0), (near, 1)),
+        (4, (send_a, 0), (density1_own, 0)),
+        (5, (sib, 0), (density1_sib, 0)),
+        (6, (sib_near, 0), (sib_near, 1)),
+        (7, (sib_near, 2), (sib_near, 3)),
+        (8, (sib_far, 0), (sib_far, 1)),
     ):
-        index = 4 + sign * at
-        cres[index] = ref[first * half : (first + 1) * half, :]
-        cden[index] = ref[(first + 1) * half : (first + 2) * half, :]
+        cres[index] = ref[i * half : (i + 1) * half, :]
+        cden[index] = ref_density[k * half : (k + 1) * half, :]
 
     body = pl.ds(8, half)
-    factors = []
-    for i in range(9):
-        place = brick + (i - 4)
+    c1[0, body, :] = far[2 * half : 3 * half, :]
+    for i in range(1, 9):
+        place = brick + jnp.where(core == 0, i - 4, 4 - i)
         valid = ((place >= 0) & (place < bricks)).astype(f32)
         factor = (WEIGHT * valid) / (cden[i] + 14.0 * scale1)
         cden[i] = factor
@@ -386,9 +439,8 @@
 
     for i in range(7):
         value = relax(c1, i + 1, i + 1)
-        pieces = [
-            jnp.broadcast_to(spread[i + 1 : i + 2, t * half : (t + 1) * half], (block, half)) for t in range(TILES)
-        ]
+        row = jnp.where(core == 0, spread[i + 1 : i + 2], spread[7 - i : 8 - i])
+        pieces = [jnp.broadcast_to(row[:, t * half : (t + 1) * half], (block, half)) for t in range(TILES)]
         c2[i, body, :] = value + jnp.concatenate(pieces, 0)
     for i in range(5):
         c3[i, body, :] = relax(c2, i + 1, i + 2)
@@ -398,14 +450,19 @@
         put_halves(grown, i, pl.ds(0, half, stride=2), fine)
         put_halves(grown, i, pl.ds(1, half, stride=2), fine)
 
-    load_halo.wait()
+    wait_all(loads)
+    inner = pl.ds(8, height)
     for k in range(2):
         side = slice(k * half, (k + 1) * half)
-        for i in range(4):
-            s3[i + 1, inner, side] = s2[i, :, side] + grown[(i + 1) >> 1, k]
-        s3[5 * core, inner, side] = near_f[0, :, side] + grown[2 * core, k]
-        s3[5 * (1 - core), inner, side] = sib[2 * (k + 1) * half : 2 * (k + 2) * half, :] + grown[2 * (1 - core), k]
-
+        s3[0, inner, side] = near_f[0, :, side] + grown[0, k]
+        s3[1, inner, side] = s2_lo[0, :, side] + grown[0, k]
+        s3[2, inner, side] = s2_lo[1, :, side] + grown[1, k]
+        s3[3, inner, side] = s2_hi[0, inner, side] + grown[1, k]
+        s3[4, inner, side] = s2_hi[1, inner, side] + grown[2, k]
+        s3[5, inner, side] = sib_f[0, :, side] + grown[2, k]
+
+    at_start = jnp.where(core == 0, brick > 0, brick < bricks - 1).astype(f32)
+    at_end = jnp.where(core == 0, brick < bricks - 1, brick > 0).astype(f32)
     for j in range(4):
 
         def smooth(row, j=j):
@@ -413,29 +470,28 @@
             v = s3[j + 1, pl.ds(row + 8, CHUNK), :]
             f = stencil(s3, j + 1, row, CHUNK)
             if j in (1, 2):
-                source, density, top = rhs[0, j - 1, part, :], dens[j - 1, part, :], WEIGHT
+                layer = core if j == 1 else 1 - core
+                source, density, top = rhs[0, layer, part, :], dens[layer, part, :], WEIGHT
             else:
-                edge = j // 3
-                source, density = halo[edge, part, :], halo[2 + edge, part, :]
-                top = WEIGHT * (brick < bricks - 1 if edge else brick > 0).astype(f32)
+                edge = 2 * (j // 3)
+                source, density = halo[edge, part, :], halo[edge + 1, part, :]
+                top = WEIGHT * (at_end if edge else at_start)
             factor = top / (density + 14.0 * scale)
             wd[j, part, :] = factor
             new = (1.0 - WEIGHT) * v + factor * (source + 2.0 * scale * (f - v))
             s4[j, pl.ds(row + 8, CHUNK), :] = new
 
         chunks(height, smooth)
-    for j in range(2):
-
-        def smooth_last(row, j=j):
+    for j, out in ((0, to_b), (1, to_a)):
+
+        def smooth_last(row, j=j, out=out):
             part = pl.ds(row, CHUNK)
             v = s4[j + 1, pl.ds(row + 8, CHUNK), :]
             f = stencil(s4, j + 1, row, CHUNK)
-            new = (1.0 - WEIGHT) * v + wd[j + 1, part, :] * (rhs[0, j, part, :] + 2.0 * scale * (f - v))
-            last[j, part, :] = new
+            source = rhs[0, core if j == 0 else 1 - core, part, :]
+            out[0, part, :] = (1.0 - WEIGHT) * v + wd[j + 1, part, :] * (source + 2.0 * scale * (f - v))
 
         chunks(height, smooth_last)
-    to_a[0] = last[1 - core]
-    to_b[0] = last[core]
 
 
 def inside_kernel(kappa_in, rhs, dens, to_a, to_b, sol_out, out, s, kappa, sems):
@@ -531,52 +587,76 @@
 
     dens_b = swap_b(dens)
     dens_a = swap_a(dens)
-    s2, halo, send_a, send_b, payload = pl.pallas_call(
+    s1_own, s2_hi, wd_own, halo_hi, density1_own, density1_sib, send_b = pl.pallas_call(
+        near_kernel,
+        out_shape=(
+            shape(2, height + 16, width),
+            shape(2, height + 16, width),
+            shape(height, width),
+            pltpu.HBM((2, height, width), f32),
+            shape(half, half),
+            shape(half, half),
+            shape(1, height, width),
+        ),
+        in_specs=[ANY] + [VM] * 4 + [ANY],
+        out_specs=[VM, VM, VM, HBM, VM, VM, VM],
+        scratch_shapes=[
+            pltpu.VMEM((4, height + 16, width), f32),
+            pltpu.VMEM((3, height, width), f32),
+            pltpu.VMEM((2, 2, height, half), f32),
+            pltpu.SMEM((1,), f32),
+            pltpu.SemaphoreType.DMA((3,)),
+        ],
+        compiler_params=PARAMS,
+        name="smooth_in_chip",
+    )(kappa, rhs, dens, rhs_a, dens_a, rhs_b)
+    near_f = swap_b(send_b)
+    s2_lo, halo_lo, send_a, send_f, payload = pl.pallas_call(
         first_kernel,
         out_shape=(
-            shape(4, height, width),
-            pltpu.HBM((4, height, width), f32),
-            shape(6 * half, half),
+            shape(2, height, width),
+            pltpu.HBM((2, height, width), f32),
+            shape(2 * half, half),
             shape(1, height, width),
             shape(bricks, 8, 128),
         ),
-        in_specs=[ANY] + [VM] * 6,
+        in_specs=[ANY] + [VM] * 9,
         out_specs=[VM, HBM, VM, VM, VM],
         scratch_shapes=[
-            pltpu.VMEM((6, height + 16, width), f32),
             pltpu.VMEM((4, height + 16, width), f32),
-            pltpu.VMEM((6, height, width), f32),
-            pltpu.VMEM((6, height, width), f32),
-            pltpu.VMEM((4, 2, height, half), f32),
+            pltpu.VMEM((4, height + 16, width), f32),
+            pltpu.VMEM((1, height, width), f32),
+            pltpu.VMEM((2, 2, height, half), f32),
             pltpu.SMEM((1,), f32),
-            pltpu.SemaphoreType.DMA((5,)),
+            pltpu.SemaphoreType.DMA((3,)),
         ],
         compiler_params=PARAMS,
         name="smooth_and_restrict",
-    )(kappa, rhs, dens, rhs_a, dens_a, rhs_b, dens_b)
+    )(kappa, rhs, dens, rhs_b, dens_b, s1_own, s2_hi, wd_own, density1_own, density1_sib)
 
     gathered = lax.all_to_all(payload, "brick", 0, 0, tiled=True)
     sib = swap_a(send_a)
-    near_f = swap_b(send_b)
-    both = pl.pallas_call(
+    sib_f = swap_a(send_f)
+    near_out, far_out = pl.pallas_call(
         join_kernel,
-        out_shape=shape(4 * half, half),
-        in_specs=[ANY] * 2,
-        out_specs=VM,
-        scratch_shapes=[pltpu.SemaphoreType.DMA((2,))],
+        out_shape=(shape(4 * half, half), shape(3 * half, half)),
+        in_specs=[ANY] * 5,
+        out_specs=[VM] * 2,
+        scratch_shapes=[pltpu.SemaphoreType.DMA((7,))],
         compiler_params=PARAMS,
         name="join_chip",
-    )(send_a, sib)
-    near = swap_b(both)
-    far = swap_far(both)
+    )(send_a, sib, density1_sib, density1_own, near_f)
+    near = swap_b(near_out)
+    far = swap_far(far_out)
     near, far, gathered = lax.optimization_barrier((near, far, gathered))
     sib_near = swap_a(near)
     sib_far = swap_a(far)
 
+    in_hbm = functools.partial(pltpu.with_memory_space_constraint, memory_space=pltpu.HBM)
     to_a, to_b = pl.pallas_call(
         second_kernel,
         out_shape=(shape(1, height, width), shape(1, height, width)),
-        in_specs=[ANY, HBM] + [VM] * 12,
+        in_specs=[ANY, HBM, HBM] + [VM] * 16,
         out_specs=[VM] * 2,
         scratch_shapes=[
             pltpu.VMEM((bricks + 32, 128), f32),
@@ -590,14 +670,15 @@
             pltpu.VMEM((4, height + 16, width), f32),
             pltpu.VMEM((4, height, width), f32),
             pltpu.VMEM((4, height, width), f32),
-            pltpu.VMEM((2, height, width), f32),
             pltpu.SMEM((1,), f32),
-            pltpu.SemaphoreType.DMA((2,)),
+            pltpu.SemaphoreType.DMA((3,)),
         ],
         compiler_params=PARAMS,
         name="correct_and_smooth",
     )(
-        kappa, pltpu.with_memory_space_constraint(halo, pltpu.HBM), rhs, dens, s2, near_f, send_a, sib, near, far, sib_near, sib_far, gathered, block_group
+        kappa, in_hbm(halo_lo), in_hbm(halo_hi), rhs, dens, s2_lo, s2_hi, near_f, sib_f, density1_sib, density1_own, send_a,
+        sib, near, far, sib_near, sib_far,
+        gathered, block_group
     )
 
     halo_b = swap_b(to_b)

time: 81.2 us -> 77.6 us (0.956)
  waiting for transfers between devices: 18.9 us -> 17 us
  starting transfers between devices: 45.7 us -> 44.2 us
    ppermute x5, waiting for transfers between devices: 18.9 us -> 7.04 us  [swap_b(): return lax.ppermute(x, 'brick', next_chip)]
    ppermute x1, waiting for transfers between devices: 0.01 us -> 7.63 us  [swap_far(): return lax.ppermute(x, 'brick', second_chip)]
    ppermute x1, starting transfers between devices: 5.47 us -> 3.12 us  [swap_far(): return lax.ppermute(x, 'brick', second_chip)]
    ppermute x6 -> x7, waiting for transfers between devices: 0.02 us -> 2.35 us  [swap_a(): return lax.ppermute(x, 'brick', in_chip)]
    ppermute x5, starting transfers between devices: 23.2 us -> 25.4 us  [swap_b(): return lax.ppermute(x, 'brick', next_chip)]
    ppermute x6 -> x7, starting transfers between devices: 2.58 us -> 1.93 us  [swap_a(): return lax.ppermute(x, 'brick', in_chip)]
    pallas_call x2 -> x3, Pallas kernels: 5.56 us -> 5.62 us  [the longest x1 2.94 us: local(): pl.pallas_call(first_kernel, out_shape=(shape(2, height, width), pltpu.HB...]
  transfers between devices with their start and end apart: 16 -> 17, of which waited for: 5 -> 6; matrix products, arithmetic and copies ran while one was open for 0% -> 0% of each run, Pallas kernels for 4% -> 10%
where the time goes in v4:
time: 77.6 us; the launch traced here: 77.2 us
  starting transfers between devices  44.2 us (57%)
  waiting for transfers between devices  17 us (22%)
  Pallas kernels  14.3 us (18%)
  between operations  1.62 us (2%)
    ppermute x5, starting transfers between devices, swap_b(): return lax.ppermute(x, 'brick', next_chip)  25.4 us
    all_to_all x1, starting transfers between devices, local(): gathered = lax.all_to_all(payload, 'brick', 0, 0, tiled=True)  8.68 us
    ppermute x1, waiting for transfers between devices, swap_far(): return lax.ppermute(x, 'brick', second_chip)  7.63 us
    ppermute x5, waiting for transfers between devices, swap_b(): return lax.ppermute(x, 'brick', next_chip)  7.04 us
    pallas_call x1, Pallas kernels, local(): pl.pallas_call(second_kernel, out_shape=(shape(1, height, width), shape(1...  5.13 us
    ppermute x3, starting transfers between devices, around(): lax.ppermute(x, 'spec', [(i, (i + k) % species) for i in range(species)])  5.06 us
    ppermute x1, starting transfers between devices, swap_far(): return lax.ppermute(x, 'brick', second_chip)  3.12 us
    pallas_call x1, Pallas kernels, local(): pl.pallas_call(first_kernel, out_shape=(shape(2, height, width), pltpu.HB...  2.94 us
  transfers between devices with their start and end apart: 17, of which 6 were waited for; matrix products, arithmetic and copies ran while one was open for 0% of the time, Pallas kernels for 10%

profile of v4, /device:TPU:103, one launch (start us, length us, event | category | flops | bytes accessed | tf_op | source)
XLA Modules:
  0.0 77.2 jit_solution(5022511365367460816)
XLA Ops:
  0.6 0.0 copy-start
  0.6 1.4 %collective-permute-start = (f32[2,64,256]{2,1,0:T(8,128)}, f32[2,64,256]{2,1,0:T(8,128)S(1)}, u32[]{:S(2)}, u32[]{:S(2)}) collective-permute-start(f32[2,64,256]{2,1,0:T(8,128)} %shard.1), channel_id=1, source_target_pairs={{0,1},{1,2},{2,3},{3,0},{4,5},{5,6},{6,7},{7,4},{8,9},{9,10},{10,1... | collective-permute-start | bytes 393224 | tf_op jit(solution)/shard_map/ppermute | solution.py:573
  2.0 2.6 %collective-permute-start.1 = (f32[2,64,256]{2,1,0:T(8,128)}, f32[2,64,256]{2,1,0:T(8,128)S(1)}, u32[]{:S(2)}, u32[]{:S(2)}) collective-permute-start(f32[2,64,256]{2,1,0:T(8,128)} %shard.1), channel_id=1, source_target_pairs={{0,2},{1,3},{2,0},{3,1},{4,6},{5,7},{6,4},{7,5},{8,10},{9,11},{10,... | collective-permute-start | bytes 393224 | tf_op jit(solution)/shard_map/ppermute | solution.py:573
  4.6 1.1 %collective-permute-start.2 = (f32[2,64,256]{2,1,0:T(8,128)}, f32[2,64,256]{2,1,0:T(8,128)S(1)}, u32[]{:S(2)}, u32[]{:S(2)}) collective-permute-start(f32[2,64,256]{2,1,0:T(8,128)} %shard.1), channel_id=1, source_target_pairs={{0,3},{1,0},{2,1},{3,2},{4,7},{5,4},{6,5},{7,6},{8,11},{9,8},{10,9... | collective-permute-start | bytes 393224 | tf_op jit(solution)/shard_map/ppermute | solution.py:573
  5.7 6.1 %collective-permute-start.3 = (f32[1,2,256,256]{3,2,1,0:T(8,128)}, f32[1,2,256,256]{3,2,1,0:T(8,128)S(1)}, u32[]{:S(2)}, u32[]{:S(2)}) collective-permute-start(f32[1,2,256,256]{3,2,1,0:T(8,128)} %rhs.7), channel_id=1, source_target_pairs={{4,8},{8,4},{12,16},{16,12},{20,24},{24,20},{28,32},{32,28},{36,40... | collective-permute-start | bytes 1572872 | tf_op jit(solution)/shard_map/ppermute | solution.py:567
  11.8 0.1 collective-permute-start.5
  11.9 0.0 collective-permute-done.p1
  11.9 0.0 collective-permute-done.1.p2
  11.9 0.0 collective-permute-done.2.p3
  11.9 1.0 %collect_density.1.dens = f32[2,256,256]{2,1,0:T(8,128)S(1)} custom-call(f32[2,64,256]{2,1,0:T(8,128)} %shard.1, f32[2,64,256]{2,1,0:T(8,128)S(1)} %collective-permute-done.p1, f32[2,64,256]{2,1,0:T(8,128)S(1)} %collective-permute-done.1.p2, f32[2,64,256]{2,1,0:T(8,128)S(1)} %collective-permute-done.2.p3), custom_call_target="tpu_custom_call" | custom-call | tf_op jit(solution)/shard_map/collect_density/pallas_call | solution.py:578
  12.9 0.6 collective-permute-start.6
  13.4 4.3 %collective-permute-start.4 = (f32[2,256,256]{2,1,0:T(8,128)S(1)}, f32[2,256,256]{2,1,0:T(8,128)S(1)}, u32[]{:S(2)}, u32[]{:S(2)}) collective-permute-start(f32[2,256,256]{2,1,0:T(8,128)S(1)} %collect_density.1.dens), channel_id=1, source_target_pairs={{4,8},{8,4},{12,16},{16,12},{20,24},{24,20},{28,32},{32,28},{36,40... | collective-permute-start | bytes 1572872 | tf_op jit(solution)/shard_map/ppermute | solution.py:567
  18.4 1.4 %collective-permute-done.3.rhs_b = f32[1,2,256,256]{3,2,1,0:T(8,128)S(1)} collective-permute-done((f32[1,2,256,256]{3,2,1,0:T(8,128)}, f32[1,2,256,256]{3,2,1,0:T(8,128)S(1)}, u32[]{:S(2)}, u32[]{:S(2)}) %collective-permute-start.3) | collective-permute-done | bytes 524320 | tf_op jit(solution)/shard_map/ppermute | solution.py:567
  19.7 0.0 collective-permute-done.5.rhs_a
  19.7 0.0 collective-permute-done.6.dens_a
  19.7 0.0 copy-done
  19.7 1.3 %smooth_in_chip.1 = (f32[2,272,256]{2,1,0:T(8,128)S(1)}, f32[2,272,256]{2,1,0:T(8,128)S(1)}, f32[256,256]{1,0:T(8,128)S(1)}, f32[2,256,256]{2,1,0:T(8,128)}, f32...) custom-call(f32[1]{0:T(128)S(6)} %copy.7.kappa_in, f32[1,2,256,256]{3,2,1,0:T(8,128)S(1)} %copy-done, ...), custom_call_target="tpu_custom_call" | custom-call | tf_op jit(solution)/shard_map/smooth_in_chip/pallas_call | solution.py:590
  21.1 6.1 %collective-permute-start.7 = (f32[1,256,256]{2,1,0:T(8,128)S(1)}, f32[1,256,256]{2,1,0:T(8,128)S(1)}, u32[]{:S(2)}, u32[]{:S(2)}) collective-permute-start(f32[1,256,256]{2,1,0:T(8,128)S(1)} %get-tuple-element.31), channel_id=1, source_target_pairs={{4,8},{8,4},{12,16},{16,12},{20,24},{24,20},{28,32},{32,28},{36,40... | collective-permute-start | bytes 786440 | tf_op jit(solution)/shard_map/ppermute | solution.py:567
  27.1 0.1 collective-permute-done.4.dens_b
  27.2 2.9 %smooth_and_restrict.1 = (f32[2,256,256]{2,1,0:T(8,128)S(1)}, f32[2,256,256]{2,1,0:T(8,128)}, f32[256,128]{1,0:T(8,128)S(1)}, f32[1,256,256]{2,1,0:T(8,128)}, f32[64,8,128]{2,1,0:T(8,128)}) custom-call(f32[1]{0:T(128)S(6)} %copy.7.kappa_in, f32[1,2,256,256]{3,2,1,0:T(8,128)S(1)} %copy-done, f32[2,256,256]{2,1,0:T(8,128)S(1)} %collect_density.1.dens, ...), custom_call_target="tpu_custom_call" | custom-call | tf_op jit(solution)/shard_map/smooth_and_restrict/pallas_call | solution.py:614
  30.2 8.7 %all-to-all-start = ((f32[64,8,128]{2,1,0:T(8,128)}), f32[64,8,128]{2,1,0:T(8,128)S(1)}, u32[]{:S(2)}, u32[]{:S(2)}) async-start(f32[64,8,128]{2,1,0:T(8,128)} %get-tuple-element.36), calls=%async_computation | async-start | bytes 524288 | tf_op jit(solution)/shard_map/all_to_all | solution.py:637
  38.9 0.4 collective-permute-start.9
  39.3 1.0 %collective-permute-done.9.other.sib = f32[256,128]{1,0:T(8,128)S(1)} collective-permute-done((f32[256,128]{1,0:T(8,128)S(1)}, f32[256,128]{1,0:T(8,128)S(1)}, u32[]{:S(2)}, u32[]{:S(2)}) %collective-permute-start.9) | collective-permute-done | bytes 131104 | tf_op jit(solution)/shard_map/ppermute | solution.py:564
  40.3 0.0 collective-permute-done.7.near_f
  40.3 0.0 copy-start.1
  40.3 1.4 %join_chip.1 = (f32[512,128]{1,0:T(8,128)}, f32[384,128]{1,0:T(8,128)S(1)}) custom-call(f32[256,128]{1,0:T(8,128)S(1)} %get-tuple-element.33.mine.send_a, f32[256,128]{1,0:T(8,128)S(1)} %collective-permute-done.9.other.sib, f32[128,128]{1,0:T(8,128)S(1)} %get-tuple-element.27.density1_sib, f32[128,128]{1,0:T(8,128)S(1)} %get-tuple-element.26.density1_own, ...), custom_call_target="tpu_custom_call" | custom-call | tf_op jit(solution)/shard_map/join_chip/pallas_call | solution.py:640
  41.7 4.6 %collective-permute-start.10 = (f32[512,128]{1,0:T(8,128)}, f32[512,128]{1,0:T(8,128)S(1)}, u32[]{:S(2)}, u32[]{:S(2)}) collective-permute-start(f32[512,128]{1,0:T(8,128)} %get-tuple-element.34), channel_id=1, source_target_pairs={{4,8},{8,4},{12,16},{16,12},{20,24},{24,20},{28,32},{32,28},{36,40... | collective-permute-start | bytes 786440 | tf_op jit(solution)/shard_map/ppermute | solution.py:567
  46.3 3.1 %collective-permute-start.11 = (f32[384,128]{1,0:T(8,128)S(1)}, f32[384,128]{1,0:T(8,128)S(1)}, u32[]{:S(2)}, u32[]{:S(2)}) collective-permute-start(f32[384,128]{1,0:T(8,128)S(1)} %get-tuple-element.35), channel_id=1, source_target_pairs={{16,4},{24,12},{32,20},{40,28},{48,36},{56,44},{64,52},{72,60},{80... | collective-permute-start | bytes 589832 | tf_op jit(solution)/shard_map/ppermute | solution.py:570
  49.4 0.1 collective-permute-start.8
  49.5 7.6 %collective-permute-done.11.far = f32[384,128]{1,0:T(8,128)S(1)} collective-permute-done((f32[384,128]{1,0:T(8,128)S(1)}, f32[384,128]{1,0:T(8,128)S(1)}, u32[]{:S(2)}, u32[]{:S(2)}) %collective-permute-start.11) | collective-permute-done | bytes 196640 | tf_op jit(solution)/shard_map/ppermute | solution.py:570
  57.1 0.0 all-to-all-done.gathered
  57.1 0.0 collective-permute-done.10.near
  57.1 0.0 collective-permute-start.12
  57.1 0.5 collective-permute-start.13
  57.6 0.0 copy-done.1
  57.6 0.1 copy.6.groups
  57.7 0.0 collective-permute-done.8.sib_f
  57.7 1.3 %collective-permute-done.13.sib_far = f32[384,128]{1,0:T(8,128)} collective-permute-done((f32[384,128]{1,0:T(8,128)S(1)}, f32[384,128]{1,0:T(8,128)}, u32[]{:S(2)}, u32[]{:S(2)}) %collective-permute-start.13) | collective-permute-done | bytes 196640 | tf_op jit(solution)/shard_map/ppermute | solution.py:564
  59.1 0.0 collective-permute-done.12.sib_near
  59.1 5.1 %correct_and_smooth.1 = (f32[1,256,256]{2,1,0:T(8,128)S(1)}, f32[1,256,256]{2,1,0:T(8,128)S(1)}) custom-call(f32[1]{0:T(128)S(6)} %copy.7.kappa_in, f32[2,256,256]{2,1,0:T(8,128)} %get-tuple-element.28.halo_lo_in, f32[2,256,256]{2,1,0:T(8,128)} %get-tuple-element.29.halo_hi_in, f32[1,2,256,256]{3,2,1,0:T(8,128)S(1)} %copy-done, ...), custom_call_target="tpu_custom_call" | custom-call | tf_op jit(solution)/shard_map/correct_and_smooth/pallas_call | solution.py:656
  64.2 0.2 collective-permute-start.14
  64.4 4.4 %collective-permute-start.15 = (f32[1,256,256]{2,1,0:T(8,128)S(1)}, f32[1,256,256]{2,1,0:T(8,128)S(1)}, u32[]{:S(2)}, u32[]{:S(2)}) collective-permute-start(f32[1,256,256]{2,1,0:T(8,128)S(1)} %get-tuple-element.41.to_b), channel_id=1, source_target_pairs={{4,8},{8,4},{12,16},{16,12},{20,24},{24,20},{28,32},{32,28},{36,40... | collective-permute-start | bytes 786440 | tf_op jit(solution)/shard_map/ppermute | solution.py:567
  68.9 1.0 %residual_inside.1 = (f32[1,2,256,256]{3,2,1,0:T(8,128)}, f32[2,256,256]{2,1,0:T(8,128)S(1)}) custom-call(f32[1]{0:T(128)S(6)} %copy.7.kappa_in, f32[1,2,256,256]{3,2,1,0:T(8,128)S(1)} %copy-done, f32[2,256,256]{2,1,0:T(8,128)S(1)} %collect_density.1.dens, f32[1,256,256]{2,1,0:T(8,128)S(1)} %get-tuple-element.40.to_a, f32[1,256,256]{2,1,0:T(8,128)S(1)} %get-tuple-element.41.to_b), custom_call_target="tpu_custom_call" | custom-call | tf_op jit(solution)/shard_map/residual_inside/pallas_call | solution.py:686
  69.9 0.0 collective-permute-done.14.halo_a
  69.9 5.6 %collective-permute-done.15.halo_b = f32[1,256,256]{2,1,0:T(8,128)S(1)} collective-permute-done((f32[1,256,256]{2,1,0:T(8,128)S(1)}, f32[1,256,256]{2,1,0:T(8,128)S(1)}, u32[]{:S(2)}, u32[]{:S(2)}) %collective-permute-start.15) | collective-permute-done | bytes 262176 | tf_op jit(solution)/shard_map/ppermute | solution.py:567
  75.4 1.6 %residual.1 = f32[1,2,256,256]{3,2,1,0:T(8,128)} custom-call(f32[1]{0:T(128)S(6)} %copy.7.kappa_in, f32[2,256,256]{2,1,0:T(8,128)S(1)} %get-tuple-element.43.inside, f32[1,256,256]{2,1,0:T(8,128)S(1)} %collective-permute-done.14.halo_a, f32[1,256,256]{2,1,0:T(8,128)S(1)} %collective-permute-done.15.halo_b), custom_call_target="tpu_custom_call" | custom-call | tf_op jit(solution)/shard_map/residual/pallas_call | solution.py:699
Async XLA Ops:
  0.6 19.1 %copy-start = (f32[1,2,256,256]{3,2,1,0:T(8,128)S(1)}, f32[1,2,256,256]{3,2,1,0:T(8,128)}, u32[]{:S(2)}) copy-start(f32[1,2,256,256]{3,2,1,0:T(8,128)} %rhs.7) | copy-start | bytes 1572868
  0.6 11.2 %collective-permute-start = (f32[2,64,256]{2,1,0:T(8,128)}, f32[2,64,256]{2,1,0:T(8,128)S(1)}, u32[]{:S(2)}, u32[]{:S(2)}) collective-permute-start(f32[2,64,256]{2,1,0:T(8,128)} %shard.1), channel_id=1, source_target_pairs={{0,1},{1,2},{2,3},{3,0},{4,5},{5,6},{6,7},{7,4},{8,9},{9,10},{10,1... | collective-permute-start | bytes 393224 | tf_op jit(solution)/shard_map/ppermute | solution.py:573
  2.0 9.9 %collective-permute-start.1 = (f32[2,64,256]{2,1,0:T(8,128)}, f32[2,64,256]{2,1,0:T(8,128)S(1)}, u32[]{:S(2)}, u32[]{:S(2)}) collective-permute-start(f32[2,64,256]{2,1,0:T(8,128)} %shard.1), channel_id=1, source_target_pairs={{0,2},{1,3},{2,0},{3,1},{4,6},{5,7},{6,4},{7,5},{8,10},{9,11},{10,... | collective-permute-start | bytes 393224 | tf_op jit(solution)/shard_map/ppermute | solution.py:573
  4.6 7.3 %collective-permute-start.2 = (f32[2,64,256]{2,1,0:T(8,128)}, f32[2,64,256]{2,1,0:T(8,128)S(1)}, u32[]{:S(2)}, u32[]{:S(2)}) collective-permute-start(f32[2,64,256]{2,1,0:T(8,128)} %shard.1), channel_id=1, source_target_pairs={{0,3},{1,0},{2,1},{3,2},{4,7},{5,4},{6,5},{7,6},{8,11},{9,8},{10,9... | collective-permute-start | bytes 393224 | tf_op jit(solution)/shard_map/ppermute | solution.py:573
  5.7 14.0 %collective-permute-start.3 = (f32[1,2,256,256]{3,2,1,0:T(8,128)}, f32[1,2,256,256]{3,2,1,0:T(8,128)S(1)}, u32[]{:S(2)}, u32[]{:S(2)}) collective-permute-start(f32[1,2,256,256]{3,2,1,0:T(8,128)} %rhs.7), channel_id=1, source_target_pairs={{4,8},{8,4},{12,16},{16,12},{20,24},{24,20},{28,32},{32,28},{36,40... | collective-permute-start | bytes 1572872 | tf_op jit(solution)/shard_map/ppermute | solution.py:567
  11.8 8.0 %collective-permute-start.5 = (f32[1,2,256,256]{3,2,1,0:T(8,128)}, f32[1,2,256,256]{3,2,1,0:T(8,128)S(1)}, u32[]{:S(2)}, u32[]{:S(2)}) collective-permute-start(f32[1,2,256,256]{3,2,1,0:T(8,128)} %rhs.7), channel_id=1, source_target_pairs={{0,4},{4,0},{8,12},{12,8},{16,20},{20,16},{24,28},{28,24},{32,36},... | collective-permute-start | bytes 1572872 | tf_op jit(solution)/shard_map/ppermute | solution.py:564
  12.9 6.9 %collective-permute-start.6 = (f32[2,256,256]{2,1,0:T(8,128)S(1)}, f32[2,256,256]{2,1,0:T(8,128)S(1)}, u32[]{:S(2)}, u32[]{:S(2)}) collective-permute-start(f32[2,256,256]{2,1,0:T(8,128)S(1)} %collect_density.1.dens), channel_id=1, source_target_pairs={{0,4},{4,0},{8,12},{12,8},{16,20},{20,16},{24,28},{28,24},{32,36},... | collective-permute-start | bytes 1572872 | tf_op jit(solution)/shard_map/ppermute | solution.py:564
  13.4 13.8 %collective-permute-start.4 = (f32[2,256,256]{2,1,0:T(8,128)S(1)}, f32[2,256,256]{2,1,0:T(8,128)S(1)}, u32[]{:S(2)}, u32[]{:S(2)}) collective-permute-start(f32[2,256,256]{2,1,0:T(8,128)S(1)} %collect_density.1.dens), channel_id=1, source_target_pairs={{4,8},{8,4},{12,16},{16,12},{20,24},{24,20},{28,32},{32,28},{36,40... | collective-permute-start | bytes 1572872 | tf_op jit(solution)/shard_map/ppermute | solution.py:567
  21.1 19.3 %collective-permute-start.7 = (f32[1,256,256]{2,1,0:T(8,128)S(1)}, f32[1,256,256]{2,1,0:T(8,128)S(1)}, u32[]{:S(2)}, u32[]{:S(2)}) collective-permute-start(f32[1,256,256]{2,1,0:T(8,128)S(1)} %get-tuple-element.31), channel_id=1, source_target_pairs={{4,8},{8,4},{12,16},{16,12},{20,24},{24,20},{28,32},{32,28},{36,40... | collective-permute-start | bytes 786440 | tf_op jit(solution)/shard_map/ppermute | solution.py:567
  30.2 26.9 %all-to-all-start = ((f32[64,8,128]{2,1,0:T(8,128)}), f32[64,8,128]{2,1,0:T(8,128)S(1)}, u32[]{:S(2)}, u32[]{:S(2)}) async-start(f32[64,8,128]{2,1,0:T(8,128)} %get-tuple-element.36), calls=%async_computation | async-start | bytes 524288 | tf_op jit(solution)/shard_map/all_to_all | solution.py:637
  38.9 1.4 %collective-permute-start.9 = (f32[256,128]{1,0:T(8,128)S(1)}, f32[256,128]{1,0:T(8,128)S(1)}, u32[]{:S(2)}, u32[]{:S(2)}) collective-permute-start(f32[256,128]{1,0:T(8,128)S(1)} %get-tuple-element.33.mine.send_a), channel_id=1, source_target_pairs={{0,4},{4,0},{8,12},{12,8},{16,20},{20,16},{24,28},{28,24},{32,36},... | collective-permute-start | bytes 393224 | tf_op jit(solution)/shard_map/ppermute | solution.py:564
  40.3 17.3 %copy-start.1 = (s32[64,16]{0,1:T(8,128)S(1)}, s32[64,16]{0,1:T(8,128)}, u32[]{:S(2)}) copy-start(s32[64,16]{0,1:T(8,128)} %param.7) | copy-start | bytes 12292
  41.7 15.4 %collective-permute-start.10 = (f32[512,128]{1,0:T(8,128)}, f32[512,128]{1,0:T(8,128)S(1)}, u32[]{:S(2)}, u32[]{:S(2)}) collective-permute-start(f32[512,128]{1,0:T(8,128)} %get-tuple-element.34), channel_id=1, source_target_pairs={{4,8},{8,4},{12,16},{16,12},{20,24},{24,20},{28,32},{32,28},{36,40... | collective-permute-start | bytes 786440 | tf_op jit(solution)/shard_map/ppermute | solution.py:567
  46.3 10.9 %collective-permute-start.11 = (f32[384,128]{1,0:T(8,128)S(1)}, f32[384,128]{1,0:T(8,128)S(1)}, u32[]{:S(2)}, u32[]{:S(2)}) collective-permute-start(f32[384,128]{1,0:T(8,128)S(1)} %get-tuple-element.35), channel_id=1, source_target_pairs={{16,4},{24,12},{32,20},{40,28},{48,36},{56,44},{64,52},{72,60},{80... | collective-permute-start | bytes 589832 | tf_op jit(solution)/shard_map/ppermute | solution.py:570
  49.4 8.3 %collective-permute-start.8 = (f32[1,256,256]{2,1,0:T(8,128)}, f32[1,256,256]{2,1,0:T(8,128)}, u32[]{:S(2)}, u32[]{:S(2)}) collective-permute-start(f32[1,256,256]{2,1,0:T(8,128)} %get-tuple-element.32), channel_id=1, source_target_pairs={{0,4},{4,0},{8,12},{12,8},{16,20},{20,16},{24,28},{28,24},{32,36},... | collective-permute-start | bytes 786440 | tf_op jit(solution)/shard_map/ppermute | solution.py:564
  57.1 2.0 %collective-permute-start.12 = (f32[512,128]{1,0:T(8,128)S(1)}, f32[512,128]{1,0:T(8,128)}, u32[]{:S(2)}, u32[]{:S(2)}) collective-permute-start(f32[512,128]{1,0:T(8,128)S(1)} %collective-permute-done.10.near), channel_id=1, source_target_pairs={{0,4},{4,0},{8,12},{12,8},{16,20},{20,16},{24,28},{28,24},{32,36},... | collective-permute-start | bytes 786440 | tf_op jit(solution)/shard_map/ppermute | solution.py:564
  57.1 1.9 %collective-permute-start.13 = (f32[384,128]{1,0:T(8,128)S(1)}, f32[384,128]{1,0:T(8,128)}, u32[]{:S(2)}, u32[]{:S(2)}) collective-permute-start(f32[384,128]{1,0:T(8,128)S(1)} %collective-permute-done.11.far), channel_id=1, source_target_pairs={{0,4},{4,0},{8,12},{12,8},{16,20},{20,16},{24,28},{28,24},{32,36},... | collective-permute-start | bytes 589832 | tf_op jit(solution)/shard_map/ppermute | solution.py:564
  64.2 5.6 %collective-permute-start.14 = (f32[1,256,256]{2,1,0:T(8,128)S(1)}, f32[1,256,256]{2,1,0:T(8,128)S(1)}, u32[]{:S(2)}, u32[]{:S(2)}) collective-permute-start(f32[1,256,256]{2,1,0:T(8,128)S(1)} %get-tuple-element.40.to_a), channel_id=1, source_target_pairs={{0,4},{4,0},{8,12},{12,8},{16,20},{20,16},{24,28},{28,24},{32,36},... | collective-permute-start | bytes 786440 | tf_op jit(solution)/shard_map/ppermute | solution.py:564
  64.4 11.0 %collective-permute-start.15 = (f32[1,256,256]{2,1,0:T(8,128)S(1)}, f32[1,256,256]{2,1,0:T(8,128)S(1)}, u32[]{:S(2)}, u32[]{:S(2)}) collective-permute-start(f32[1,256,256]{2,1,0:T(8,128)S(1)} %get-tuple-element.41.to_b), channel_id=1, source_target_pairs={{4,8},{8,4},{12,16},{16,12},{20,24},{24,20},{28,32},{32,28},{36,40... | collective-permute-start | bytes 786440 | tf_op jit(solution)/shard_map/ppermute | solution.py:567

commit v5 on v4

--- a/solution.py
+++ b/solution.py
@@ -16,6 +16,7 @@
 bf16 = jnp.bfloat16
 VM = pl.BlockSpec(memory_space=pltpu.VMEM)
 ANY = pl.BlockSpec(memory_space=pl.ANY)
+SM = pl.BlockSpec(memory_space=pltpu.SMEM)
 HBM = pl.BlockSpec(memory_space=pltpu.HBM)
 PARAMS = pltpu.CompilerParams(vmem_limit_bytes=16 * 1024 * 1024)
 
@@ -99,33 +100,32 @@
         copy.wait()
 
 
-def join_kernel(mine, other, density1_sib, density1_own, near_f, near, far, sems):
+def join_kernel(mine, other, density1_sib, density1_own, near_f, near, far):
     del near_f
     half = far.shape[0] // 3
     parts = [pl.ds(i * half, half) for i in range(4)]
-    copies = [
-        pltpu.make_async_copy(mine.at[parts[0]], near.at[parts[0]], sems.at[0]),
-        pltpu.make_async_copy(density1_own, near.at[parts[1]], sems.at[1]),
-        pltpu.make_async_copy(other.at[parts[0]], near.at[parts[2]], sems.at[2]),
-        pltpu.make_async_copy(density1_sib, near.at[parts[3]], sems.at[3]),
-        pltpu.make_async_copy(mine.at[parts[0]], far.at[parts[0]], sems.at[4]),
-        pltpu.make_async_copy(density1_own, far.at[parts[1]], sems.at[5]),
-        pltpu.make_async_copy(other.at[parts[1]], far.at[parts[2]], sems.at[6]),
-    ]
-    start_all(copies)
-    wait_all(copies)
+    near[parts[0], :] = mine[parts[0], :]
+    near[parts[1], :] = density1_own[...]
+    near[parts[2], :] = other[parts[0], :]
+    near[parts[3], :] = density1_sib[...]
+    far[parts[0], :] = mine[parts[0], :]
+    far[parts[1], :] = density1_own[...]
+    far[parts[2], :] = other[parts[1], :]
 
 
 def gather_kernel(shard, p1, p2, p3, dens, sems):
     count = 4
     rows = shard.shape[1]
-    copies = []
-    for k, piece in enumerate((shard, p1, p2, p3)):
+
+    def place(k):
         owner = lax.rem(lax.axis_index("spec") - k + count, count)
-        place = pl.ds(pl.multiple_of(owner * rows, rows), rows)
-        copies.append(pltpu.make_async_copy(piece, dens.at[:, place, :], sems.at[k]))
-    start_all(copies)
-    wait_all(copies)
+        return pl.ds(pl.multiple_of(owner * rows, rows), rows)
+
+    own = pltpu.make_async_copy(shard, dens.at[:, place(0), :], sems.at[0])
+    own.start()
+    for k, piece in ((1, p1), (2, p2), (3, p3)):
+        dens[:, place(k), :] = piece[...]
+    own.wait()
 
 
 def begin_layers(source, density, layers, work, index, wd, s1, scale, top, keep):
@@ -145,24 +145,21 @@
 
 
 def near_kernel(
-    kappa_in, rhs, dens, rhs_a, dens_a, rhs_b,
+    kappa, rhs, dens, rhs_a, dens_a, rhs_b,
     s1_own, s2_hi, wd_own, halo_out, density1_own, density1_sib, send_b,
-    s1, wd, work, kappa, sems,
+    s1, wd, work, sems,
 ):
     del rhs_b
     core, brick, bricks = position()
-    load = pltpu.make_async_copy(kappa_in, kappa, sems.at[0])
     stores = [
         pltpu.make_async_copy(rhs_a.at[0, core], halo_out.at[0], sems.at[1]),
         pltpu.make_async_copy(dens_a.at[core], halo_out.at[1], sems.at[2]),
     ]
-    load.start()
     start_all(stores)
     height, width = dens.shape[1:]
     half = height // 2
     clear_edges(s1)
     clear_edges(s2_hi)
-    load.wait()
     scale = kappa[0]
     valid = jnp.where(core == 0, brick < bricks - 1, brick > 0).astype(f32)
     begin_layers(rhs, dens, ((core, 0), (1 - core, 1)), work, 0, wd, s1, scale, WEIGHT, {0: 0, 1: 1})
@@ -189,17 +186,15 @@
 
 
 def first_kernel(
-    kappa_in, rhs, dens, rhs_b, dens_b, s1_own, s2_hi, wd_own, density1_own, density1_sib,
+    kappa, rhs, dens, rhs_b, dens_b, s1_own, s2_hi, wd_own, density1_own, density1_sib,
     s2_lo, halo_out, send_a, send_f, payload,
-    s1, s2, wd, work, kappa, sems,
+    s1, s2, wd, work, sems,
 ):
     core, brick, bricks = position()
-    load = pltpu.make_async_copy(kappa_in, kappa, sems.at[0])
     stores = [
         pltpu.make_async_copy(rhs_b.at[0, 1 - core], halo_out.at[0], sems.at[1]),
         pltpu.make_async_copy(dens_b.at[1 - core], halo_out.at[1], sems.at[2]),
     ]
-    load.start()
     start_all(stores)
     height, width = dens.shape[1:]
     half = height // 2
@@ -207,7 +202,6 @@
     clear_edges(s2)
     s1[2:4] = s1_own[...]
     s2[2:4] = s2_hi[...]
-    load.wait()
     scale = kappa[0]
     scale1 = 0.25 * scale
     valid_lo = jnp.where(core == 0, brick > 0, brick < bricks - 1).astype(f32)
@@ -243,7 +237,8 @@
     coarse_res = 0.125 * dot_exact(pair_rows(work, 1, half), columns)
 
     send_a[0:half, :] = coarse_res
-    send_f[0] = s2_lo[1]
+    stores.append(pltpu.make_async_copy(s2.at[1, pl.ds(8, height), :], send_f.at[0], sems.at[0]))
+    stores[-1].start()
 
     first = WEIGHT * coarse_res / (density1[1] + 14.0 * scale1)
     send_a[half : 2 * half, :] = first
@@ -379,14 +374,32 @@
     return fix
 
 
+def solve_kernel(kappa, gathered, groups, spread, fixes):
+    core, brick, _ = position()
+    scale1 = 0.25 * kappa[0]
+    half = spread.shape[1] // TILES
+    block = half // TILES
+    fixes[0:8, :] = jnp.zeros((8, 128), f32)
+    count = gathered.shape[0]
+    fixes[8 + count : 32 + count, :] = jnp.zeros((24, 128), f32)
+    fixes[8 : 8 + count, :] = solve_groups(gathered[:, 0, :], groups[...], scale1, block)
+    window = fixes[pl.ds(brick + 4, 16), :]
+    turn = jnp.zeros_like(window)
+    row = iota(window.shape, 0)
+    for i in range(9):
+        turn = jnp.where(row == i, window[8 - i : 9 - i], turn)
+    window = jnp.where(core == 0, window, turn)
+    lane = iota((128, TILES * half), 1)
+    per = (lane >> (half.bit_length() - 1)) * 4 + ((lane & (half - 1)) >> (block.bit_length() - 1))
+    spread[...] = dot_exact(window, (iota((128, TILES * half), 0) == per).astype(bf16))
+
+
 def second_kernel(
-    kappa_in, halo_lo_in, halo_hi_in, rhs, dens, s2_lo, s2_hi, near_f, sib_f, density1_sib, density1_own, send_a, sib, near, far, sib_near, sib_far, gathered, groups,
+    kappa, halo_lo_in, halo_hi_in, rhs, dens, s2_lo, s2_hi, near_f, sib_f, density1_sib, density1_own, send_a, sib, near, far, sib_near, sib_far, spread,
     to_a, to_b,
-    fixes, cres, cden, c1, c2, c3, grown, s3, s4, wd, halo, kappa, sems,
+    cres, cden, c1, c2, c3, grown, s3, s4, wd, halo, sems,
 ):
     core, brick, bricks = position()
-    load = pltpu.make_async_copy(kappa_in, kappa, sems.at[0])
-    load.start()
     loads = [
         pltpu.make_async_copy(halo_lo_in, halo.at[pl.ds(0, 2)], sems.at[1]),
         pltpu.make_async_copy(halo_hi_in, halo.at[pl.ds(2, 2)], sems.at[2]),
@@ -397,18 +410,8 @@
     block = half // TILES
     for ref in (c1, c2, c3, s3, s4):
         clear_edges(ref)
-    load.wait()
     scale = kappa[0]
     scale1 = 0.25 * scale
-
-    fixes[0:8, :] = jnp.zeros((8, 128), f32)
-    count = gathered.shape[0]
-    fixes[8 + count : 32 + count, :] = jnp.zeros((24, 128), f32)
-    fixes[8 : 8 + count, :] = solve_groups(gathered[:, 0, :], groups[...], scale1, block)
-    window = fixes[pl.ds(brick + 4, 16), :]
-    lane = iota((128, TILES * half), 1)
-    per = (lane >> (half.bit_length() - 1)) * 4 + ((lane & (half - 1)) >> (block.bit_length() - 1))
-    spread = dot_exact(window, (iota((128, TILES * half), 0) == per).astype(bf16))
 
     for index, (ref, i), (ref_density, k) in (
         (1, (far, 0), (far, 1)),
@@ -439,7 +442,7 @@
 
     for i in range(7):
         value = relax(c1, i + 1, i + 1)
-        row = jnp.where(core == 0, spread[i + 1 : i + 2], spread[7 - i : 8 - i])
+        row = spread[i + 1 : i + 2, :]
         pieces = [jnp.broadcast_to(row[:, t * half : (t + 1) * half], (block, half)) for t in range(TILES)]
         c2[i, body, :] = value + jnp.concatenate(pieces, 0)
     for i in range(5):
@@ -494,21 +497,18 @@
         chunks(height, smooth_last)
 
 
-def inside_kernel(kappa_in, rhs, dens, to_a, to_b, sol_out, out, s, kappa, sems):
+def inside_kernel(kappa, rhs, dens, to_a, to_b, sol_out, out, s, sems):
     core = position()[0]
-    load = pltpu.make_async_copy(kappa_in, kappa, sems.at[0])
     stores = [
         pltpu.make_async_copy(to_b.at[0], sol_out.at[0, core], sems.at[1]),
         pltpu.make_async_copy(to_a.at[0], sol_out.at[0, 1 - core], sems.at[2]),
     ]
-    load.start()
     start_all(stores)
     height = dens.shape[1]
     inner = pl.ds(8, height)
     clear_edges(s)
     s[core, inner, :] = to_b[0]
     s[1 - core, inner, :] = to_a[0]
-    load.wait()
     scale = kappa[0]
     for j in range(2):
 
@@ -523,16 +523,13 @@
     wait_all(stores)
 
 
-def residual_kernel(kappa_in, inside, halo_a, halo_b, out, s, done, kappa, sems):
+def residual_kernel(kappa, inside, halo_a, halo_b, out, s, done, sems):
     core = position()[0]
-    load = pltpu.make_async_copy(kappa_in, kappa, sems.at[0])
-    load.start()
     height = inside.shape[1]
     inner = pl.ds(8, height)
     clear_edges(s)
     s[core, inner, :] = halo_b[0]
     s[1 - core, inner, :] = halo_a[0]
-    load.wait()
     scale = kappa[0]
     stores = []
     for j in range(2):
@@ -578,9 +575,9 @@
     dens = pl.pallas_call(
         gather_kernel,
         out_shape=shape(2, height, width),
-        in_specs=[HBM] + [ANY] * 3,
+        in_specs=[HBM] + [VM] * 3,
         out_specs=VM,
-        scratch_shapes=[pltpu.SemaphoreType.DMA((4,))],
+        scratch_shapes=[pltpu.SemaphoreType.DMA((1,))],
         compiler_params=PARAMS,
         name="collect_density",
     )(pltpu.with_memory_space_constraint(density, pltpu.HBM), *pieces)
@@ -598,13 +595,12 @@
             shape(half, half),
             shape(1, height, width),
         ),
-        in_specs=[ANY] + [VM] * 4 + [ANY],
+        in_specs=[SM] + [VM] * 4 + [ANY],
         out_specs=[VM, VM, VM, HBM, VM, VM, VM],
         scratch_shapes=[
             pltpu.VMEM((4, height + 16, width), f32),
             pltpu.VMEM((3, height, width), f32),
             pltpu.VMEM((2, 2, height, half), f32),
-            pltpu.SMEM((1,), f32),
             pltpu.SemaphoreType.DMA((3,)),
         ],
         compiler_params=PARAMS,
@@ -617,17 +613,16 @@
             shape(2, height, width),
             pltpu.HBM((2, height, width), f32),
             shape(2 * half, half),
-            shape(1, height, width),
-            shape(bricks, 8, 128),
+            pltpu.HBM((1, height, width), f32),
+            shape(bricks, 5, 128),
         ),
-        in_specs=[ANY] + [VM] * 9,
-        out_specs=[VM, HBM, VM, VM, VM],
+        in_specs=[SM] + [VM] * 9,
+        out_specs=[VM, HBM, VM, HBM, VM],
         scratch_shapes=[
             pltpu.VMEM((4, height + 16, width), f32),
             pltpu.VMEM((4, height + 16, width), f32),
             pltpu.VMEM((1, height, width), f32),
             pltpu.VMEM((2, 2, height, half), f32),
-            pltpu.SMEM((1,), f32),
             pltpu.SemaphoreType.DMA((3,)),
         ],
         compiler_params=PARAMS,
@@ -640,15 +635,24 @@
     near_out, far_out = pl.pallas_call(
         join_kernel,
         out_shape=(shape(4 * half, half), shape(3 * half, half)),
-        in_specs=[ANY] * 5,
+        in_specs=[VM] * 4 + [ANY],
         out_specs=[VM] * 2,
-        scratch_shapes=[pltpu.SemaphoreType.DMA((7,))],
         compiler_params=PARAMS,
         name="join_chip",
     )(send_a, sib, density1_sib, density1_own, near_f)
     near = swap_b(near_out)
     far = swap_far(far_out)
-    near, far, gathered = lax.optimization_barrier((near, far, gathered))
+    half_lanes = TILES * half
+    spread = pl.pallas_call(
+        solve_kernel,
+        out_shape=shape(16, half_lanes),
+        in_specs=[SM] + [VM] * 2,
+        out_specs=VM,
+        scratch_shapes=[pltpu.VMEM((bricks + 32, 128), f32)],
+        compiler_params=PARAMS,
+        name="solve_aggregates",
+    )(kappa, gathered, block_group)
+    near, far, spread = lax.optimization_barrier((near, far, spread))
     sib_near = swap_a(near)
     sib_far = swap_a(far)
 
@@ -656,10 +660,9 @@
     to_a, to_b = pl.pallas_call(
         second_kernel,
         out_shape=(shape(1, height, width), shape(1, height, width)),
-        in_specs=[ANY, HBM, HBM] + [VM] * 16,
+        in_specs=[SM, HBM, HBM] + [VM] * 15,
         out_specs=[VM] * 2,
         scratch_shapes=[
-            pltpu.VMEM((bricks + 32, 128), f32),
             pltpu.VMEM((9, half, half), f32),
             pltpu.VMEM((9, half, half), f32),
             pltpu.VMEM((9, half + 16, half), f32),
@@ -670,15 +673,13 @@
             pltpu.VMEM((4, height + 16, width), f32),
             pltpu.VMEM((4, height, width), f32),
             pltpu.VMEM((4, height, width), f32),
-            pltpu.SMEM((1,), f32),
             pltpu.SemaphoreType.DMA((3,)),
         ],
         compiler_params=PARAMS,
         name="correct_and_smooth",
     )(
         kappa, in_hbm(halo_lo), in_hbm(halo_hi), rhs, dens, s2_lo, s2_hi, near_f, sib_f, density1_sib, density1_own, send_a,
-        sib, near, far, sib_near, sib_far,
-        gathered, block_group
+        sib, near, far, sib_near, sib_far, spread
     )
 
     halo_b = swap_b(to_b)
@@ -686,11 +687,10 @@
     solution, inside = pl.pallas_call(
         inside_kernel,
         out_shape=(shape(1, 2, height, width), shape(2, height, width)),
-        in_specs=[ANY] + [VM] * 4,
+        in_specs=[SM] + [VM] * 4,
         out_specs=[ANY, VM],
         scratch_shapes=[
             pltpu.VMEM((2, height + 16, width), f32),
-            pltpu.SMEM((1,), f32),
             pltpu.SemaphoreType.DMA((3,)),
         ],
         compiler_params=PARAMS,
@@ -699,12 +699,11 @@
     residual = pl.pallas_call(
         residual_kernel,
         out_shape=shape(1, 2, height, width),
-        in_specs=[ANY] + [VM] * 3,
+        in_specs=[SM] + [VM] * 3,
         out_specs=ANY,
         scratch_shapes=[
             pltpu.VMEM((2, height + 16, width), f32),
             pltpu.VMEM((2, height, width), f32),
-            pltpu.SMEM((1,), f32),
             pltpu.SemaphoreType.DMA((3,)),
         ],
         compiler_params=PARAMS,

time: 77.6 us -> 74.8 us (0.964)
  waiting for transfers between devices: 17 us -> 14.3 us
    ppermute x1, waiting for transfers between devices: 7.63 us -> 5.77 us  [swap_far(): return lax.ppermute(x, 'brick', second_chip)]
    pallas_call x0 -> x1, Pallas kernels: none -> 1.43 us  [local(): pl.pallas_call(solve_kernel, out_shape=shape(16, half_lanes), in_specs=[S...]
    ppermute x7, waiting for transfers between devices: 2.35 us -> 1.32 us  [swap_a(): return lax.ppermute(x, 'brick', in_chip)]
  transfers between devices with their start and end apart: 17 -> 17, of which waited for: 6 -> 5; matrix products, arithmetic and copies ran while one was open for 0% -> 0% of each run, Pallas kernels for 10% -> 12%
where the time goes in v5:
time: 74.8 us; the launch traced here: 74.4 us
  starting transfers between devices  44.1 us (59%)
  waiting for transfers between devices  14.3 us (19%)
  Pallas kernels  14.3 us (19%)
  between operations  1.65 us (2%)
    ppermute x5, starting transfers between devices, swap_b(): return lax.ppermute(x, 'brick', next_chip)  25.3 us
    all_to_all x1, starting transfers between devices, local(): gathered = lax.all_to_all(payload, 'brick', 0, 0, tiled=True)  9.04 us
    ppermute x5, waiting for transfers between devices, swap_b(): return lax.ppermute(x, 'brick', next_chip)  6.75 us
    ppermute x1, waiting for transfers between devices, swap_far(): return lax.ppermute(x, 'brick', second_chip)  5.77 us
    ppermute x3, starting transfers between devices, around(): lax.ppermute(x, 'spec', [(i, (i + k) % species) for i in range(species)])  5.06 us
    pallas_call x1, Pallas kernels, local(): pl.pallas_call(second_kernel, out_shape=(shape(1, height, width), shape(1...  4.39 us
    ppermute x1, starting transfers between devices, swap_far(): return lax.ppermute(x, 'brick', second_chip)  3.12 us
    pallas_call x1, Pallas kernels, local(): pl.pallas_call(first_kernel, out_shape=(shape(2, height, width), pltpu.HB...  2.98 us
  transfers between devices with their start and end apart: 17, of which 5 were waited for; matrix products, arithmetic and copies ran while one was open for 0% of the time, Pallas kernels for 12%

profile of v5, /device:TPU:103, one launch (start us, length us, event | category | flops | bytes accessed | tf_op | source)
XLA Modules:
  0.0 74.4 jit_solution(5098894813527894714)
XLA Ops:
  0.6 0.0 copy-start
  0.6 1.4 %collective-permute-start = (f32[2,64,256]{2,1,0:T(8,128)}, f32[2,64,256]{2,1,0:T(8,128)S(1)}, u32[]{:S(2)}, u32[]{:S(2)}) collective-permute-start(f32[2,64,256]{2,1,0:T(8,128)} %shard.1), channel_id=1, source_target_pairs={{0,1},{1,2},{2,3},{3,0},{4,5},{5,6},{6,7},{7,4},{8,9},{9,10},{10,1... | collective-permute-start | bytes 393224 | tf_op jit(solution)/shard_map/ppermute | solution.py:570
  2.0 2.6 %collective-permute-start.1 = (f32[2,64,256]{2,1,0:T(8,128)}, f32[2,64,256]{2,1,0:T(8,128)S(1)}, u32[]{:S(2)}, u32[]{:S(2)}) collective-permute-start(f32[2,64,256]{2,1,0:T(8,128)} %shard.1), channel_id=1, source_target_pairs={{0,2},{1,3},{2,0},{3,1},{4,6},{5,7},{6,4},{7,5},{8,10},{9,11},{10,... | collective-permute-start | bytes 393224 | tf_op jit(solution)/shard_map/ppermute | solution.py:570
  4.6 1.1 %collective-permute-start.2 = (f32[2,64,256]{2,1,0:T(8,128)}, f32[2,64,256]{2,1,0:T(8,128)S(1)}, u32[]{:S(2)}, u32[]{:S(2)}) collective-permute-start(f32[2,64,256]{2,1,0:T(8,128)} %shard.1), channel_id=1, source_target_pairs={{0,3},{1,0},{2,1},{3,2},{4,7},{5,4},{6,5},{7,6},{8,11},{9,8},{10,9... | collective-permute-start | bytes 393224 | tf_op jit(solution)/shard_map/ppermute | solution.py:570
  5.7 6.1 %collective-permute-start.3 = (f32[1,2,256,256]{3,2,1,0:T(8,128)}, f32[1,2,256,256]{3,2,1,0:T(8,128)S(1)}, u32[]{:S(2)}, u32[]{:S(2)}) collective-permute-start(f32[1,2,256,256]{3,2,1,0:T(8,128)} %rhs.7), channel_id=1, source_target_pairs={{4,8},{8,4},{12,16},{16,12},{20,24},{24,20},{28,32},{32,28},{36,40... | collective-permute-start | bytes 1572872 | tf_op jit(solution)/shard_map/ppermute | solution.py:564
  11.8 0.1 collective-permute-start.5
  11.9 0.0 collective-permute-done.p1
  11.9 0.0 collective-permute-done.1.p2
  11.9 0.0 collective-permute-done.2.p3
  11.9 0.9 %collect_density.1.dens = f32[2,256,256]{2,1,0:T(8,128)S(1)} custom-call(f32[2,64,256]{2,1,0:T(8,128)} %shard.1, f32[2,64,256]{2,1,0:T(8,128)S(1)} %collective-permute-done.p1, f32[2,64,256]{2,1,0:T(8,128)S(1)} %collective-permute-done.1.p2, f32[2,64,256]{2,1,0:T(8,128)S(1)} %collective-permute-done.2.p3), custom_call_target="tpu_custom_call" | custom-call | tf_op jit(solution)/shard_map/collect_density/pallas_call | solution.py:575
  12.8 0.6 collective-permute-start.6
  13.4 4.3 %collective-permute-start.4 = (f32[2,256,256]{2,1,0:T(8,128)S(1)}, f32[2,256,256]{2,1,0:T(8,128)S(1)}, u32[]{:S(2)}, u32[]{:S(2)}) collective-permute-start(f32[2,256,256]{2,1,0:T(8,128)S(1)} %collect_density.1.dens), channel_id=1, source_target_pairs={{4,8},{8,4},{12,16},{16,12},{20,24},{24,20},{28,32},{32,28},{36,40... | collective-permute-start | bytes 1572872 | tf_op jit(solution)/shard_map/ppermute | solution.py:564
  18.3 1.4 %collective-permute-done.3.rhs_b = f32[1,2,256,256]{3,2,1,0:T(8,128)S(1)} collective-permute-done((f32[1,2,256,256]{3,2,1,0:T(8,128)}, f32[1,2,256,256]{3,2,1,0:T(8,128)S(1)}, u32[]{:S(2)}, u32[]{:S(2)}) %collective-permute-start.3) | collective-permute-done | bytes 524320 | tf_op jit(solution)/shard_map/ppermute | solution.py:564
  19.7 0.0 collective-permute-done.5.rhs_a
  19.7 0.0 collective-permute-done.6.dens_a
  19.7 0.0 copy-done
  19.7 1.4 %smooth_in_chip.1 = (f32[2,272,256]{2,1,0:T(8,128)S(1)}, f32[2,272,256]{2,1,0:T(8,128)S(1)}, f32[256,256]{1,0:T(8,128)S(1)}, f32[2,256,256]{2,1,0:T(8,128)}, f32...) custom-call(f32[1]{0:T(128)S(6)} %copy.7.kappa, f32[1,2,256,256]{3,2,1,0:T(8,128)S(1)} %copy-done, ...), custom_call_target="tpu_custom_call" | custom-call | tf_op jit(solution)/shard_map/smooth_in_chip/pallas_call | solution.py:587
  21.1 6.1 %collective-permute-start.7 = (f32[1,256,256]{2,1,0:T(8,128)S(1)}, f32[1,256,256]{2,1,0:T(8,128)S(1)}, u32[]{:S(2)}, u32[]{:S(2)}) collective-permute-start(f32[1,256,256]{2,1,0:T(8,128)S(1)} %get-tuple-element.31), channel_id=1, source_target_pairs={{4,8},{8,4},{12,16},{16,12},{20,24},{24,20},{28,32},{32,28},{36,40... | collective-permute-start | bytes 786440 | tf_op jit(solution)/shard_map/ppermute | solution.py:564
  27.2 0.0 collective-permute-done.4.dens_b
  27.2 3.0 %smooth_and_restrict.1 = (f32[2,256,256]{2,1,0:T(8,128)S(1)}, f32[2,256,256]{2,1,0:T(8,128)}, f32[256,128]{1,0:T(8,128)S(1)}, f32[1,256,256]{2,1,0:T(8,128)}, f32[64,5,128]{2,1,0:T(8,128)}) custom-call(f32[1]{0:T(128)S(6)} %copy.7.kappa, f32[1,2,256,256]{3,2,1,0:T(8,128)S(1)} %copy-done, f32[2,256,256]{2,1,0:T(8,128)S(1)} %collect_density.1.dens, ...), custom_call_target="tpu_custom_call" | custom-call | tf_op jit(solution)/shard_map/smooth_and_restrict/pallas_call | solution.py:610
  30.2 0.1 collective-permute-start.9
  30.3 9.0 %all-to-all-start = ((f32[64,5,128]{2,1,0:T(8,128)}), f32[64,5,128]{2,1,0:T(8,128)S(1)}, u32[]{:S(2)}, u32[]{:S(2)}) async-start(f32[64,5,128]{2,1,0:T(8,128)} %get-tuple-element.36), calls=%async_computation | async-start | bytes 524288 | tf_op jit(solution)/shard_map/all_to_all | solution.py:632
  39.4 0.0 collective-permute-done.9.other.sib
  39.4 0.0 collective-permute-done.7.near_f
  39.4 0.0 copy-start.1
  39.4 0.8 %join_chip.1 = (f32[512,128]{1,0:T(8,128)}, f32[384,128]{1,0:T(8,128)}) custom-call(f32[256,128]{1,0:T(8,128)S(1)} %get-tuple-element.33.mine.send_a, f32[256,128]{1,0:T(8,128)S(1)} %collective-permute-done.9.other.sib, f32[128,128]{1,0:T(8,128)S(1)} %get-tuple-element.27.density1_sib, f32[128,128]{1,0:T(8,128)S(1)} %get-tuple-element.26.density1_own, ...), custom_call_target="tpu_custom_call" | custom-call | tf_op jit(solution)/shard_map/join_chip/pallas_call | solution.py:635
  40.2 4.5 %collective-permute-start.10 = (f32[512,128]{1,0:T(8,128)}, f32[512,128]{1,0:T(8,128)S(1)}, u32[]{:S(2)}, u32[]{:S(2)}) collective-permute-start(f32[512,128]{1,0:T(8,128)} %get-tuple-element.34), channel_id=1, source_target_pairs={{4,8},{8,4},{12,16},{16,12},{20,24},{24,20},{28,32},{32,28},{36,40... | collective-permute-start | bytes 786440 | tf_op jit(solution)/shard_map/ppermute | solution.py:564
  44.8 3.1 %collective-permute-start.11 = (f32[384,128]{1,0:T(8,128)}, f32[384,128]{1,0:T(8,128)S(1)}, u32[]{:S(2)}, u32[]{:S(2)}) collective-permute-start(f32[384,128]{1,0:T(8,128)} %get-tuple-element.35), channel_id=1, source_target_pairs={{16,4},{24,12},{32,20},{40,28},{48,36},{56,44},{64,52},{72,60},{80... | collective-permute-start | bytes 589832 | tf_op jit(solution)/shard_map/ppermute | solution.py:567
  47.9 0.0 copy-done.1
  47.9 0.1 copy.6.groups
  48.0 0.1 collective-permute-start.8
  48.1 0.4 all-to-all-done.gathered
  48.5 1.4 %solve_aggregates.1.spread = f32[16,512]{1,0:T(8,128)S(1)} custom-call(f32[1]{0:T(128)S(6)} %copy.7.kappa, f32[64,5,128]{2,1,0:T(8,128)S(1)} %all-to-all-done.gathered, s32[64,16]{1,0:T(8,128)S(1)} %copy.6.groups), custom_call_target="tpu_custom_call" | custom-call | tf_op jit(solution)/shard_map/solve_aggregates/pallas_call | solution.py:646
  49.9 5.8 %collective-permute-done.11.far = f32[384,128]{1,0:T(8,128)S(1)} collective-permute-done((f32[384,128]{1,0:T(8,128)}, f32[384,128]{1,0:T(8,128)S(1)}, u32[]{:S(2)}, u32[]{:S(2)}) %collective-permute-start.11) | collective-permute-done | bytes 196640 | tf_op jit(solution)/shard_map/ppermute | solution.py:567
  55.7 0.0 collective-permute-done.10.near
  55.7 0.0 collective-permute-start.12
  55.7 0.5 collective-permute-start.13
  56.2 0.0 collective-permute-done.8.sib_f
  56.2 1.3 %collective-permute-done.13.sib_far = f32[384,128]{1,0:T(8,128)S(1)} collective-permute-done((f32[384,128]{1,0:T(8,128)S(1)}, f32[384,128]{1,0:T(8,128)S(1)}, u32[]{:S(2)}, u32[]{:S(2)}) %collective-permute-start.13) | collective-permute-done | bytes 196640 | tf_op jit(solution)/shard_map/ppermute | solution.py:561
  57.5 0.0 collective-permute-done.12.sib_near
  57.5 4.4 %correct_and_smooth.1 = (f32[1,256,256]{2,1,0:T(8,128)S(1)}, f32[1,256,256]{2,1,0:T(8,128)S(1)}) custom-call(f32[1]{0:T(128)S(6)} %copy.7.kappa, f32[2,256,256]{2,1,0:T(8,128)} %get-tuple-element.28.halo_lo_in, f32[2,256,256]{2,1,0:T(8,128)} %get-tuple-element.29.halo_hi_in, f32[1,2,256,256]{3,2,1,0:T(8,128)S(1)} %copy-done, ...), custom_call_target="tpu_custom_call" | custom-call | tf_op jit(solution)/shard_map/correct_and_smooth/pallas_call | solution.py:660
  61.9 0.2 collective-permute-start.14
  62.1 4.4 %collective-permute-start.15 = (f32[1,256,256]{2,1,0:T(8,128)S(1)}, f32[1,256,256]{2,1,0:T(8,128)S(1)}, u32[]{:S(2)}, u32[]{:S(2)}) collective-permute-start(f32[1,256,256]{2,1,0:T(8,128)S(1)} %get-tuple-element.41.to_b), channel_id=1, source_target_pairs={{4,8},{8,4},{12,16},{16,12},{20,24},{24,20},{28,32},{32,28},{36,40... | collective-permute-start | bytes 786440 | tf_op jit(solution)/shard_map/ppermute | solution.py:564
  66.5 1.2 %residual_inside.1 = (f32[1,2,256,256]{3,2,1,0:T(8,128)}, f32[2,256,256]{2,1,0:T(8,128)S(1)}) custom-call(f32[1]{0:T(128)S(6)} %copy.7.kappa, f32[1,2,256,256]{3,2,1,0:T(8,128)S(1)} %copy-done, f32[2,256,256]{2,1,0:T(8,128)S(1)} %collect_density.1.dens, f32[1,256,256]{2,1,0:T(8,128)S(1)} %get-tuple-element.40.to_a, f32[1,256,256]{2,1,0:T(8,128)S(1)} %get-tuple-element.41.to_b), custom_call_target="tpu_custom_call" | custom-call | tf_op jit(solution)/shard_map/residual_inside/pallas_call | solution.py:687
  67.7 0.0 collective-permute-done.14.halo_a
  67.8 5.4 %collective-permute-done.15.halo_b = f32[1,256,256]{2,1,0:T(8,128)S(1)} collective-permute-done((f32[1,256,256]{2,1,0:T(8,128)S(1)}, f32[1,256,256]{2,1,0:T(8,128)S(1)}, u32[]{:S(2)}, u32[]{:S(2)}) %collective-permute-start.15) | collective-permute-done | bytes 262176 | tf_op jit(solution)/shard_map/ppermute | solution.py:564
  73.1 1.1 %residual.1 = f32[1,2,256,256]{3,2,1,0:T(8,128)} custom-call(f32[1]{0:T(128)S(6)} %copy.7.kappa, f32[2,256,256]{2,1,0:T(8,128)S(1)} %get-tuple-element.43.inside, f32[1,256,256]{2,1,0:T(8,128)S(1)} %collective-permute-done.14.halo_a, f32[1,256,256]{2,1,0:T(8,128)S(1)} %collective-permute-done.15.halo_b), custom_call_target="tpu_custom_call" | custom-call | tf_op jit(solution)/shard_map/residual/pallas_call | solution.py:699
Async XLA Ops:
  0.6 19.1 %copy-start = (f32[1,2,256,256]{3,2,1,0:T(8,128)S(1)}, f32[1,2,256,256]{3,2,1,0:T(8,128)}, u32[]{:S(2)}) copy-start(f32[1,2,256,256]{3,2,1,0:T(8,128)} %rhs.7) | copy-start | bytes 1572868
  0.6 11.2 %collective-permute-start = (f32[2,64,256]{2,1,0:T(8,128)}, f32[2,64,256]{2,1,0:T(8,128)S(1)}, u32[]{:S(2)}, u32[]{:S(2)}) collective-permute-start(f32[2,64,256]{2,1,0:T(8,128)} %shard.1), channel_id=1, source_target_pairs={{0,1},{1,2},{2,3},{3,0},{4,5},{5,6},{6,7},{7,4},{8,9},{9,10},{10,1... | collective-permute-start | bytes 393224 | tf_op jit(solution)/shard_map/ppermute | solution.py:570
  2.0 9.9 %collective-permute-start.1 = (f32[2,64,256]{2,1,0:T(8,128)}, f32[2,64,256]{2,1,0:T(8,128)S(1)}, u32[]{:S(2)}, u32[]{:S(2)}) collective-permute-start(f32[2,64,256]{2,1,0:T(8,128)} %shard.1), channel_id=1, source_target_pairs={{0,2},{1,3},{2,0},{3,1},{4,6},{5,7},{6,4},{7,5},{8,10},{9,11},{10,... | collective-permute-start | bytes 393224 | tf_op jit(solution)/shard_map/ppermute | solution.py:570
  4.6 7.3 %collective-permute-start.2 = (f32[2,64,256]{2,1,0:T(8,128)}, f32[2,64,256]{2,1,0:T(8,128)S(1)}, u32[]{:S(2)}, u32[]{:S(2)}) collective-permute-start(f32[2,64,256]{2,1,0:T(8,128)} %shard.1), channel_id=1, source_target_pairs={{0,3},{1,0},{2,1},{3,2},{4,7},{5,4},{6,5},{7,6},{8,11},{9,8},{10,9... | collective-permute-start | bytes 393224 | tf_op jit(solution)/shard_map/ppermute | solution.py:570
  5.7 14.0 %collective-permute-start.3 = (f32[1,2,256,256]{3,2,1,0:T(8,128)}, f32[1,2,256,256]{3,2,1,0:T(8,128)S(1)}, u32[]{:S(2)}, u32[]{:S(2)}) collective-permute-start(f32[1,2,256,256]{3,2,1,0:T(8,128)} %rhs.7), channel_id=1, source_target_pairs={{4,8},{8,4},{12,16},{16,12},{20,24},{24,20},{28,32},{32,28},{36,40... | collective-permute-start | bytes 1572872 | tf_op jit(solution)/shard_map/ppermute | solution.py:564
  11.8 8.0 %collective-permute-start.5 = (f32[1,2,256,256]{3,2,1,0:T(8,128)}, f32[1,2,256,256]{3,2,1,0:T(8,128)S(1)}, u32[]{:S(2)}, u32[]{:S(2)}) collective-permute-start(f32[1,2,256,256]{3,2,1,0:T(8,128)} %rhs.7), channel_id=1, source_target_pairs={{0,4},{4,0},{8,12},{12,8},{16,20},{20,16},{24,28},{28,24},{32,36},... | collective-permute-start | bytes 1572872 | tf_op jit(solution)/shard_map/ppermute | solution.py:561
  12.8 6.9 %collective-permute-start.6 = (f32[2,256,256]{2,1,0:T(8,128)S(1)}, f32[2,256,256]{2,1,0:T(8,128)S(1)}, u32[]{:S(2)}, u32[]{:S(2)}) collective-permute-start(f32[2,256,256]{2,1,0:T(8,128)S(1)} %collect_density.1.dens), channel_id=1, source_target_pairs={{0,4},{4,0},{8,12},{12,8},{16,20},{20,16},{24,28},{28,24},{32,36},... | collective-permute-start | bytes 1572872 | tf_op jit(solution)/shard_map/ppermute | solution.py:561
  13.4 13.8 %collective-permute-start.4 = (f32[2,256,256]{2,1,0:T(8,128)S(1)}, f32[2,256,256]{2,1,0:T(8,128)S(1)}, u32[]{:S(2)}, u32[]{:S(2)}) collective-permute-start(f32[2,256,256]{2,1,0:T(8,128)S(1)} %collect_density.1.dens), channel_id=1, source_target_pairs={{4,8},{8,4},{12,16},{16,12},{20,24},{24,20},{28,32},{32,28},{36,40... | collective-permute-start | bytes 1572872 | tf_op jit(solution)/shard_map/ppermute | solution.py:564
  21.1 18.2 %collective-permute-start.7 = (f32[1,256,256]{2,1,0:T(8,128)S(1)}, f32[1,256,256]{2,1,0:T(8,128)S(1)}, u32[]{:S(2)}, u32[]{:S(2)}) collective-permute-start(f32[1,256,256]{2,1,0:T(8,128)S(1)} %get-tuple-element.31), channel_id=1, source_target_pairs={{4,8},{8,4},{12,16},{16,12},{20,24},{24,20},{28,32},{32,28},{36,40... | collective-permute-start | bytes 786440 | tf_op jit(solution)/shard_map/ppermute | solution.py:564
  30.2 9.1 %collective-permute-start.9 = (f32[256,128]{1,0:T(8,128)S(1)}, f32[256,128]{1,0:T(8,128)S(1)}, u32[]{:S(2)}, u32[]{:S(2)}) collective-permute-start(f32[256,128]{1,0:T(8,128)S(1)} %get-tuple-element.33.mine.send_a), channel_id=1, source_target_pairs={{0,4},{4,0},{8,12},{12,8},{16,20},{20,16},{24,28},{28,24},{32,36},... | collective-permute-start | bytes 393224 | tf_op jit(solution)/shard_map/ppermute | solution.py:561
  30.3 18.2 %all-to-all-start = ((f32[64,5,128]{2,1,0:T(8,128)}), f32[64,5,128]{2,1,0:T(8,128)S(1)}, u32[]{:S(2)}, u32[]{:S(2)}) async-start(f32[64,5,128]{2,1,0:T(8,128)} %get-tuple-element.36), calls=%async_computation | async-start | bytes 524288 | tf_op jit(solution)/shard_map/all_to_all | solution.py:632
  39.4 8.5 %copy-start.1 = (s32[64,16]{0,1:T(8,128)S(1)}, s32[64,16]{0,1:T(8,128)}, u32[]{:S(2)}) copy-start(s32[64,16]{0,1:T(8,128)} %param.7) | copy-start | bytes 12292
  40.2 15.5 %collective-permute-start.10 = (f32[512,128]{1,0:T(8,128)}, f32[512,128]{1,0:T(8,128)S(1)}, u32[]{:S(2)}, u32[]{:S(2)}) collective-permute-start(f32[512,128]{1,0:T(8,128)} %get-tuple-element.34), channel_id=1, source_target_pairs={{4,8},{8,4},{12,16},{16,12},{20,24},{24,20},{28,32},{32,28},{36,40... | collective-permute-start | bytes 786440 | tf_op jit(solution)/shard_map/ppermute | solution.py:564
  44.8 10.9 %collective-permute-start.11 = (f32[384,128]{1,0:T(8,128)}, f32[384,128]{1,0:T(8,128)S(1)}, u32[]{:S(2)}, u32[]{:S(2)}) collective-permute-start(f32[384,128]{1,0:T(8,128)} %get-tuple-element.35), channel_id=1, source_target_pairs={{16,4},{24,12},{32,20},{40,28},{48,36},{56,44},{64,52},{72,60},{80... | collective-permute-start | bytes 589832 | tf_op jit(solution)/shard_map/ppermute | solution.py:567
  48.0 8.2 %collective-permute-start.8 = (f32[1,256,256]{2,1,0:T(8,128)}, f32[1,256,256]{2,1,0:T(8,128)}, u32[]{:S(2)}, u32[]{:S(2)}) collective-permute-start(f32[1,256,256]{2,1,0:T(8,128)} %get-tuple-element.32), channel_id=1, source_target_pairs={{0,4},{4,0},{8,12},{12,8},{16,20},{20,16},{24,28},{28,24},{32,36},... | collective-permute-start | bytes 786440 | tf_op jit(solution)/shard_map/ppermute | solution.py:561
  55.7 1.8 %collective-permute-start.12 = (f32[512,128]{1,0:T(8,128)S(1)}, f32[512,128]{1,0:T(8,128)S(1)}, u32[]{:S(2)}, u32[]{:S(2)}) collective-permute-start(f32[512,128]{1,0:T(8,128)S(1)} %collective-permute-done.10.near), channel_id=1, source_target_pairs={{0,4},{4,0},{8,12},{12,8},{16,20},{20,16},{24,28},{28,24},{32,36},... | collective-permute-start | bytes 786440 | tf_op jit(solution)/shard_map/ppermute | solution.py:561
  55.7 1.8 %collective-permute-start.13 = (f32[384,128]{1,0:T(8,128)S(1)}, f32[384,128]{1,0:T(8,128)S(1)}, u32[]{:S(2)}, u32[]{:S(2)}) collective-permute-start(f32[384,128]{1,0:T(8,128)S(1)} %collective-permute-done.11.far), channel_id=1, source_target_pairs={{0,4},{4,0},{8,12},{12,8},{16,20},{20,16},{24,28},{28,24},{32,36},... | collective-permute-start | bytes 589832 | tf_op jit(solution)/shard_map/ppermute | solution.py:561
  61.9 5.8 %collective-permute-start.14 = (f32[1,256,256]{2,1,0:T(8,128)S(1)}, f32[1,256,256]{2,1,0:T(8,128)S(1)}, u32[]{:S(2)}, u32[]{:S(2)}) collective-permute-start(f32[1,256,256]{2,1,0:T(8,128)S(1)} %get-tuple-element.40.to_a), channel_id=1, source_target_pairs={{0,4},{4,0},{8,12},{12,8},{16,20},{20,16},{24,28},{28,24},{32,36},... | collective-permute-start | bytes 786440 | tf_op jit(solution)/shard_map/ppermute | solution.py:561
  62.1 11.0 %collective-permute-start.15 = (f32[1,256,256]{2,1,0:T(8,128)S(1)}, f32[1,256,256]{2,1,0:T(8,128)S(1)}, u32[]{:S(2)}, u32[]{:S(2)}) collective-permute-start(f32[1,256,256]{2,1,0:T(8,128)S(1)} %get-tuple-element.41.to_b), channel_id=1, source_target_pairs={{4,8},{8,4},{12,16},{16,12},{20,24},{24,20},{28,32},{32,28},{36,40... | collective-permute-start | bytes 786440 | tf_op jit(solution)/shard_map/ppermute | solution.py:564

commit v6 on v5

--- a/solution.py
+++ b/solution.py
@@ -396,8 +396,8 @@
 
 def second_kernel(
     kappa, halo_lo_in, halo_hi_in, rhs, dens, s2_lo, s2_hi, near_f, sib_f, density1_sib, density1_own, send_a, sib, near, far, sib_near, sib_far, spread,
-    to_a, to_b,
-    cres, cden, c1, c2, c3, grown, s3, s4, wd, halo, sems,
+    to_b, s4, wd_last,
+    cres, cden, c1, c2, c3, grown, s3, wd, halo, sems,
 ):
     core, brick, bricks = position()
     loads = [
@@ -485,42 +485,51 @@
             s4[j, pl.ds(row + 8, CHUNK), :] = new
 
         chunks(height, smooth)
-    for j, out in ((0, to_b), (1, to_a)):
-
-        def smooth_last(row, j=j, out=out):
-            part = pl.ds(row, CHUNK)
-            v = s4[j + 1, pl.ds(row + 8, CHUNK), :]
-            f = stencil(s4, j + 1, row, CHUNK)
-            source = rhs[0, core if j == 0 else 1 - core, part, :]
-            out[0, part, :] = (1.0 - WEIGHT) * v + wd[j + 1, part, :] * (source + 2.0 * scale * (f - v))
-
-        chunks(height, smooth_last)
-
-
-def inside_kernel(kappa, rhs, dens, to_a, to_b, sol_out, out, s, sems):
+    to_b[0, height : height + 8, :] = jnp.zeros((8, width), f32)
+
+    def smooth_last(row):
+        part = pl.ds(row, CHUNK)
+        v = s4[1, pl.ds(row + 8, CHUNK), :]
+        f = stencil(s4, 1, row, CHUNK)
+        to_b[0, part, :] = (1.0 - WEIGHT) * v + wd[1, part, :] * (rhs[0, core, part, :] + 2.0 * scale * (f - v))
+        wd_last[part, :] = wd[2, part, :]
+
+    chunks(height, smooth_last)
+
+
+def inside_kernel(kappa, rhs, dens, to_b, s4, wd, to_a, sol_out, out, s, sems):
     core = position()[0]
-    stores = [
-        pltpu.make_async_copy(to_b.at[0], sol_out.at[0, core], sems.at[1]),
-        pltpu.make_async_copy(to_a.at[0], sol_out.at[0, 1 - core], sems.at[2]),
-    ]
-    start_all(stores)
+    scale = kappa[0]
     height = dens.shape[1]
     inner = pl.ds(8, height)
+    store_b = pltpu.make_async_copy(to_b.at[0, pl.ds(0, height)], sol_out.at[0, core], sems.at[1])
+    store_b.start()
     clear_edges(s)
-    s[core, inner, :] = to_b[0]
-    s[1 - core, inner, :] = to_a[0]
-    scale = kappa[0]
-    for j in range(2):
-
-        def finish(row, j=j):
+    s[0, inner, :] = to_b[0, :height, :]
+
+    def smooth_last(row):
+        part = pl.ds(row, CHUNK)
+        v = s4[2, pl.ds(row + 8, CHUNK), :]
+        f = stencil(s4, 2, row, CHUNK)
+        new = (1.0 - WEIGHT) * v + wd[part, :] * (rhs[0, 1 - core, part, :] + 2.0 * scale * (f - v))
+        to_a[0, part, :] = new
+        s[1, pl.ds(row + 8, CHUNK), :] = new
+
+    chunks(height, smooth_last)
+    store_a = pltpu.make_async_copy(to_a.at[0], sol_out.at[0, 1 - core], sems.at[2])
+    store_a.start()
+    for j, layer in ((0, core), (1, 1 - core)):
+
+        def finish(row, j=j, layer=layer):
             part = pl.ds(row, CHUNK)
             more = pl.ds(row, CHUNK + 16)
             f = filter_yz(s[j, more, :] + 0.5 * s[1 - j, more, :])
-            center = dens[j, part, :] + 16.0 * scale
-            out[j, part, :] = rhs[0, j, part, :] - center * s[j, pl.ds(row + 8, CHUNK), :] + 2.0 * scale * f
+            center = dens[layer, part, :] + 16.0 * scale
+            out[layer, part, :] = rhs[0, layer, part, :] - center * s[j, pl.ds(row + 8, CHUNK), :] + 2.0 * scale * f
 
         chunks(height, finish)
-    wait_all(stores)
+    store_b.wait()
+    store_a.wait()
 
 
 def residual_kernel(kappa, inside, halo_a, halo_b, out, s, done, sems):
@@ -528,7 +537,7 @@
     height = inside.shape[1]
     inner = pl.ds(8, height)
     clear_edges(s)
-    s[core, inner, :] = halo_b[0]
+    s[core, inner, :] = halo_b[0, :height, :]
     s[1 - core, inner, :] = halo_a[0]
     scale = kappa[0]
     stores = []
@@ -657,11 +666,11 @@
     sib_far = swap_a(far)
 
     in_hbm = functools.partial(pltpu.with_memory_space_constraint, memory_space=pltpu.HBM)
-    to_a, to_b = pl.pallas_call(
+    to_b, s4, wd_last = pl.pallas_call(
         second_kernel,
-        out_shape=(shape(1, height, width), shape(1, height, width)),
+        out_shape=(shape(1, height + 8, width), shape(4, height + 16, width), shape(height, width)),
         in_specs=[SM, HBM, HBM] + [VM] * 15,
-        out_specs=[VM] * 2,
+        out_specs=[VM] * 3,
         scratch_shapes=[
             pltpu.VMEM((9, half, half), f32),
             pltpu.VMEM((9, half, half), f32),
@@ -670,7 +679,6 @@
             pltpu.VMEM((5, half + 16, half), f32),
             pltpu.VMEM((3, 2, height, half), f32),
             pltpu.VMEM((6, height + 16, width), f32),
-            pltpu.VMEM((4, height + 16, width), f32),
             pltpu.VMEM((4, height, width), f32),
             pltpu.VMEM((4, height, width), f32),
             pltpu.SemaphoreType.DMA((3,)),
@@ -683,19 +691,19 @@
     )
 
     halo_b = swap_b(to_b)
-    halo_a = swap_a(to_a)
-    solution, inside = pl.pallas_call(
+    to_a, solution, inside = pl.pallas_call(
         inside_kernel,
-        out_shape=(shape(1, 2, height, width), shape(2, height, width)),
-        in_specs=[SM] + [VM] * 4,
-        out_specs=[ANY, VM],
+        out_shape=(shape(1, height, width), shape(1, 2, height, width), shape(2, height, width)),
+        in_specs=[SM] + [VM] * 5,
+        out_specs=[VM, ANY, VM],
         scratch_shapes=[
             pltpu.VMEM((2, height + 16, width), f32),
             pltpu.SemaphoreType.DMA((3,)),
         ],
         compiler_params=PARAMS,
         name="residual_inside",
-    )(kappa, rhs, dens, to_a, to_b)
+    )(kappa, rhs, dens, to_b, s4, wd_last)
+    halo_a = swap_a(to_a)
     residual = pl.pallas_call(
         residual_kernel,
         out_shape=shape(1, 2, height, width),

time: 74.8 us -> 74.9 us (level)
  waiting for transfers between devices: 14.3 us -> 16.2 us
  starting transfers between devices: 44.1 us -> 42.5 us
    ppermute x5, starting transfers between devices: 25.3 us -> 22.4 us  [swap_b(): return lax.ppermute(x, 'brick', next_chip)]
    ppermute x7, waiting for transfers between devices: 1.32 us -> 2.84 us  [swap_a(): return lax.ppermute(x, 'brick', in_chip)]
    ppermute x7, starting transfers between devices: 1.54 us -> 2.36 us  [swap_a(): return lax.ppermute(x, 'brick', in_chip)]
  transfers between devices with their start and end apart: 17 -> 17, of which waited for: 5 -> 6; matrix products, arithmetic and copies ran while one was open for 0% -> 0% of each run, Pallas kernels for 12% -> 12%
where the time goes in v6:
time: 74.9 us; the launch traced here: 74.5 us
  starting transfers between devices  42.5 us (57%)
  waiting for transfers between devices  16.2 us (22%)
  Pallas kernels  14.2 us (19%)
  between operations  1.49 us (2%)
    ppermute x5, starting transfers between devices, swap_b(): return lax.ppermute(x, 'brick', next_chip)  22.4 us
    all_to_all x1, starting transfers between devices, local(): gathered = lax.all_to_all(payload, 'brick', 0, 0, tiled=True)  8.97 us
    ppermute x5, waiting for transfers between devices, swap_b(): return lax.ppermute(x, 'brick', next_chip)  7.14 us
    ppermute x1, waiting for transfers between devices, swap_far(): return lax.ppermute(x, 'brick', second_chip)  5.76 us
    ppermute x3, starting transfers between devices, around(): lax.ppermute(x, 'spec', [(i, (i + k) % species) for i in range(species)])  5.68 us
    pallas_call x1, Pallas kernels, local(): pl.pallas_call(second_kernel, out_shape=(shape(1, height + 8, width), sha...  4.21 us
    ppermute x1, starting transfers between devices, swap_far(): return lax.ppermute(x, 'brick', second_chip)  3.12 us
    pallas_call x1, Pallas kernels, local(): pl.pallas_call(first_kernel, out_shape=(shape(2, height, width), pltpu.HB...  2.99 us
  transfers between devices with their start and end apart: 17, of which 6 were waited for; matrix products, arithmetic and copies ran while one was open for 0% of the time, Pallas kernels for 12%

profile of v6, /device:TPU:103, one launch (start us, length us, event | category | flops | bytes accessed | tf_op | source)
XLA Modules:
  0.0 74.5 jit_solution(16260109366855582668)
XLA Ops:
  0.6 0.0 copy-start
  0.6 3.0 %collective-permute-start.1 = (f32[2,64,256]{2,1,0:T(8,128)}, f32[2,64,256]{2,1,0:T(8,128)S(1)}, u32[]{:S(2)}, u32[]{:S(2)}) collective-permute-start(f32[2,64,256]{2,1,0:T(8,128)} %shard.1), channel_id=1, source_target_pairs={{0,2},{1,3},{2,0},{3,1},{4,6},{5,7},{6,4},{7,5},{8,10},{9,11},{10,... | collective-permute-start | bytes 393224 | tf_op jit(solution)/shard_map/ppermute | solution.py:579
  3.6 0.4 collective-permute-start
  4.0 2.3 %collective-permute-start.2 = (f32[2,64,256]{2,1,0:T(8,128)}, f32[2,64,256]{2,1,0:T(8,128)S(1)}, u32[]{:S(2)}, u32[]{:S(2)}) collective-permute-start(f32[2,64,256]{2,1,0:T(8,128)} %shard.1), channel_id=1, source_target_pairs={{0,3},{1,0},{2,1},{3,2},{4,7},{5,4},{6,5},{7,6},{8,11},{9,8},{10,9... | collective-permute-start | bytes 393224 | tf_op jit(solution)/shard_map/ppermute | solution.py:579
  6.3 1.5 %collective-permute-start.5 = (f32[1,2,256,256]{3,2,1,0:T(8,128)}, f32[1,2,256,256]{3,2,1,0:T(8,128)S(1)}, u32[]{:S(2)}, u32[]{:S(2)}) collective-permute-start(f32[1,2,256,256]{3,2,1,0:T(8,128)} %rhs.7), channel_id=1, source_target_pairs={{0,4},{4,0},{8,12},{12,8},{16,20},{20,16},{24,28},{28,24},{32,36},... | collective-permute-start | bytes 1572872 | tf_op jit(solution)/shard_map/ppermute | solution.py:570
  7.8 4.5 %collective-permute-start.3 = (f32[1,2,256,256]{3,2,1,0:T(8,128)}, f32[1,2,256,256]{3,2,1,0:T(8,128)S(1)}, u32[]{:S(2)}, u32[]{:S(2)}) collective-permute-start(f32[1,2,256,256]{3,2,1,0:T(8,128)} %rhs.7), channel_id=1, source_target_pairs={{4,8},{8,4},{12,16},{16,12},{20,24},{24,20},{28,32},{32,28},{36,40... | collective-permute-start | bytes 1572872 | tf_op jit(solution)/shard_map/ppermute | solution.py:573
  12.4 0.0 collective-permute-done.1.p2
  12.4 0.0 collective-permute-done.p1
  12.4 0.0 collective-permute-done.2.p3
  12.4 0.9 %collect_density.1.dens = f32[2,256,256]{2,1,0:T(8,128)S(1)} custom-call(f32[2,64,256]{2,1,0:T(8,128)} %shard.1, f32[2,64,256]{2,1,0:T(8,128)S(1)} %collective-permute-done.p1, f32[2,64,256]{2,1,0:T(8,128)S(1)} %collective-permute-done.1.p2, f32[2,64,256]{2,1,0:T(8,128)S(1)} %collective-permute-done.2.p3), custom_call_target="tpu_custom_call" | custom-call | tf_op jit(solution)/shard_map/collect_density/pallas_call | solution.py:584
  13.4 0.1 collective-permute-start.6
  13.5 4.3 %collective-permute-start.4 = (f32[2,256,256]{2,1,0:T(8,128)S(1)}, f32[2,256,256]{2,1,0:T(8,128)S(1)}, u32[]{:S(2)}, u32[]{:S(2)}) collective-permute-start(f32[2,256,256]{2,1,0:T(8,128)S(1)} %collect_density.1.dens), channel_id=1, source_target_pairs={{4,8},{8,4},{12,16},{16,12},{20,24},{24,20},{28,32},{32,28},{36,40... | collective-permute-start | bytes 1572872 | tf_op jit(solution)/shard_map/ppermute | solution.py:573
  18.4 0.0 collective-permute-done.5.rhs_a
  18.4 3.4 %collective-permute-done.3.rhs_b = f32[1,2,256,256]{3,2,1,0:T(8,128)S(1)} collective-permute-done((f32[1,2,256,256]{3,2,1,0:T(8,128)}, f32[1,2,256,256]{3,2,1,0:T(8,128)S(1)}, u32[]{:S(2)}, u32[]{:S(2)}) %collective-permute-start.3) | collective-permute-done | bytes 524320 | tf_op jit(solution)/shard_map/ppermute | solution.py:573
  21.9 0.0 collective-permute-done.6.dens_a
  21.9 0.0 copy-done
  21.9 1.4 %smooth_in_chip.1 = (f32[2,272,256]{2,1,0:T(8,128)S(1)}, f32[2,272,256]{2,1,0:T(8,128)S(1)}, f32[256,256]{1,0:T(8,128)S(1)}, f32[2,256,256]{2,1,0:T(8,128)}, f32...) custom-call(f32[1]{0:T(128)S(6)} %copy.7.kappa, f32[1,2,256,256]{3,2,1,0:T(8,128)S(1)} %copy-done, ...), custom_call_target="tpu_custom_call" | custom-call | tf_op jit(solution)/shard_map/smooth_in_chip/pallas_call | solution.py:596
  23.2 4.6 %collective-permute-start.7 = (f32[1,256,256]{2,1,0:T(8,128)S(1)}, f32[1,256,256]{2,1,0:T(8,128)S(1)}, u32[]{:S(2)}, u32[]{:S(2)}) collective-permute-start(f32[1,256,256]{2,1,0:T(8,128)S(1)} %get-tuple-element.33), channel_id=1, source_target_pairs={{4,8},{8,4},{12,16},{16,12},{20,24},{24,20},{28,32},{32,28},{36,40... | collective-permute-start | bytes 786440 | tf_op jit(solution)/shard_map/ppermute | solution.py:573
  27.8 0.0 collective-permute-done.4.dens_b
  27.8 3.0 %smooth_and_restrict.1 = (f32[2,256,256]{2,1,0:T(8,128)S(1)}, f32[2,256,256]{2,1,0:T(8,128)}, f32[256,128]{1,0:T(8,128)S(1)}, f32[1,256,256]{2,1,0:T(8,128)}, f32[64,5,128]{2,1,0:T(8,128)}) custom-call(f32[1]{0:T(128)S(6)} %copy.7.kappa, f32[1,2,256,256]{3,2,1,0:T(8,128)S(1)} %copy-done, f32[2,256,256]{2,1,0:T(8,128)S(1)} %collect_density.1.dens, ...), custom_call_target="tpu_custom_call" | custom-call | tf_op jit(solution)/shard_map/smooth_and_restrict/pallas_call | solution.py:619
  30.8 0.0 copy-start.1
  30.8 0.1 collective-permute-start.9
  30.9 9.0 %all-to-all-start = ((f32[64,5,128]{2,1,0:T(8,128)}), f32[64,5,128]{2,1,0:T(8,128)S(1)}, u32[]{:S(2)}, u32[]{:S(2)}) async-start(f32[64,5,128]{2,1,0:T(8,128)} %get-tuple-element.38), calls=%async_computation | async-start | bytes 524288 | tf_op jit(solution)/shard_map/all_to_all | solution.py:641
  39.9 0.0 collective-permute-done.9.other.sib
  39.9 0.0 collective-permute-done.7.near_f
  39.9 0.8 %join_chip.1 = (f32[512,128]{1,0:T(8,128)}, f32[384,128]{1,0:T(8,128)}) custom-call(f32[256,128]{1,0:T(8,128)S(1)} %get-tuple-element.35.mine.send_a, f32[256,128]{1,0:T(8,128)S(1)} %collective-permute-done.9.other.sib, f32[128,128]{1,0:T(8,128)S(1)} %get-tuple-element.29.density1_sib, f32[128,128]{1,0:T(8,128)S(1)} %get-tuple-element.28.density1_own, ...), custom_call_target="tpu_custom_call" | custom-call | tf_op jit(solution)/shard_map/join_chip/pallas_call | solution.py:644
  40.8 4.5 %collective-permute-start.10 = (f32[512,128]{1,0:T(8,128)}, f32[512,128]{1,0:T(8,128)S(1)}, u32[]{:S(2)}, u32[]{:S(2)}) collective-permute-start(f32[512,128]{1,0:T(8,128)} %get-tuple-element.36), channel_id=1, source_target_pairs={{4,8},{8,4},{12,16},{16,12},{20,24},{24,20},{28,32},{32,28},{36,40... | collective-permute-start | bytes 786440 | tf_op jit(solution)/shard_map/ppermute | solution.py:573
  45.3 3.1 %collective-permute-start.11 = (f32[384,128]{1,0:T(8,128)}, f32[384,128]{1,0:T(8,128)S(1)}, u32[]{:S(2)}, u32[]{:S(2)}) collective-permute-start(f32[384,128]{1,0:T(8,128)} %get-tuple-element.37), channel_id=1, source_target_pairs={{16,4},{24,12},{32,20},{40,28},{48,36},{56,44},{64,52},{72,60},{80... | collective-permute-start | bytes 589832 | tf_op jit(solution)/shard_map/ppermute | solution.py:576
  48.4 0.0 copy-done.1
  48.4 0.1 copy.6.groups
  48.5 0.1 collective-permute-start.8
  48.6 0.4 all-to-all-done.gathered
  49.0 1.4 %solve_aggregates.1.spread = f32[16,512]{1,0:T(8,128)S(1)} custom-call(f32[1]{0:T(128)S(6)} %copy.7.kappa, f32[64,5,128]{2,1,0:T(8,128)S(1)} %all-to-all-done.gathered, s32[64,16]{1,0:T(8,128)S(1)} %copy.6.groups), custom_call_target="tpu_custom_call" | custom-call | tf_op jit(solution)/shard_map/solve_aggregates/pallas_call | solution.py:655
  50.5 5.8 %collective-permute-done.11.far = f32[384,128]{1,0:T(8,128)S(1)} collective-permute-done((f32[384,128]{1,0:T(8,128)}, f32[384,128]{1,0:T(8,128)S(1)}, u32[]{:S(2)}, u32[]{:S(2)}) %collective-permute-start.11) | collective-permute-done | bytes 196640 | tf_op jit(solution)/shard_map/ppermute | solution.py:576
  56.2 0.0 collective-permute-done.10.near
  56.2 0.0 collective-permute-start.12
  56.2 0.5 collective-permute-start.13
  56.7 0.0 collective-permute-done.8.sib_f
  56.7 1.3 %collective-permute-done.13.sib_far = f32[384,128]{1,0:T(8,128)S(1)} collective-permute-done((f32[384,128]{1,0:T(8,128)S(1)}, f32[384,128]{1,0:T(8,128)S(1)}, u32[]{:S(2)}, u32[]{:S(2)}) %collective-permute-start.13) | collective-permute-done | bytes 196640 | tf_op jit(solution)/shard_map/ppermute | solution.py:570
  58.0 0.0 collective-permute-done.12.sib_near
  58.0 4.2 %correct_and_smooth.1 = (f32[1,264,256]{2,1,0:T(8,128)S(1)}, f32[4,272,256]{2,1,0:T(8,128)S(1)}, f32[256,256]{1,0:T(8,128)S(1)}) custom-call(f32[1]{0:T(128)S(6)} %copy.7.kappa, f32[2,256,256]{2,1,0:T(8,128)} %get-tuple-element.30.halo_lo_in, f32[2,256,256]{2,1,0:T(8,128)} %get-tuple-element.31.halo_hi_in, f32[1,2,256,256]{3,2,1,0:T(8,128)S(1)} %copy-done, ...), custom_call_target="tpu_custom_call" | custom-call | tf_op jit(solution)/shard_map/correct_and_smooth/pallas_call | solution.py:669
  62.3 4.4 %collective-permute-start.15 = (f32[1,264,256]{2,1,0:T(8,128)S(1)}, f32[1,264,256]{2,1,0:T(8,128)S(1)}, u32[]{:S(2)}, u32[]{:S(2)}) collective-permute-start(f32[1,264,256]{2,1,0:T(8,128)S(1)} %get-tuple-element.42.to_b), channel_id=1, source_target_pairs={{4,8},{8,4},{12,16},{16,12},{20,24},{24,20},{28,32},{32,28},{36,40... | collective-permute-start | bytes 811016 | tf_op jit(solution)/shard_map/ppermute | solution.py:573
  66.7 1.4 %residual_inside.1 = (f32[1,256,256]{2,1,0:T(8,128)S(1)}, f32[1,2,256,256]{3,2,1,0:T(8,128)}, f32[2,256,256]{2,1,0:T(8,128)S(1)}) custom-call(f32[1]{0:T(128)S(6)} %copy.7.kappa, f32[1,2,256,256]{3,2,1,0:T(8,128)S(1)} %copy-done, f32[2,256,256]{2,1,0:T(8,128)S(1)} %collect_density.1.dens, f32[1,264,256]{2,1,0:T(8,128)S(1)} %get-tuple-element.42.to_b, ...), custom_call_target="tpu_custom_call" | custom-call | tf_op jit(solution)/shard_map/residual_inside/pallas_call | solution.py:694
  68.0 0.1 collective-permute-start.14
  68.1 1.5 %collective-permute-done.14.halo_a = f32[1,256,256]{2,1,0:T(8,128)S(1)} collective-permute-done((f32[1,256,256]{2,1,0:T(8,128)S(1)}, f32[1,256,256]{2,1,0:T(8,128)S(1)}, u32[]{:S(2)}, u32[]{:S(2)}) %collective-permute-start.14) | collective-permute-done | bytes 262176 | tf_op jit(solution)/shard_map/ppermute | solution.py:570
  69.6 3.7 %collective-permute-done.15.halo_b = f32[1,264,256]{2,1,0:T(8,128)S(1)} collective-permute-done((f32[1,264,256]{2,1,0:T(8,128)S(1)}, f32[1,264,256]{2,1,0:T(8,128)S(1)}, u32[]{:S(2)}, u32[]{:S(2)}) %collective-permute-start.15) | collective-permute-done | bytes 270368 | tf_op jit(solution)/shard_map/ppermute | solution.py:573
  73.4 1.1 %residual.1 = f32[1,2,256,256]{3,2,1,0:T(8,128)} custom-call(f32[1]{0:T(128)S(6)} %copy.7.kappa, f32[2,256,256]{2,1,0:T(8,128)S(1)} %get-tuple-element.46.inside, f32[1,256,256]{2,1,0:T(8,128)S(1)} %collective-permute-done.14.halo_a, f32[1,264,256]{2,1,0:T(8,128)S(1)} %collective-permute-done.15.halo_b), custom_call_target="tpu_custom_call" | custom-call | tf_op jit(solution)/shard_map/residual/pallas_call | solution.py:707
Async XLA Ops:
  0.6 21.2 %copy-start = (f32[1,2,256,256]{3,2,1,0:T(8,128)S(1)}, f32[1,2,256,256]{3,2,1,0:T(8,128)}, u32[]{:S(2)}) copy-start(f32[1,2,256,256]{3,2,1,0:T(8,128)} %rhs.7) | copy-start | bytes 1572868
  0.6 11.8 %collective-permute-start.1 = (f32[2,64,256]{2,1,0:T(8,128)}, f32[2,64,256]{2,1,0:T(8,128)S(1)}, u32[]{:S(2)}, u32[]{:S(2)}) collective-permute-start(f32[2,64,256]{2,1,0:T(8,128)} %shard.1), channel_id=1, source_target_pairs={{0,2},{1,3},{2,0},{3,1},{4,6},{5,7},{6,4},{7,5},{8,10},{9,11},{10,... | collective-permute-start | bytes 393224 | tf_op jit(solution)/shard_map/ppermute | solution.py:579
  3.6 8.8 %collective-permute-start = (f32[2,64,256]{2,1,0:T(8,128)}, f32[2,64,256]{2,1,0:T(8,128)S(1)}, u32[]{:S(2)}, u32[]{:S(2)}) collective-permute-start(f32[2,64,256]{2,1,0:T(8,128)} %shard.1), channel_id=1, source_target_pairs={{0,1},{1,2},{2,3},{3,0},{4,5},{5,6},{6,7},{7,4},{8,9},{9,10},{10,1... | collective-permute-start | bytes 393224 | tf_op jit(solution)/shard_map/ppermute | solution.py:579
  4.0 8.4 %collective-permute-start.2 = (f32[2,64,256]{2,1,0:T(8,128)}, f32[2,64,256]{2,1,0:T(8,128)S(1)}, u32[]{:S(2)}, u32[]{:S(2)}) collective-permute-start(f32[2,64,256]{2,1,0:T(8,128)} %shard.1), channel_id=1, source_target_pairs={{0,3},{1,0},{2,1},{3,2},{4,7},{5,4},{6,5},{7,6},{8,11},{9,8},{10,9... | collective-permute-start | bytes 393224 | tf_op jit(solution)/shard_map/ppermute | solution.py:579
  6.3 12.1 %collective-permute-start.5 = (f32[1,2,256,256]{3,2,1,0:T(8,128)}, f32[1,2,256,256]{3,2,1,0:T(8,128)S(1)}, u32[]{:S(2)}, u32[]{:S(2)}) collective-permute-start(f32[1,2,256,256]{3,2,1,0:T(8,128)} %rhs.7), channel_id=1, source_target_pairs={{0,4},{4,0},{8,12},{12,8},{16,20},{20,16},{24,28},{28,24},{32,36},... | collective-permute-start | bytes 1572872 | tf_op jit(solution)/shard_map/ppermute | solution.py:570
  7.8 14.0 %collective-permute-start.3 = (f32[1,2,256,256]{3,2,1,0:T(8,128)}, f32[1,2,256,256]{3,2,1,0:T(8,128)S(1)}, u32[]{:S(2)}, u32[]{:S(2)}) collective-permute-start(f32[1,2,256,256]{3,2,1,0:T(8,128)} %rhs.7), channel_id=1, source_target_pairs={{4,8},{8,4},{12,16},{16,12},{20,24},{24,20},{28,32},{32,28},{36,40... | collective-permute-start | bytes 1572872 | tf_op jit(solution)/shard_map/ppermute | solution.py:573
  13.4 8.5 %collective-permute-start.6 = (f32[2,256,256]{2,1,0:T(8,128)S(1)}, f32[2,256,256]{2,1,0:T(8,128)S(1)}, u32[]{:S(2)}, u32[]{:S(2)}) collective-permute-start(f32[2,256,256]{2,1,0:T(8,128)S(1)} %collect_density.1.dens), channel_id=1, source_target_pairs={{0,4},{4,0},{8,12},{12,8},{16,20},{20,16},{24,28},{28,24},{32,36},... | collective-permute-start | bytes 1572872 | tf_op jit(solution)/shard_map/ppermute | solution.py:570
  13.5 14.4 %collective-permute-start.4 = (f32[2,256,256]{2,1,0:T(8,128)S(1)}, f32[2,256,256]{2,1,0:T(8,128)S(1)}, u32[]{:S(2)}, u32[]{:S(2)}) collective-permute-start(f32[2,256,256]{2,1,0:T(8,128)S(1)} %collect_density.1.dens), channel_id=1, source_target_pairs={{4,8},{8,4},{12,16},{16,12},{20,24},{24,20},{28,32},{32,28},{36,40... | collective-permute-start | bytes 1572872 | tf_op jit(solution)/shard_map/ppermute | solution.py:573
  23.2 16.7 %collective-permute-start.7 = (f32[1,256,256]{2,1,0:T(8,128)S(1)}, f32[1,256,256]{2,1,0:T(8,128)S(1)}, u32[]{:S(2)}, u32[]{:S(2)}) collective-permute-start(f32[1,256,256]{2,1,0:T(8,128)S(1)} %get-tuple-element.33), channel_id=1, source_target_pairs={{4,8},{8,4},{12,16},{16,12},{20,24},{24,20},{28,32},{32,28},{36,40... | collective-permute-start | bytes 786440 | tf_op jit(solution)/shard_map/ppermute | solution.py:573
  30.8 17.6 %copy-start.1 = (s32[64,16]{0,1:T(8,128)S(1)}, s32[64,16]{0,1:T(8,128)}, u32[]{:S(2)}) copy-start(s32[64,16]{0,1:T(8,128)} %param.7) | copy-start | bytes 12292
  30.8 9.1 %collective-permute-start.9 = (f32[256,128]{1,0:T(8,128)S(1)}, f32[256,128]{1,0:T(8,128)S(1)}, u32[]{:S(2)}, u32[]{:S(2)}) collective-permute-start(f32[256,128]{1,0:T(8,128)S(1)} %get-tuple-element.35.mine.send_a), channel_id=1, source_target_pairs={{0,4},{4,0},{8,12},{12,8},{16,20},{20,16},{24,28},{28,24},{32,36},... | collective-permute-start | bytes 393224 | tf_op jit(solution)/shard_map/ppermute | solution.py:570
  30.9 18.1 %all-to-all-start = ((f32[64,5,128]{2,1,0:T(8,128)}), f32[64,5,128]{2,1,0:T(8,128)S(1)}, u32[]{:S(2)}, u32[]{:S(2)}) async-start(f32[64,5,128]{2,1,0:T(8,128)} %get-tuple-element.38), calls=%async_computation | async-start | bytes 524288 | tf_op jit(solution)/shard_map/all_to_all | solution.py:641
  40.8 15.5 %collective-permute-start.10 = (f32[512,128]{1,0:T(8,128)}, f32[512,128]{1,0:T(8,128)S(1)}, u32[]{:S(2)}, u32[]{:S(2)}) collective-permute-start(f32[512,128]{1,0:T(8,128)} %get-tuple-element.36), channel_id=1, source_target_pairs={{4,8},{8,4},{12,16},{16,12},{20,24},{24,20},{28,32},{32,28},{36,40... | collective-permute-start | bytes 786440 | tf_op jit(solution)/shard_map/ppermute | solution.py:573
  45.3 10.9 %collective-permute-start.11 = (f32[384,128]{1,0:T(8,128)}, f32[384,128]{1,0:T(8,128)S(1)}, u32[]{:S(2)}, u32[]{:S(2)}) collective-permute-start(f32[384,128]{1,0:T(8,128)} %get-tuple-element.37), channel_id=1, source_target_pairs={{16,4},{24,12},{32,20},{40,28},{48,36},{56,44},{64,52},{72,60},{80... | collective-permute-start | bytes 589832 | tf_op jit(solution)/shard_map/ppermute | solution.py:576
  48.5 8.2 %collective-permute-start.8 = (f32[1,256,256]{2,1,0:T(8,128)}, f32[1,256,256]{2,1,0:T(8,128)}, u32[]{:S(2)}, u32[]{:S(2)}) collective-permute-start(f32[1,256,256]{2,1,0:T(8,128)} %get-tuple-element.34), channel_id=1, source_target_pairs={{0,4},{4,0},{8,12},{12,8},{16,20},{20,16},{24,28},{28,24},{32,36},... | collective-permute-start | bytes 786440 | tf_op jit(solution)/shard_map/ppermute | solution.py:570
  56.2 1.8 %collective-permute-start.12 = (f32[512,128]{1,0:T(8,128)S(1)}, f32[512,128]{1,0:T(8,128)S(1)}, u32[]{:S(2)}, u32[]{:S(2)}) collective-permute-start(f32[512,128]{1,0:T(8,128)S(1)} %collective-permute-done.10.near), channel_id=1, source_target_pairs={{0,4},{4,0},{8,12},{12,8},{16,20},{20,16},{24,28},{28,24},{32,36},... | collective-permute-start | bytes 786440 | tf_op jit(solution)/shard_map/ppermute | solution.py:570
  56.2 1.8 %collective-permute-start.13 = (f32[384,128]{1,0:T(8,128)S(1)}, f32[384,128]{1,0:T(8,128)S(1)}, u32[]{:S(2)}, u32[]{:S(2)}) collective-permute-start(f32[384,128]{1,0:T(8,128)S(1)} %collective-permute-done.11.far), channel_id=1, source_target_pairs={{0,4},{4,0},{8,12},{12,8},{16,20},{20,16},{24,28},{28,24},{32,36},... | collective-permute-start | bytes 589832 | tf_op jit(solution)/shard_map/ppermute | solution.py:570
  62.3 11.1 %collective-permute-start.15 = (f32[1,264,256]{2,1,0:T(8,128)S(1)}, f32[1,264,256]{2,1,0:T(8,128)S(1)}, u32[]{:S(2)}, u32[]{:S(2)}) collective-permute-start(f32[1,264,256]{2,1,0:T(8,128)S(1)} %get-tuple-element.42.to_b), channel_id=1, source_target_pairs={{4,8},{8,4},{12,16},{16,12},{20,24},{24,20},{28,32},{32,28},{36,40... | collective-permute-start | bytes 811016 | tf_op jit(solution)/shard_map/ppermute | solution.py:573
  68.0 1.6 %collective-permute-start.14 = (f32[1,256,256]{2,1,0:T(8,128)S(1)}, f32[1,256,256]{2,1,0:T(8,128)S(1)}, u32[]{:S(2)}, u32[]{:S(2)}) collective-permute-start(f32[1,256,256]{2,1,0:T(8,128)S(1)} %get-tuple-element.47), channel_id=1, source_target_pairs={{0,4},{4,0},{8,12},{12,8},{16,20},{20,16},{24,28},{28,24},{32,36},... | collective-permute-start | bytes 786440 | tf_op jit(solution)/shard_map/ppermute | solution.py:570

commit v7 on v6

--- a/solution.py
+++ b/solution.py
@@ -102,12 +102,11 @@
 
 def join_kernel(mine, other, density1_sib, density1_own, near_f, near, far):
     del near_f
-    half = far.shape[0] // 3
+    half = near.shape[0] // 3
     parts = [pl.ds(i * half, half) for i in range(4)]
     near[parts[0], :] = mine[parts[0], :]
-    near[parts[1], :] = density1_own[...]
-    near[parts[2], :] = other[parts[0], :]
-    near[parts[3], :] = density1_sib[...]
+    near[parts[1], :] = other[parts[0], :]
+    near[parts[2], :] = density1_sib[...]
     far[parts[0], :] = mine[parts[0], :]
     far[parts[1], :] = density1_own[...]
     far[parts[2], :] = other[parts[1], :]
@@ -242,6 +241,7 @@
 
     first = WEIGHT * coarse_res / (density1[1] + 14.0 * scale1)
     send_a[half : 2 * half, :] = first
+    send_a[2 * half : 3 * half, :] = density1[0]
     pad = jnp.zeros((8, half), f32)
     spread = filter_yz(jnp.concatenate([pad, first, pad], 0))
     own_factor = WEIGHT / (density1[1] + 14.0 * scale1)
@@ -415,12 +415,12 @@
 
     for index, (ref, i), (ref_density, k) in (
         (1, (far, 0), (far, 1)),
-        (2, (near, 2), (near, 3)),
-        (3, (near, 0), (near, 1)),
+        (2, (near, 1), (near, 2)),
+        (3, (near, 0), (send_a, 2)),
         (4, (send_a, 0), (density1_own, 0)),
         (5, (sib, 0), (density1_sib, 0)),
-        (6, (sib_near, 0), (sib_near, 1)),
-        (7, (sib_near, 2), (sib_near, 3)),
+        (6, (sib_near, 0), (sib, 2)),
+        (7, (sib_near, 1), (sib_near, 2)),
         (8, (sib_far, 0), (sib_far, 1)),
     ):
         cres[index] = ref[i * half : (i + 1) * half, :]
@@ -621,7 +621,7 @@
         out_shape=(
             shape(2, height, width),
             pltpu.HBM((2, height, width), f32),
-            shape(2 * half, half),
+            shape(3 * half, half),
             pltpu.HBM((1, height, width), f32),
             shape(bricks, 5, 128),
         ),
@@ -643,7 +643,7 @@
     sib_f = swap_a(send_f)
     near_out, far_out = pl.pallas_call(
         join_kernel,
-        out_shape=(shape(4 * half, half), shape(3 * half, half)),
+        out_shape=(shape(3 * half, half), shape(3 * half, half)),
         in_specs=[VM] * 4 + [ANY],
         out_specs=[VM] * 2,
         compiler_params=PARAMS,

time: 74.9 us -> 75 us (level)
    ppermute x5, waiting for transfers between devices: 7.14 us -> 9.44 us  [swap_b(): return lax.ppermute(x, 'brick', next_chip)]
    ppermute x1, waiting for transfers between devices: 5.76 us -> 3.49 us  [swap_far(): return lax.ppermute(x, 'brick', second_chip)]
  transfers between devices with their start and end apart: 17 -> 17, of which waited for: 6 -> 8; matrix products, arithmetic and copies ran while one was open for 0% -> 0% of each run, Pallas kernels for 12% -> 12%
where the time goes in v7:
time: 75 us; the launch traced here: 74.6 us
  starting transfers between devices  42.5 us (57%)
  waiting for transfers between devices  16.3 us (22%)
  Pallas kernels  14.3 us (19%)
  between operations  1.49 us (2%)
    ppermute x5, starting transfers between devices, swap_b(): return lax.ppermute(x, 'brick', next_chip)  22.3 us
    ppermute x5, waiting for transfers between devices, swap_b(): return lax.ppermute(x, 'brick', next_chip)  9.44 us
    all_to_all x1, starting transfers between devices, local(): gathered = lax.all_to_all(payload, 'brick', 0, 0, tiled=True)  8.97 us
    ppermute x3, starting transfers between devices, around(): lax.ppermute(x, 'spec', [(i, (i + k) % species) for i in range(species)])  5.68 us
    pallas_call x1, Pallas kernels, local(): pl.pallas_call(second_kernel, out_shape=(shape(1, height + 8, width), sha...  4.28 us
    ppermute x1, waiting for transfers between devices, swap_far(): return lax.ppermute(x, 'brick', second_chip)  3.49 us
    ppermute x1, starting transfers between devices, swap_far(): return lax.ppermute(x, 'brick', second_chip)  3.13 us
    pallas_call x1, Pallas kernels, local(): pl.pallas_call(first_kernel, out_shape=(shape(2, height, width), pltpu.HB...  2.99 us
  transfers between devices with their start and end apart: 17, of which 8 were waited for; matrix products, arithmetic and copies ran while one was open for 0% of the time, Pallas kernels for 12%

profile of v7, /device:TPU:103, one launch (start us, length us, event | category | flops | bytes accessed | tf_op | source)
XLA Modules:
  0.0 74.6 jit_solution(873211199683773210)
XLA Ops:
  0.6 0.0 copy-start
  0.6 3.0 %collective-permute-start.1 = (f32[2,64,256]{2,1,0:T(8,128)}, f32[2,64,256]{2,1,0:T(8,128)S(1)}, u32[]{:S(2)}, u32[]{:S(2)}) collective-permute-start(f32[2,64,256]{2,1,0:T(8,128)} %shard.1), channel_id=1, source_target_pairs={{0,2},{1,3},{2,0},{3,1},{4,6},{5,7},{6,4},{7,5},{8,10},{9,11},{10,... | collective-permute-start | bytes 393224 | tf_op jit(solution)/shard_map/ppermute | solution.py:579
  3.6 0.4 collective-permute-start
  4.0 2.3 %collective-permute-start.2 = (f32[2,64,256]{2,1,0:T(8,128)}, f32[2,64,256]{2,1,0:T(8,128)S(1)}, u32[]{:S(2)}, u32[]{:S(2)}) collective-permute-start(f32[2,64,256]{2,1,0:T(8,128)} %shard.1), channel_id=1, source_target_pairs={{0,3},{1,0},{2,1},{3,2},{4,7},{5,4},{6,5},{7,6},{8,11},{9,8},{10,9... | collective-permute-start | bytes 393224 | tf_op jit(solution)/shard_map/ppermute | solution.py:579
  6.3 1.5 %collective-permute-start.5 = (f32[1,2,256,256]{3,2,1,0:T(8,128)}, f32[1,2,256,256]{3,2,1,0:T(8,128)S(1)}, u32[]{:S(2)}, u32[]{:S(2)}) collective-permute-start(f32[1,2,256,256]{3,2,1,0:T(8,128)} %rhs.7), channel_id=1, source_target_pairs={{0,4},{4,0},{8,12},{12,8},{16,20},{20,16},{24,28},{28,24},{32,36},... | collective-permute-start | bytes 1572872 | tf_op jit(solution)/shard_map/ppermute | solution.py:570
  7.8 4.5 %collective-permute-start.3 = (f32[1,2,256,256]{3,2,1,0:T(8,128)}, f32[1,2,256,256]{3,2,1,0:T(8,128)S(1)}, u32[]{:S(2)}, u32[]{:S(2)}) collective-permute-start(f32[1,2,256,256]{3,2,1,0:T(8,128)} %rhs.7), channel_id=1, source_target_pairs={{4,8},{8,4},{12,16},{16,12},{20,24},{24,20},{28,32},{32,28},{36,40... | collective-permute-start | bytes 1572872 | tf_op jit(solution)/shard_map/ppermute | solution.py:573
  12.4 0.0 collective-permute-done.1.p2
  12.4 0.0 collective-permute-done.p1
  12.4 0.0 collective-permute-done.2.p3
  12.4 0.9 %collect_density.1.dens = f32[2,256,256]{2,1,0:T(8,128)S(1)} custom-call(f32[2,64,256]{2,1,0:T(8,128)} %shard.1, f32[2,64,256]{2,1,0:T(8,128)S(1)} %collective-permute-done.p1, f32[2,64,256]{2,1,0:T(8,128)S(1)} %collective-permute-done.1.p2, f32[2,64,256]{2,1,0:T(8,128)S(1)} %collective-permute-done.2.p3), custom_call_target="tpu_custom_call" | custom-call | tf_op jit(solution)/shard_map/collect_density/pallas_call | solution.py:584
  13.4 0.1 collective-permute-start.6
  13.5 4.3 %collective-permute-start.4 = (f32[2,256,256]{2,1,0:T(8,128)S(1)}, f32[2,256,256]{2,1,0:T(8,128)S(1)}, u32[]{:S(2)}, u32[]{:S(2)}) collective-permute-start(f32[2,256,256]{2,1,0:T(8,128)S(1)} %collect_density.1.dens), channel_id=1, source_target_pairs={{4,8},{8,4},{12,16},{16,12},{20,24},{24,20},{28,32},{32,28},{36,40... | collective-permute-start | bytes 1572872 | tf_op jit(solution)/shard_map/ppermute | solution.py:573
  18.4 0.0 collective-permute-done.5.rhs_a
  18.4 3.4 %collective-permute-done.3.rhs_b = f32[1,2,256,256]{3,2,1,0:T(8,128)S(1)} collective-permute-done((f32[1,2,256,256]{3,2,1,0:T(8,128)}, f32[1,2,256,256]{3,2,1,0:T(8,128)S(1)}, u32[]{:S(2)}, u32[]{:S(2)}) %collective-permute-start.3) | collective-permute-done | bytes 524320 | tf_op jit(solution)/shard_map/ppermute | solution.py:573
  21.9 0.0 collective-permute-done.6.dens_a
  21.9 0.0 copy-done
  21.9 1.4 %smooth_in_chip.1 = (f32[2,272,256]{2,1,0:T(8,128)S(1)}, f32[2,272,256]{2,1,0:T(8,128)S(1)}, f32[256,256]{1,0:T(8,128)S(1)}, f32[2,256,256]{2,1,0:T(8,128)}, f32...) custom-call(f32[1]{0:T(128)S(6)} %copy.7.kappa, f32[1,2,256,256]{3,2,1,0:T(8,128)S(1)} %copy-done, ...), custom_call_target="tpu_custom_call" | custom-call | tf_op jit(solution)/shard_map/smooth_in_chip/pallas_call | solution.py:596
  23.2 4.6 %collective-permute-start.7 = (f32[1,256,256]{2,1,0:T(8,128)S(1)}, f32[1,256,256]{2,1,0:T(8,128)S(1)}, u32[]{:S(2)}, u32[]{:S(2)}) collective-permute-start(f32[1,256,256]{2,1,0:T(8,128)S(1)} %get-tuple-element.33), channel_id=1, source_target_pairs={{4,8},{8,4},{12,16},{16,12},{20,24},{24,20},{28,32},{32,28},{36,40... | collective-permute-start | bytes 786440 | tf_op jit(solution)/shard_map/ppermute | solution.py:573
  27.8 0.0 collective-permute-done.4.dens_b
  27.8 3.0 %smooth_and_restrict.1 = (f32[2,256,256]{2,1,0:T(8,128)S(1)}, f32[2,256,256]{2,1,0:T(8,128)}, f32[384,128]{1,0:T(8,128)S(1)}, f32[1,256,256]{2,1,0:T(8,128)}, f32[64,5,128]{2,1,0:T(8,128)}) custom-call(f32[1]{0:T(128)S(6)} %copy.7.kappa, f32[1,2,256,256]{3,2,1,0:T(8,128)S(1)} %copy-done, f32[2,256,256]{2,1,0:T(8,128)S(1)} %collect_density.1.dens, ...), custom_call_target="tpu_custom_call" | custom-call | tf_op jit(solution)/shard_map/smooth_and_restrict/pallas_call | solution.py:619
  30.8 0.0 copy-start.1
  30.8 0.1 collective-permute-start.9
  30.9 9.0 %all-to-all-start = ((f32[64,5,128]{2,1,0:T(8,128)}), f32[64,5,128]{2,1,0:T(8,128)S(1)}, u32[]{:S(2)}, u32[]{:S(2)}) async-start(f32[64,5,128]{2,1,0:T(8,128)} %get-tuple-element.38), calls=%async_computation | async-start | bytes 524288 | tf_op jit(solution)/shard_map/all_to_all | solution.py:641
  39.9 0.0 collective-permute-done.9.other.sib
  39.9 0.0 collective-permute-done.7.near_f
  39.9 0.8 %join_chip.1 = (f32[384,128]{1,0:T(8,128)}, f32[384,128]{1,0:T(8,128)}) custom-call(f32[384,128]{1,0:T(8,128)S(1)} %get-tuple-element.35.mine.send_a, f32[384,128]{1,0:T(8,128)S(1)} %collective-permute-done.9.other.sib, f32[128,128]{1,0:T(8,128)S(1)} %get-tuple-element.29.density1_sib, f32[128,128]{1,0:T(8,128)S(1)} %get-tuple-element.28.density1_own, ...), custom_call_target="tpu_custom_call" | custom-call | tf_op jit(solution)/shard_map/join_chip/pallas_call | solution.py:644
  40.7 4.6 %collective-permute-start.10 = (f32[384,128]{1,0:T(8,128)}, f32[384,128]{1,0:T(8,128)}, u32[]{:S(2)}, u32[]{:S(2)}) collective-permute-start(f32[384,128]{1,0:T(8,128)} %get-tuple-element.36), channel_id=1, source_target_pairs={{4,8},{8,4},{12,16},{16,12},{20,24},{24,20},{28,32},{32,28},{36,40... | collective-permute-start | bytes 589832 | tf_op jit(solution)/shard_map/ppermute | solution.py:573
  45.3 3.1 %collective-permute-start.11 = (f32[384,128]{1,0:T(8,128)}, f32[384,128]{1,0:T(8,128)}, u32[]{:S(2)}, u32[]{:S(2)}) collective-permute-start(f32[384,128]{1,0:T(8,128)} %get-tuple-element.37), channel_id=1, source_target_pairs={{16,4},{24,12},{32,20},{40,28},{48,36},{56,44},{64,52},{72,60},{80... | collective-permute-start | bytes 589832 | tf_op jit(solution)/shard_map/ppermute | solution.py:576
  48.4 0.1 collective-permute-start.8
  48.5 0.0 copy-done.1
  48.5 0.1 copy.6.groups
  48.6 0.4 all-to-all-done.gathered
  49.0 1.4 %solve_aggregates.1.spread = f32[16,512]{1,0:T(8,128)S(1)} custom-call(f32[1]{0:T(128)S(6)} %copy.7.kappa, f32[64,5,128]{2,1,0:T(8,128)S(1)} %all-to-all-done.gathered, s32[64,16]{1,0:T(8,128)S(1)} %copy.6.groups), custom_call_target="tpu_custom_call" | custom-call | tf_op jit(solution)/shard_map/solve_aggregates/pallas_call | solution.py:655
  50.5 2.2 %collective-permute-done.10.near = f32[384,128]{1,0:T(8,128)} collective-permute-done((f32[384,128]{1,0:T(8,128)}, f32[384,128]{1,0:T(8,128)}, u32[]{:S(2)}, u32[]{:S(2)}) %collective-permute-start.10) | collective-permute-done | bytes 196640 | tf_op jit(solution)/shard_map/ppermute | solution.py:573
  52.7 3.5 %collective-permute-done.11.far = f32[384,128]{1,0:T(8,128)} collective-permute-done((f32[384,128]{1,0:T(8,128)}, f32[384,128]{1,0:T(8,128)}, u32[]{:S(2)}, u32[]{:S(2)}) %collective-permute-start.11) | collective-permute-done | bytes 196640 | tf_op jit(solution)/shard_map/ppermute | solution.py:576
  56.2 0.0 collective-permute-start.12
  56.2 0.5 collective-permute-start.13
  56.7 0.0 collective-permute-done.8.sib_f
  56.7 1.1 %collective-permute-done.12.sib_near = f32[384,128]{1,0:T(8,128)S(1)} collective-permute-done((f32[384,128]{1,0:T(8,128)}, f32[384,128]{1,0:T(8,128)S(1)}, u32[]{:S(2)}, u32[]{:S(2)}) %collective-permute-start.12) | collective-permute-done | bytes 196640 | tf_op jit(solution)/shard_map/ppermute | solution.py:570
  57.9 0.3 collective-permute-done.13.sib_far
  58.1 4.3 %correct_and_smooth.1 = (f32[1,264,256]{2,1,0:T(8,128)S(1)}, f32[4,272,256]{2,1,0:T(8,128)S(1)}, f32[256,256]{1,0:T(8,128)S(1)}) custom-call(f32[1]{0:T(128)S(6)} %copy.7.kappa, f32[2,256,256]{2,1,0:T(8,128)} %get-tuple-element.30.halo_lo_in, f32[2,256,256]{2,1,0:T(8,128)} %get-tuple-element.31.halo_hi_in, f32[1,2,256,256]{3,2,1,0:T(8,128)S(1)} %copy-done, ...), custom_call_target="tpu_custom_call" | custom-call | tf_op jit(solution)/shard_map/correct_and_smooth/pallas_call | solution.py:669
  62.4 4.3 %collective-permute-start.15 = (f32[1,264,256]{2,1,0:T(8,128)S(1)}, f32[1,264,256]{2,1,0:T(8,128)S(1)}, u32[]{:S(2)}, u32[]{:S(2)}) collective-permute-start(f32[1,264,256]{2,1,0:T(8,128)S(1)} %get-tuple-element.42.to_b), channel_id=1, source_target_pairs={{4,8},{8,4},{12,16},{16,12},{20,24},{24,20},{28,32},{32,28},{36,40... | collective-permute-start | bytes 811016 | tf_op jit(solution)/shard_map/ppermute | solution.py:573
  66.7 1.4 %residual_inside.1 = (f32[1,256,256]{2,1,0:T(8,128)S(1)}, f32[1,2,256,256]{3,2,1,0:T(8,128)}, f32[2,256,256]{2,1,0:T(8,128)S(1)}) custom-call(f32[1]{0:T(128)S(6)} %copy.7.kappa, f32[1,2,256,256]{3,2,1,0:T(8,128)S(1)} %copy-done, f32[2,256,256]{2,1,0:T(8,128)S(1)} %collect_density.1.dens, f32[1,264,256]{2,1,0:T(8,128)S(1)} %get-tuple-element.42.to_b, ...), custom_call_target="tpu_custom_call" | custom-call | tf_op jit(solution)/shard_map/residual_inside/pallas_call | solution.py:694
  68.1 0.1 collective-permute-start.14
  68.2 1.5 %collective-permute-done.14.halo_a = f32[1,256,256]{2,1,0:T(8,128)S(1)} collective-permute-done((f32[1,256,256]{2,1,0:T(8,128)S(1)}, f32[1,256,256]{2,1,0:T(8,128)S(1)}, u32[]{:S(2)}, u32[]{:S(2)}) %collective-permute-start.14) | collective-permute-done | bytes 262176 | tf_op jit(solution)/shard_map/ppermute | solution.py:570
  69.7 3.8 %collective-permute-done.15.halo_b = f32[1,264,256]{2,1,0:T(8,128)S(1)} collective-permute-done((f32[1,264,256]{2,1,0:T(8,128)S(1)}, f32[1,264,256]{2,1,0:T(8,128)S(1)}, u32[]{:S(2)}, u32[]{:S(2)}) %collective-permute-start.15) | collective-permute-done | bytes 270368 | tf_op jit(solution)/shard_map/ppermute | solution.py:573
  73.5 1.1 %residual.1 = f32[1,2,256,256]{3,2,1,0:T(8,128)} custom-call(f32[1]{0:T(128)S(6)} %copy.7.kappa, f32[2,256,256]{2,1,0:T(8,128)S(1)} %get-tuple-element.46.inside, f32[1,256,256]{2,1,0:T(8,128)S(1)} %collective-permute-done.14.halo_a, f32[1,264,256]{2,1,0:T(8,128)S(1)} %collective-permute-done.15.halo_b), custom_call_target="tpu_custom_call" | custom-call | tf_op jit(solution)/shard_map/residual/pallas_call | solution.py:707
Async XLA Ops:
  0.6 21.2 %copy-start = (f32[1,2,256,256]{3,2,1,0:T(8,128)S(1)}, f32[1,2,256,256]{3,2,1,0:T(8,128)}, u32[]{:S(2)}) copy-start(f32[1,2,256,256]{3,2,1,0:T(8,128)} %rhs.7) | copy-start | bytes 1572868
  0.6 11.8 %collective-permute-start.1 = (f32[2,64,256]{2,1,0:T(8,128)}, f32[2,64,256]{2,1,0:T(8,128)S(1)}, u32[]{:S(2)}, u32[]{:S(2)}) collective-permute-start(f32[2,64,256]{2,1,0:T(8,128)} %shard.1), channel_id=1, source_target_pairs={{0,2},{1,3},{2,0},{3,1},{4,6},{5,7},{6,4},{7,5},{8,10},{9,11},{10,... | collective-permute-start | bytes 393224 | tf_op jit(solution)/shard_map/ppermute | solution.py:579
  3.6 8.8 %collective-permute-start = (f32[2,64,256]{2,1,0:T(8,128)}, f32[2,64,256]{2,1,0:T(8,128)S(1)}, u32[]{:S(2)}, u32[]{:S(2)}) collective-permute-start(f32[2,64,256]{2,1,0:T(8,128)} %shard.1), channel_id=1, source_target_pairs={{0,1},{1,2},{2,3},{3,0},{4,5},{5,6},{6,7},{7,4},{8,9},{9,10},{10,1... | collective-permute-start | bytes 393224 | tf_op jit(solution)/shard_map/ppermute | solution.py:579
  4.0 8.4 %collective-permute-start.2 = (f32[2,64,256]{2,1,0:T(8,128)}, f32[2,64,256]{2,1,0:T(8,128)S(1)}, u32[]{:S(2)}, u32[]{:S(2)}) collective-permute-start(f32[2,64,256]{2,1,0:T(8,128)} %shard.1), channel_id=1, source_target_pairs={{0,3},{1,0},{2,1},{3,2},{4,7},{5,4},{6,5},{7,6},{8,11},{9,8},{10,9... | collective-permute-start | bytes 393224 | tf_op jit(solution)/shard_map/ppermute | solution.py:579
  6.3 12.1 %collective-permute-start.5 = (f32[1,2,256,256]{3,2,1,0:T(8,128)}, f32[1,2,256,256]{3,2,1,0:T(8,128)S(1)}, u32[]{:S(2)}, u32[]{:S(2)}) collective-permute-start(f32[1,2,256,256]{3,2,1,0:T(8,128)} %rhs.7), channel_id=1, source_target_pairs={{0,4},{4,0},{8,12},{12,8},{16,20},{20,16},{24,28},{28,24},{32,36},... | collective-permute-start | bytes 1572872 | tf_op jit(solution)/shard_map/ppermute | solution.py:570
  7.8 14.0 %collective-permute-start.3 = (f32[1,2,256,256]{3,2,1,0:T(8,128)}, f32[1,2,256,256]{3,2,1,0:T(8,128)S(1)}, u32[]{:S(2)}, u32[]{:S(2)}) collective-permute-start(f32[1,2,256,256]{3,2,1,0:T(8,128)} %rhs.7), channel_id=1, source_target_pairs={{4,8},{8,4},{12,16},{16,12},{20,24},{24,20},{28,32},{32,28},{36,40... | collective-permute-start | bytes 1572872 | tf_op jit(solution)/shard_map/ppermute | solution.py:573
  13.4 8.5 %collective-permute-start.6 = (f32[2,256,256]{2,1,0:T(8,128)S(1)}, f32[2,256,256]{2,1,0:T(8,128)S(1)}, u32[]{:S(2)}, u32[]{:S(2)}) collective-permute-start(f32[2,256,256]{2,1,0:T(8,128)S(1)} %collect_density.1.dens), channel_id=1, source_target_pairs={{0,4},{4,0},{8,12},{12,8},{16,20},{20,16},{24,28},{28,24},{32,36},... | collective-permute-start | bytes 1572872 | tf_op jit(solution)/shard_map/ppermute | solution.py:570
  13.5 14.4 %collective-permute-start.4 = (f32[2,256,256]{2,1,0:T(8,128)S(1)}, f32[2,256,256]{2,1,0:T(8,128)S(1)}, u32[]{:S(2)}, u32[]{:S(2)}) collective-permute-start(f32[2,256,256]{2,1,0:T(8,128)S(1)} %collect_density.1.dens), channel_id=1, source_target_pairs={{4,8},{8,4},{12,16},{16,12},{20,24},{24,20},{28,32},{32,28},{36,40... | collective-permute-start | bytes 1572872 | tf_op jit(solution)/shard_map/ppermute | solution.py:573
  23.2 16.7 %collective-permute-start.7 = (f32[1,256,256]{2,1,0:T(8,128)S(1)}, f32[1,256,256]{2,1,0:T(8,128)S(1)}, u32[]{:S(2)}, u32[]{:S(2)}) collective-permute-start(f32[1,256,256]{2,1,0:T(8,128)S(1)} %get-tuple-element.33), channel_id=1, source_target_pairs={{4,8},{8,4},{12,16},{16,12},{20,24},{24,20},{28,32},{32,28},{36,40... | collective-permute-start | bytes 786440 | tf_op jit(solution)/shard_map/ppermute | solution.py:573
  30.8 17.7 %copy-start.1 = (s32[64,16]{0,1:T(8,128)S(1)}, s32[64,16]{0,1:T(8,128)}, u32[]{:S(2)}) copy-start(s32[64,16]{0,1:T(8,128)} %param.7) | copy-start | bytes 12292
  30.8 9.1 %collective-permute-start.9 = (f32[384,128]{1,0:T(8,128)S(1)}, f32[384,128]{1,0:T(8,128)S(1)}, u32[]{:S(2)}, u32[]{:S(2)}) collective-permute-start(f32[384,128]{1,0:T(8,128)S(1)} %get-tuple-element.35.mine.send_a), channel_id=1, source_target_pairs={{0,4},{4,0},{8,12},{12,8},{16,20},{20,16},{24,28},{28,24},{32,36},... | collective-permute-start | bytes 589832 | tf_op jit(solution)/shard_map/ppermute | solution.py:570
  30.9 18.1 %all-to-all-start = ((f32[64,5,128]{2,1,0:T(8,128)}), f32[64,5,128]{2,1,0:T(8,128)S(1)}, u32[]{:S(2)}, u32[]{:S(2)}) async-start(f32[64,5,128]{2,1,0:T(8,128)} %get-tuple-element.38), calls=%async_computation | async-start | bytes 524288 | tf_op jit(solution)/shard_map/all_to_all | solution.py:641
  40.7 12.0 %collective-permute-start.10 = (f32[384,128]{1,0:T(8,128)}, f32[384,128]{1,0:T(8,128)}, u32[]{:S(2)}, u32[]{:S(2)}) collective-permute-start(f32[384,128]{1,0:T(8,128)} %get-tuple-element.36), channel_id=1, source_target_pairs={{4,8},{8,4},{12,16},{16,12},{20,24},{24,20},{28,32},{32,28},{36,40... | collective-permute-start | bytes 589832 | tf_op jit(solution)/shard_map/ppermute | solution.py:573
  45.3 10.9 %collective-permute-start.11 = (f32[384,128]{1,0:T(8,128)}, f32[384,128]{1,0:T(8,128)}, u32[]{:S(2)}, u32[]{:S(2)}) collective-permute-start(f32[384,128]{1,0:T(8,128)} %get-tuple-element.37), channel_id=1, source_target_pairs={{16,4},{24,12},{32,20},{40,28},{48,36},{56,44},{64,52},{72,60},{80... | collective-permute-start | bytes 589832 | tf_op jit(solution)/shard_map/ppermute | solution.py:576
  48.4 8.3 %collective-permute-start.8 = (f32[1,256,256]{2,1,0:T(8,128)}, f32[1,256,256]{2,1,0:T(8,128)S(1)}, u32[]{:S(2)}, u32[]{:S(2)}) collective-permute-start(f32[1,256,256]{2,1,0:T(8,128)} %get-tuple-element.34), channel_id=1, source_target_pairs={{0,4},{4,0},{8,12},{12,8},{16,20},{20,16},{24,28},{28,24},{32,36},... | collective-permute-start | bytes 786440 | tf_op jit(solution)/shard_map/ppermute | solution.py:570
  56.2 1.7 %collective-permute-start.12 = (f32[384,128]{1,0:T(8,128)}, f32[384,128]{1,0:T(8,128)S(1)}, u32[]{:S(2)}, u32[]{:S(2)}) collective-permute-start(f32[384,128]{1,0:T(8,128)} %collective-permute-done.10.near), channel_id=1, source_target_pairs={{0,4},{4,0},{8,12},{12,8},{16,20},{20,16},{24,28},{28,24},{32,36},... | collective-permute-start | bytes 589832 | tf_op jit(solution)/shard_map/ppermute | solution.py:570
  56.2 1.9 %collective-permute-start.13 = (f32[384,128]{1,0:T(8,128)}, f32[384,128]{1,0:T(8,128)S(1)}, u32[]{:S(2)}, u32[]{:S(2)}) collective-permute-start(f32[384,128]{1,0:T(8,128)} %collective-permute-done.11.far), channel_id=1, source_target_pairs={{0,4},{4,0},{8,12},{12,8},{16,20},{20,16},{24,28},{28,24},{32,36},... | collective-permute-start | bytes 589832 | tf_op jit(solution)/shard_map/ppermute | solution.py:570
  62.4 11.1 %collective-permute-start.15 = (f32[1,264,256]{2,1,0:T(8,128)S(1)}, f32[1,264,256]{2,1,0:T(8,128)S(1)}, u32[]{:S(2)}, u32[]{:S(2)}) collective-permute-start(f32[1,264,256]{2,1,0:T(8,128)S(1)} %get-tuple-element.42.to_b), channel_id=1, source_target_pairs={{4,8},{8,4},{12,16},{16,12},{20,24},{24,20},{28,32},{32,28},{36,40... | collective-permute-start | bytes 811016 | tf_op jit(solution)/shard_map/ppermute | solution.py:573
  68.1 1.6 %collective-permute-start.14 = (f32[1,256,256]{2,1,0:T(8,128)S(1)}, f32[1,256,256]{2,1,0:T(8,128)S(1)}, u32[]{:S(2)}, u32[]{:S(2)}) collective-permute-start(f32[1,256,256]{2,1,0:T(8,128)S(1)} %get-tuple-element.47), channel_id=1, source_target_pairs={{0,4},{4,0},{8,12},{12,8},{16,20},{20,16},{24,28},{28,24},{32,36},... | collective-permute-start | bytes 786440 | tf_op jit(solution)/shard_map/ppermute | solution.py:570
